TPU v7x, 32 devices: a whole 2x2x4 slice. The times are simulated.
32 devices in a mesh: runs: 2 (over y), tm: 4 (over z), pix: 4 (over x, core).
Axes of the slice: x: 2, y: 2, z: 4, core: 2. Of those that a mesh axis runs over, the one named last changes fastest.
Arguments:
- frames: bfloat16 [448, 32768], P(('runs', 'tm'), 'pix'), parts along dimension 0, may hold values from 0.049804688 to 20
- labels: int32 [32768], P('pix'), may hold values from -1 to 127, as said below
Outputs:
- two_time: float32 [256, 224, 168], P(('runs', 'pix'), 'tm'), parts along dimension 0
There are 2 independent parts, one for each index of `runs`. A program takes and returns all parts, laid end to end along the dimension named above; an argument that names none is the same for every part. Nothing has to cross between parts.
Inputs may be any that keep to these rules, and one draw needn't show every extreme that they name: `labels`: within the block of 8192 pixels of each pixel group, pixel j lies on cycle j // 64 or is masked (-1); the first pixel of every cycle's slot in every group is unmasked.
All inputs are finite; a program needn't handle non-finite values.
Results may differ from a plain program's by a relative error of at most 0.0003.
Values may be sent and summed in bfloat16 or wider, within the bound.
No kernel may reach another device: no remote copies, remote signals or barrier semaphores. Data moves between devices by JAX's collectives and lax.ppermute only.
A program may use at most 64 MiB of HBM per device.

v0:
```python
import jax
import jax.numpy as jnp
from jax import lax
from jax.sharding import PartitionSpec as P

CYCLES = 128
CYCLE_CAP = 64


def from_behind(shard, axis, by):
    size = lax.axis_size(axis)
    return lax.ppermute(shard, axis, [(i, (i + by) % size) for i in range(size)])


def on_device(frames, labels):
    groups = lax.axis_size("pix")
    loop_size = lax.axis_size("tm")
    local_cycles = CYCLES // groups
    slot_total = loop_size // 2 + 1
    frame_rows = frames.shape[0]
    live_row = (labels >= 0).astype(jnp.bfloat16)[None, :]
    masked = frames * live_row
    own_block, live_owned = (
        lax.all_to_all(masked, "pix", split_axis=1, concat_axis=1, tiled=True),
        lax.all_to_all(live_row, "pix", split_axis=1, concat_axis=1, tiled=True),
    )

    def split_cycles(values):
        return values.reshape(values.shape[:-1] + (groups, local_cycles, CYCLE_CAP))

    counts = jnp.sum(split_cycles(live_owned).astype(jnp.float32), axis=(0, 1, 3))
    own_split = split_cycles(own_block)
    own_means = jnp.sum(own_split, axis=(1, 3), dtype=jnp.float32) / counts

    def make_tiles(blocks):
        block_split = split_cycles(blocks)
        block_means = jnp.sum(block_split, axis=(2, 4), dtype=jnp.float32) / counts
        gram_tiles = jnp.einsum(
            "tgqc,nsgqc->qtns", own_split, block_split, preferred_element_type=jnp.float32
        )
        denominator = (
            counts[:, None, None, None]
            * own_means.T[:, :, None, None]
            * jnp.transpose(block_means, (2, 0, 1))[:, None, :, :]
        )
        return (gram_tiles / denominator).reshape(
            local_cycles, frame_rows, blocks.shape[0] * frame_rows
        )

    filled = jnp.zeros((local_cycles, frame_rows, slot_total * frame_rows), jnp.float32)
    filled = lax.dynamic_update_slice(filled, make_tiles(own_block[None]), (0, 0, 0))

    def advance(offset, carry):
        moving, result = carry
        moving = from_behind(moving, "tm", -1)
        result = lax.dynamic_update_slice(
            result, make_tiles(moving[None]), (0, 0, offset * frame_rows)
        )
        return (moving, result)

    _, filled = lax.fori_loop(1, slot_total, advance, (own_block, filled))
    return filled


def solution(mesh):
    placed = (P(("runs", "tm"), "pix"), P("pix"))
    return jax.shard_map(
        on_device,
        mesh=mesh,
        in_specs=placed,
        out_specs=P(("runs", "pix"), "tm", None),
        check_vma=False,
    )
```

profile of v0, /device:TPU:0, one launch (start us, length us, event | category | flops | bytes accessed | tf_op | source)
XLA Modules:
  0.0 114.2 jit_solution(7265024914933329808)
XLA Ops:
  0.0 0.8 compare_convert_fusion
  0.8 0.5 broadcast.82
  1.3 0.7 reduce.11
  2.0 0.6 reshape.160
  2.6 4.2 %all-to-all-start.1 = ((bf16[4,2,1024]{2,1,0:T(2,128)(2,1)}), bf16[4,2,1024]{2,1,0:T(2,128)(2,1)S(1)}, u32[]{:S(2)}, u32[]{:S(2)}) async-start(bf16[4,2,1024]{2,1,0:T(2,128)(2,1)} %reshape.160), calls=%async_computation.1 | async-start | bytes 32768 | tf_op jit(solution)/shard_map/all_to_all | solution.py:25
  6.9 1.2 %broadcast_multiply_fusion = bf16[56,8192]{1,0:T(8,128)(2,1)S(1)} fusion(bf16[56,8192]{1,0:T(8,128)(2,1)} %param.4, bf16[8192]{0:T(1024)(128)(2,1)S(1)} %compare_convert_fusion), kind=kLoop, calls=%fused_computation.12 | loop fusion | flops 458752 | bytes 1851392 | tf_op jit(solution)/shard_map/mul | solution.py:22
  8.1 1.0 copy.48
  9.1 1.6 %all-to-all-done.1 = bf16[4,2,1024]{2,1,0:T(2,128)(2,1)S(1)} async-done(((bf16[4,2,1024]{2,1,0:T(2,128)(2,1)}), bf16[4,2,1024]{2,1,0:T(2,128)(2,1)S(1)}, u32[]{:S(2)}, u32[]{:S(2)}) %all-to-all-start.1) | async-done | bytes 16416 | tf_op jit(solution)/shard_map/all_to_all | solution.py:25
  10.7 3.5 %all-to-all-start = ((bf16[56,4,2048]{2,0,1:T(8,128)(2,1)}), bf16[56,4,2048]{2,0,1:T(8,128)(2,1)S(1)}, u32[]{:S(2)}, u32[]{:S(2)}) async-start(bf16[56,4,2048]{2,0,1:T(8,128)(2,1)} %bitcast.41), calls=%async_computation | async-start | bytes 1835008 | tf_op jit(solution)/shard_map/all_to_all | solution.py:24
  14.3 0.1 reduce_sum.52
  14.4 0.1 reduce_sum.53
  14.5 12.8 %all-to-all-done = bf16[56,4,2048]{2,0,1:T(8,128)(2,1)S(1)} async-done(((bf16[56,4,2048]{2,0,1:T(8,128)(2,1)}), bf16[56,4,2048]{2,0,1:T(8,128)(2,1)S(1)}, u32[]{:S(2)}, u32[]{:S(2)}) %all-to-all-start) | async-done | bytes 917536 | tf_op jit(solution)/shard_map/all_to_all | solution.py:24
  27.3 0.1 convert_reduce_fusion.1
  27.4 0.4 reduce_sum.55
  27.8 0.3 reduce_sum.56
  28.3 1.9 %reshape.157 = bf16[56,4,32,64]{3,2,0,1:T(8,128)(2,1)S(1)} reshape(bf16[56,4,2048]{2,0,1:T(8,128)(2,1)S(1)} %all-to-all-done) | data formatting | bytes 1835008 | tf_op jit(solution)/shard_map/reshape | solution.py:29
  30.2 2.0 %copy.28 = bf16[56,4,32,64]{3,0,1,2:T(8,128)(2,1)} copy(bf16[56,4,32,64]{3,2,0,1:T(8,128)(2,1)S(1)} %reshape.157) | data formatting | bytes 1835008 | tf_op jit(solution)/shard_map/reshape | solution.py:29
  32.1 3.5 %fusion.9 = f32[32,56,56]{2,1,0:T(8,128)S(1)} fusion(f32[32,56]{1,0:T(8,128)S(1)} %copy.32, f32[32,56]{1,0:T(8,128)S(1)} %copy.31, bf16[56,4,32,64]{3,2,0,1:T(8,128)(2,1)S(1)} %reshape.157), kind=kOutput, calls=%fused_computation.10 | convolution fusion | flops 51580928 | bytes 1333248 | tf_op jit(solution)/shard_map/tgqc,nsgqc->qtns/dot_general | solution.py:38
  35.6 1.4 %dynamic_update_slice.10 = f32[32,56,168]{2,1,0:T(8,128)} pad(f32[32,56,56]{2,1,0:T(8,128)S(1)} %fusion.9, f32[]{:T(128)} %constant.40.clone.1), padding=0_0x0_0x0_112 | pad | bytes 1605636 | tf_op jit(solution)/shard_map/dynamic_update_slice | solution.py:51
  37.1 77.1 %while.15 = (s32[]{:T(128)}, bf16[56,8192]{1,0:T(8,128)(2,1)S(1)}, f32[32,56,168]{2,1,0:T(8,128)}, bf16[56,4,32,64]{3,0,1,2:T(8,128)(2,1)}, f32[32]{0:T(128)S(1)...) while((s32[]{:T(128)}, bf16[56,8192]{1,0:T(8,128)(2,1)S(1)}, ...), condition=%wide.region_6.7_spmd, body=%wide.region_4.6_spmd.sunk | while | flops 52500224 | bytes 11361727 | solution.py:61
  37.1 4.1 %collective-permute-start = (bf16[56,8192]{1,0:T(8,128)(2,1)S(1)}, bf16[56,8192]{1,0:T(8,128)(2,1)S(1)}, u32[]{:S(2)}, u32[]{:S(2)}) collective-permute-start(bf16[56,8192]{1,0:T(8,128)(2,1)S(1)} %get-tuple-element.201), channel_id=1, source_target_pairs={{0,12},{4,0},{8,4},{12,8},{1,13},{5,1},{9,5},{13,9},{2,14},{6,2},{... | collective-permute-start | bytes 2752520 | tf_op jit(solution)/shard_map/while/body/eval_jaxpr/ppermute | solution.py:12
  41.3 19.3 %collective-permute-done = bf16[56,8192]{1,0:T(8,128)(2,1)S(1)} collective-permute-done((bf16[56,8192]{1,0:T(8,128)(2,1)S(1)}, bf16[56,8192]{1,0:T(8,128)(2,1)S(1)}, u32[]{:S(2)}, u32[]{:S(2)}) %collective-permute-start) | collective-permute-done | bytes 917536 | tf_op jit(solution)/shard_map/while/body/eval_jaxpr/ppermute | solution.py:12
  60.7 1.9 %reshape.163 = bf16[56,4,32,64]{3,2,1,0:T(8,128)(2,1)S(1)} reshape(bf16[56,8192]{1,0:T(8,128)(2,1)S(1)} %collective-permute-done) | data formatting | bytes 1835008 | tf_op jit(solution)/shard_map/reshape.88
  62.6 0.4 convert_reduce_fusion.4
  63.1 3.7 %fusion.20 = f32[32,56,56]{2,1,0:T(8,128)} fusion(bf16[56,4,32,64]{3,0,1,2:T(8,128)(2,1)} %get-tuple-element.213, bf16[56,4,32,64]{3,2,1,0:T(8,128)(2,1)S(1)} %reshape.163, f32[32,56]{1,0:T(8,128)S(1)} %copy.52, f32[32,56]{1,0:T(8,128)S(1)} %multiply_bitcast_fusion.3), kind=kOutput, calls=%fused_computation.4.clone.1 | convolution fusion | flops 51580928 | bytes 2250752 | tf_op jit(solution)/shard_map/while/body/eval_jaxpr/tgqc,nsgqc->qtns/dot_general | solution.py:38
  66.9 9.1 %dynamic_update_slice.12 = f32[32,56,168]{2,1,0:T(8,128)} dynamic-update-slice(f32[32,56,168]{2,1,0:T(8,128)} %get-tuple-element.202, f32[32,56,56]{2,1,0:T(8,128)} %fusion.20, s32[]{:T(128)} %constant.39.clone.1..sunk, s32[]{:T(128)} %constant.39.clone.1..sunk, s32[]{:T(128)S(6)} %select_n.8) | dynamic-update-slice | bytes 802820 | tf_op jit(solution)/shard_map/while/body/eval_jaxpr/dynamic_update_slice | solution.py:56
  76.0 4.3 %collective-permute-start = (bf16[56,8192]{1,0:T(8,128)(2,1)S(1)}, bf16[56,8192]{1,0:T(8,128)(2,1)S(1)}, u32[]{:S(2)}, u32[]{:S(2)}) collective-permute-start(bf16[56,8192]{1,0:T(8,128)(2,1)S(1)} %get-tuple-element.201), channel_id=1, source_target_pairs={{0,12},{4,0},{8,4},{12,8},{1,13},{5,1},{9,5},{13,9},{2,14},{6,2},{... | collective-permute-start | bytes 2752520 | tf_op jit(solution)/shard_map/while/body/eval_jaxpr/ppermute | solution.py:12
  80.4 18.4 %collective-permute-done = bf16[56,8192]{1,0:T(8,128)(2,1)S(1)} collective-permute-done((bf16[56,8192]{1,0:T(8,128)(2,1)S(1)}, bf16[56,8192]{1,0:T(8,128)(2,1)S(1)}, u32[]{:S(2)}, u32[]{:S(2)}) %collective-permute-start) | collective-permute-done | bytes 917536 | tf_op jit(solution)/shard_map/while/body/eval_jaxpr/ppermute | solution.py:12
  98.9 1.9 %reshape.163 = bf16[56,4,32,64]{3,2,1,0:T(8,128)(2,1)S(1)} reshape(bf16[56,8192]{1,0:T(8,128)(2,1)S(1)} %collective-permute-done) | data formatting | bytes 1835008 | tf_op jit(solution)/shard_map/reshape.88
  100.8 0.4 convert_reduce_fusion.4
  101.3 3.7 %fusion.20 = f32[32,56,56]{2,1,0:T(8,128)} fusion(bf16[56,4,32,64]{3,0,1,2:T(8,128)(2,1)} %get-tuple-element.213, bf16[56,4,32,64]{3,2,1,0:T(8,128)(2,1)S(1)} %reshape.163, f32[32,56]{1,0:T(8,128)S(1)} %copy.52, f32[32,56]{1,0:T(8,128)S(1)} %multiply_bitcast_fusion.3), kind=kOutput, calls=%fused_computation.4.clone.1 | convolution fusion | flops 51580928 | bytes 2250752 | tf_op jit(solution)/shard_map/while/body/eval_jaxpr/tgqc,nsgqc->qtns/dot_general | solution.py:38
  105.1 9.1 %dynamic_update_slice.12 = f32[32,56,168]{2,1,0:T(8,128)} dynamic-update-slice(f32[32,56,168]{2,1,0:T(8,128)} %get-tuple-element.202, f32[32,56,56]{2,1,0:T(8,128)} %fusion.20, s32[]{:T(128)} %constant.39.clone.1..sunk, s32[]{:T(128)} %constant.39.clone.1..sunk, s32[]{:T(128)S(6)} %select_n.8) | dynamic-update-slice | bytes 802820 | tf_op jit(solution)/shard_map/while/body/eval_jaxpr/dynamic_update_slice | solution.py:56
  (17 shorter events, 0.8 us)
Async XLA Ops:
  2.6 8.1 %all-to-all-start.1 = ((bf16[4,2,1024]{2,1,0:T(2,128)(2,1)}), bf16[4,2,1024]{2,1,0:T(2,128)(2,1)S(1)}, u32[]{:S(2)}, u32[]{:S(2)}) async-start(bf16[4,2,1024]{2,1,0:T(2,128)(2,1)} %reshape.160), calls=%async_computation.1 | async-start | bytes 32768 | tf_op jit(solution)/shard_map/all_to_all | solution.py:25
  10.7 16.5 %all-to-all-start = ((bf16[56,4,2048]{2,0,1:T(8,128)(2,1)}), bf16[56,4,2048]{2,0,1:T(8,128)(2,1)S(1)}, u32[]{:S(2)}, u32[]{:S(2)}) async-start(bf16[56,4,2048]{2,0,1:T(8,128)(2,1)} %bitcast.41), calls=%async_computation | async-start | bytes 1835008 | tf_op jit(solution)/shard_map/all_to_all | solution.py:24
  37.1 23.5 %collective-permute-start = (bf16[56,8192]{1,0:T(8,128)(2,1)S(1)}, bf16[56,8192]{1,0:T(8,128)(2,1)S(1)}, u32[]{:S(2)}, u32[]{:S(2)}) collective-permute-start(bf16[56,8192]{1,0:T(8,128)(2,1)S(1)} %get-tuple-element.201), channel_id=1, source_target_pairs={{0,12},{4,0},{8,4},{12,8},{1,13},{5,1},{9,5},{13,9},{2,14},{6,2},{... | collective-permute-start | bytes 2752520 | tf_op jit(solution)/shard_map/while/body/eval_jaxpr/ppermute | solution.py:12
  76.0 22.8 %collective-permute-start = (bf16[56,8192]{1,0:T(8,128)(2,1)S(1)}, bf16[56,8192]{1,0:T(8,128)(2,1)S(1)}, u32[]{:S(2)}, u32[]{:S(2)}) collective-permute-start(bf16[56,8192]{1,0:T(8,128)(2,1)S(1)} %get-tuple-element.201), channel_id=1, source_target_pairs={{0,12},{4,0},{8,4},{12,8},{1,13},{5,1},{9,5},{13,9},{2,14},{6,2},{... | collective-permute-start | bytes 2752520 | tf_op jit(solution)/shard_map/while/body/eval_jaxpr/ppermute | solution.py:12
where the time goes:
time: 115 us; the launch traced here: 114 us
  waiting for transfers between devices  52.1 us (45%)
  local copies, waits for them, and re-layouts  30.4 us (26%)
  starting transfers between devices  16.2 us (14%)
  matrix products  11 us (10%)
  other arithmetic  4.37 us (4%)
    ppermute x2, waiting for transfers between devices, from_behind(): lax.ppermute(shard, axis, [(i, (i + by) % size) for i in range(size)])  37.8 us
    dynamic_update_slice x2, local copies, waits for them, and re-layouts, advance(): lax.dynamic_update_slice(result, make_tiles(moving[None]), (0, 0, offset...  18.1 us
    all_to_all x1, waiting for transfers between devices, on_device(): lax.all_to_all(masked, 'pix', split_axis=1, concat_axis=1, tiled=True)  12.8 us
    dot_general x3, matrix products, make_tiles(): jnp.einsum('tgqc,nsgqc->qtns', own_split, block_split, preferred_element_...  11 us
    ppermute x2, starting transfers between devices, from_behind(): lax.ppermute(shard, axis, [(i, (i + by) % size) for i in range(size)])  8.44 us
    all_to_all x1, starting transfers between devices, on_device(): lax.all_to_all(live_row, 'pix', split_axis=1, concat_axis=1, tiled=True)  4.21 us
    another operation x2, local copies, waits for them, and re-layouts  3.88 us
    reshape x2, local copies, waits for them, and re-layouts, split_cycles(): return values.reshape(values.shape[:-1] + (groups, local_cycles, CYCLE_CAP))  3.88 us
  transfers between devices with their start and end apart: 4, of which 4 were waited for; matrix products, arithmetic and copies ran while one was open for 2% of the time, Pallas kernels for 0%

commit v1 on v0

--- a/solution.py
+++ b/solution.py
@@ -1,10 +1,16 @@
+import functools
+
 import jax
 import jax.numpy as jnp
 from jax import lax
+from jax.experimental import pallas as pl
+from jax.experimental.pallas import tpu as pltpu
 from jax.sharding import PartitionSpec as P
 
 CYCLES = 128
 CYCLE_CAP = 64
+LANES = 128
+VMEM_LIMIT = 48 * 2**20
 
 
 def from_behind(shard, axis, by):
@@ -12,7 +18,12 @@
     return lax.ppermute(shard, axis, [(i, (i + by) % size) for i in range(size)])
 
 
-def on_device(frames, labels):
+def swap(shard, axis, by):
+    size = lax.axis_size(axis)
+    return lax.ppermute(shard, axis, [(i, i ^ by) for i in range(size)])
+
+
+def ring(frames, labels):
     groups = lax.axis_size("pix")
     loop_size = lax.axis_size("tm")
     local_cycles = CYCLES // groups
@@ -62,6 +73,235 @@
     return filled
 
 
+VMEM = pl.BlockSpec(memory_space=pltpu.VMEM)
+
+
+def local_call(body, outs, count_in, scratch=()):
+    return pl.pallas_call(
+        body,
+        out_shape=outs,
+        in_specs=[VMEM] * count_in,
+        out_specs=[VMEM] * len(outs),
+        scratch_shapes=list(scratch),
+        compiler_params=pltpu.CompilerParams(vmem_limit_bytes=VMEM_LIMIT),
+    )
+
+
+def lanes_at(start, width):
+    return pl.ds(pl.multiple_of(start, LANES), width)
+
+
+def pack_kernel(loop, groups, per, first, frames, labels, *outs):
+    t, p = lax.axis_index("tm"), lax.axis_index("pix")
+    rest = per - first
+    to_time, to_owner_first, to_owner_rest = outs[:loop], outs[loop : loop + groups], outs[loop + groups :]
+
+    def tile(index):
+        live = jnp.where(labels[pl.ds(index, 1), :] >= 0, 1.0, 0.0).astype(jnp.bfloat16)
+        return frames[:, lanes_at(index * LANES, LANES)] * live
+
+    for j in range(loop):
+        for g in range(groups):
+            for s in range(first):
+                at = (g * first + s) * LANES
+                to_time[j][:, at : at + LANES] = tile((g * loop + (t ^ j)) * per + s)
+    for k in range(groups):
+        for c in range(loop):
+            for s in range(per):
+                value = tile(((p ^ k) * loop + c) * per + s)
+                if s < first:
+                    at = (c * first + s) * LANES
+                    to_owner_first[k][:, at : at + LANES] = value
+                else:
+                    at = (c * rest + s - first) * LANES
+                    to_owner_rest[k][:, at : at + LANES] = value
+
+
+def pick_kernel(axis, count, width, *refs):
+    sources, outs = refs[:count], refs[count:]
+    me = lax.axis_index(axis)
+    for j, out in enumerate(outs):
+        for k, source in enumerate(sources):
+            out[k] = source[:, lanes_at((me ^ j) * width, width)]
+
+
+def padded(value):
+    wide = value.astype(jnp.float32)
+    live = jnp.where(wide[0:1, :] != 0, 1.0, 0.0)
+    return jnp.concatenate([wide, jnp.broadcast_to(live, (8, LANES))], axis=0)
+
+
+def halves(block):
+    lane = lax.broadcasted_iota(jnp.int32, block.shape, 1) % LANES
+    zero = jnp.zeros_like(block)
+    return jnp.concatenate(
+        [jnp.where(lane < CYCLE_CAP, block, zero), jnp.where(lane < CYCLE_CAP, zero, block)], axis=0
+    )
+
+
+def normalized(product, rows):
+    result = []
+    for half in range(2):
+        cycle = product[half * (rows + 8) : (half + 1) * (rows + 8)]
+        count = cycle[rows : rows + 1, rows : rows + 1]
+        row_scale = count / cycle[:rows, rows : rows + 1]
+        column_scale = 1.0 / cycle[rows : rows + 1, :]
+        result.append(cycle[:rows] * row_scale * column_scale)
+    return result
+
+
+def dot_rows(left, right):
+    return lax.dot_general(
+        left, right, (((1,), (1,)), ((), ())), preferred_element_type=jnp.float32
+    )
+
+
+def cross_kernel(loop, groups, pairs, rows, time_major, *refs):
+    count_in = groups if time_major else loop
+    sources, outs, blocks = refs[:count_in], refs[count_in : count_in + loop], refs[-1]
+    t = lax.axis_index("tm")
+    for s in range(pairs):
+        at = slice(s * LANES, (s + 1) * LANES)
+        for j in range(loop):
+            for k in range(groups):
+                value = sources[k][j, :, at] if time_major else sources[j][k, :, at]
+                blocks[s, t ^ j, :, k * LANES : (k + 1) * LANES] = padded(value).astype(jnp.bfloat16)
+        for i in range(loop):
+            r = t ^ i
+            left = halves(blocks[s, r].astype(jnp.float32)).astype(jnp.bfloat16)
+            right = jnp.concatenate(
+                [blocks[s, (r + 1) % loop], blocks[s, (r + 2) % loop]], axis=0
+            )
+            for half, cycle in enumerate(normalized(dot_rows(left, right), rows)):
+                outs[i][2 * s + half] = cycle - 1.0
+
+
+def own_kernel(loop, groups, pairs, rows, *refs):
+    sources, out = refs[:groups], refs[groups]
+    for c in range(loop):
+        for s in range(pairs):
+            at = slice((c * pairs + s) * LANES, (c * pairs + s + 1) * LANES)
+            block = jnp.concatenate([padded(source[:, at]) for source in sources], axis=1)
+            left = halves(block).astype(jnp.bfloat16)
+            block = block.astype(jnp.bfloat16)
+            right = jnp.concatenate([block, block], axis=0)
+            for half, cycle in enumerate(normalized(dot_rows(left, right), rows)):
+                out[c, 2 * s + half] = cycle
+
+
+def place_kernel(rows, counts, me, *refs):
+    del me
+    out = refs[-1]
+    lane = lax.broadcasted_iota(jnp.int32, (rows, LANES), 1)
+    base = 0
+    for own, cross in zip(refs[0:-1:2], refs[1:-1:2]):
+        for c in range(own.shape[1]):
+            value = cross[0, c] + 1.0
+            one = pltpu.roll(value, rows, 1)
+            two = pltpu.roll(value, 2 * rows - CYCLE_CAP, 1)
+            out[base + c, :, :LANES] = jnp.where(
+                lane < rows, own[0, c], jnp.where(lane < 2 * rows, one, two)
+            )
+            out[base + c, :, LANES:] = two[:, : 3 * rows - LANES]
+        base += own.shape[1]
+
+
+def spread(frames, labels, first):
+    loop, groups = lax.axis_size("tm"), lax.axis_size("pix")
+    rows = frames.shape[0]
+    per = frames.shape[1] // (LANES * groups * loop)
+    rest = per - first
+    bf16, f32 = jnp.bfloat16, jnp.float32
+
+    def shape(*dims, dtype=bf16):
+        return jax.ShapeDtypeStruct(dims, dtype)
+
+    packed = local_call(
+        functools.partial(pack_kernel, loop, groups, per, first),
+        [shape(rows, groups * first * LANES)] * loop
+        + [shape(rows, loop * first * LANES)] * groups
+        + [shape(rows, loop * rest * LANES)] * groups,
+        2,
+    )(frames, labels.reshape(-1, LANES))
+    to_time, to_owner_first, to_owner_rest = packed[:loop], packed[loop : loop + groups], packed[loop + groups :]
+
+    def exchange(parts, axis):
+        moved = {j: swap(parts[j], axis, j) for j in range(len(parts) - 1, 0, -1)}
+        return [parts[0]] + [moved[j] for j in range(1, len(parts))]
+
+    def pick(parts, axis, width):
+        size = lax.axis_size(axis)
+        return local_call(
+            functools.partial(pick_kernel, axis, len(parts), width),
+            [shape(len(parts), rows, width)] * size,
+            len(parts),
+        )(*parts)
+
+    def cross(parts, pairs, time_major):
+        return local_call(
+            functools.partial(cross_kernel, loop, groups, pairs, rows, time_major),
+            [shape(2 * pairs, rows, LANES, dtype=f32)] * loop,
+            len(parts),
+            [pltpu.VMEM((pairs, loop, rows + 8, groups * LANES), bf16)],
+        )(*parts)
+
+    def send_back(tiles):
+        sent = lax.optimization_barrier([tile.astype(jnp.float16) for tile in tiles[1:]])
+        moved = {j: swap(sent[j - 1], "tm", j) for j in range(loop - 1, 0, -1)}
+        moved = lax.optimization_barrier(moved)
+        return jnp.stack([tiles[0]] + [moved[j].astype(f32) for j in range(1, loop)])
+
+    def own(parts, pairs):
+        return local_call(
+            functools.partial(own_kernel, loop, groups, pairs, rows),
+            [shape(loop, 2 * pairs, rows, LANES, dtype=f32)],
+            len(parts),
+        )(*parts)[0]
+
+    time_first = exchange(to_time, "tm")
+    owned_rest = exchange(to_owner_rest, "pix")
+    time_rest = exchange(pick(owned_rest, "tm", rest * LANES), "tm")
+    grouped_first = exchange(pick(time_first, "pix", first * LANES), "pix")
+    owned_first = exchange(to_owner_first, "pix")
+    own_rest = own(owned_rest, rest)
+    back_first = send_back(cross(grouped_first, first, True))
+    back_rest = send_back(cross(time_rest, rest, False))
+    own_first = own(owned_first, first)
+
+    me = lax.axis_index("tm").astype(jnp.int32)[None]
+    cycles = 2 * per
+
+    def part(pairs, order):
+        return pl.BlockSpec((1, 2 * pairs, rows, LANES), order)
+
+    return pl.pallas_call(
+        functools.partial(place_kernel, rows, (first, rest)),
+        out_shape=shape(loop * cycles, rows, 3 * rows, dtype=f32),
+        grid_spec=pltpu.PrefetchScalarGridSpec(
+            num_scalar_prefetch=1,
+            grid=(loop,),
+            in_specs=[
+                part(first, lambda i, t: (t[0] ^ i, 0, 0, 0)),
+                part(first, lambda i, t: (i, 0, 0, 0)),
+                part(rest, lambda i, t: (t[0] ^ i, 0, 0, 0)),
+                part(rest, lambda i, t: (i, 0, 0, 0)),
+            ],
+            out_specs=pl.BlockSpec((cycles, rows, 3 * rows), lambda i, t: (t[0] ^ i, 0, 0)),
+        ),
+        compiler_params=pltpu.CompilerParams(vmem_limit_bytes=VMEM_LIMIT),
+    )(me, own_first, back_first, own_rest, back_rest)
+
+
+def on_device(frames, labels):
+    loop, groups = lax.axis_size("tm"), lax.axis_size("pix")
+    pairs = CYCLES // groups // 2
+    powers = groups & (groups - 1) == 0
+    fits = frames.shape[1] == CYCLES * CYCLE_CAP and frames.shape[0] == CYCLE_CAP - 8
+    if loop == 4 and powers and fits and pairs % loop == 0 and pairs // loop >= 2:
+        return spread(frames, labels, pairs // loop // 2)
+    return ring(frames, labels)
+
+
 def solution(mesh):
     placed = (P(("runs", "tm"), "pix"), P("pix"))
     return jax.shard_map(

time: 115 us -> 50.8 us (0.44)
  waiting for transfers between devices: 52.1 us -> 12.8 us
  local copies, waits for them, and re-layouts: 30.4 us -> 1.94 us
  starting transfers between devices: 16.2 us -> 30.6 us
  matrix products: 11 us -> 0 us
  Pallas kernels: 0 us -> 4.87 us
  other arithmetic: 4.37 us -> 0.2 us
    ppermute x2 -> x21, waiting for transfers between devices: 37.8 us -> 12.8 us  [swap(): return lax.ppermute(shard, axis, [(i, i ^ by) for i in range(size)])]
    ppermute x2 -> x21, starting transfers between devices: 8.44 us -> 30.6 us  [swap(): return lax.ppermute(shard, axis, [(i, i ^ by) for i in range(size)])]
    dynamic_update_slice x3 -> x0, local copies, waits for them, and re-layouts: 19.5 us -> none  [the longest x2 18.1 us: advance(): lax.dynamic_update_slice(result, make_tiles(moving[None]), (0, 0, offset...]
    all_to_all x2 -> x0, waiting for transfers between devices: 14.3 us -> none  [the longest x1 12.8 us: on_device(): lax.all_to_all(masked, 'pix', split_axis=1, concat_axis=1, tiled=True)]
    dot_general x3 -> x0, matrix products: 11 us -> none  [make_tiles(): jnp.einsum('tgqc,nsgqc->qtns', own_split, block_split, preferred_element_...]
    all_to_all x2 -> x0, starting transfers between devices: 7.71 us -> none  [the longest x1 4.21 us: on_device(): lax.all_to_all(live_row, 'pix', split_axis=1, concat_axis=1, tiled=True)]
    pallas_call x0 -> x8, Pallas kernels: none -> 4.87 us  [the longest x1 2.14 us: spread(): pl.pallas_call(functools.partial(place_kernel, rows, (first, rest)), out_...]
    another operation x2 -> x0, local copies, waits for them, and re-layouts: 3.88 us -> none
  transfers between devices with their start and end apart: 4 -> 21, of which waited for: 4 -> 5; matrix products, arithmetic and copies ran while one was open for 2% -> 0% of each run, Pallas kernels for 0% -> 5%
where the time goes in v1:
time: 50.8 us; the launch traced here: 50.6 us
  starting transfers between devices  30.6 us (60%)
  waiting for transfers between devices  12.8 us (25%)
  Pallas kernels  4.87 us (10%)
  local copies, waits for them, and re-layouts  1.94 us (4%)
    ppermute x21, starting transfers between devices, swap(): return lax.ppermute(shard, axis, [(i, i ^ by) for i in range(size)])  30.6 us
    ppermute x21, waiting for transfers between devices, swap(): return lax.ppermute(shard, axis, [(i, i ^ by) for i in range(size)])  12.8 us
    pallas_call x1, Pallas kernels, spread(): pl.pallas_call(functools.partial(place_kernel, rows, (first, rest)), out_...  2.14 us
    unnamed x4, local copies, waits for them, and re-layouts  1.94 us
    pallas_call x2, Pallas kernels, cross(): local_call(functools.partial(cross_kernel, loop, groups, pairs, rows, tim...  1.17 us
    pallas_call x2, Pallas kernels, own(): local_call(functools.partial(own_kernel, loop, groups, pairs, rows), [sha...  1.06 us
  transfers between devices with their start and end apart: 21, of which 5 were waited for; matrix products, arithmetic and copies ran while one was open for 0% of the time, Pallas kernels for 5%

profile of v1, /device:TPU:0, one launch (start us, length us, event | category | flops | bytes accessed | tf_op | source)
XLA Modules:
  0.0 50.6 jit_solution(2333576484687866851)
XLA Ops:
  0.0 1.2 %copy-done = bf16[56,8192]{1,0:T(8,128)(2,1)S(1)} copy-done((bf16[56,8192]{1,0:T(8,128)(2,1)S(1)}, bf16[56,8192]{1,0:T(8,128)(2,1)}, u32[]{:S(2)}) %copy-start) | copy-done | bytes 917528
  1.2 0.8 %copy-done.1 = s32[8192]{0:T(1024)S(1)} copy-done((s32[8192]{0:T(1024)S(1)}, s32[8192]{0:T(1024)}, u32[]{:S(2)}) %copy-start.1) | copy-done | bytes 32792
  1.9 0.4 shard_map.28
  2.3 3.1 %collective-permute-start.3 = (bf16[56,1024]{1,0:T(8,128)(2,1)S(1)}, bf16[56,1024]{1,0:T(8,128)(2,1)S(1)}, u32[]{:S(2)}, u32[]{:S(2)}) collective-permute-start(bf16[56,1024]{1,0:T(8,128)(2,1)S(1)} %get-tuple-element.50), channel_id=1, source_target_pairs={{0,4},{4,0},{8,12},{12,8},{1,5},{5,1},{9,13},{13,9},{2,6},{6,2},{1... | collective-permute-start | bytes 344072 | tf_op jit(solution)/shard_map/ppermute | solution.py:23
  5.4 2.6 %collective-permute-start.4 = (bf16[56,1024]{1,0:T(8,128)(2,1)S(1)}, bf16[56,1024]{1,0:T(8,128)(2,1)S(1)}, u32[]{:S(2)}, u32[]{:S(2)}) collective-permute-start(bf16[56,1024]{1,0:T(8,128)(2,1)S(1)} %get-tuple-element.51), channel_id=1, source_target_pairs={{0,8},{4,12},{8,0},{12,4},{1,9},{5,13},{9,1},{13,5},{2,10},{6,14},... | collective-permute-start | bytes 344072 | tf_op jit(solution)/shard_map/ppermute | solution.py:23
  8.0 1.7 %collective-permute-start.13 = (bf16[56,1024]{1,0:T(8,128)(2,1)S(1)}, bf16[56,1024]{1,0:T(8,128)(2,1)S(1)}, u32[]{:S(2)}, u32[]{:S(2)}) collective-permute-start(bf16[56,1024]{1,0:T(8,128)(2,1)S(1)} %get-tuple-element.69), channel_id=1, source_target_pairs={{0,2},{1,3},{2,0},{3,1},{4,6},{5,7},{6,4},{7,5},{8,10},{9,11},{10,... | collective-permute-start | bytes 344072 | tf_op jit(solution)/shard_map/ppermute | solution.py:23
  9.7 0.1 collective-permute-start.14
  9.9 7.2 %collective-permute-done.4.refs_2_ = bf16[56,1024]{1,0:T(8,128)(2,1)S(1)} collective-permute-done((bf16[56,1024]{1,0:T(8,128)(2,1)S(1)}, bf16[56,1024]{1,0:T(8,128)(2,1)S(1)}, u32[]{:S(2)}, u32[]{:S(2)}) %collective-permute-start.4) | collective-permute-done | bytes 114720 | tf_op jit(solution)/shard_map/ppermute | solution.py:23
  17.1 0.1 shard_map.30
  17.2 0.6 %collective-permute-start.6 = (bf16[4,56,256]{2,1,0:T(8,128)(2,1)S(1)}, bf16[4,56,256]{2,1,0:T(8,128)(2,1)S(1)}, u32[]{:S(2)}, u32[]{:S(2)}) collective-permute-start(bf16[4,56,256]{2,1,0:T(8,128)(2,1)S(1)} %get-tuple-element.54), channel_id=1, source_target_pairs={{0,1},{1,0},{2,3},{3,2},{4,5},{5,4},{6,7},{7,6},{8,9},{9,8},{10,11... | collective-permute-start | bytes 344072 | tf_op jit(solution)/shard_map/ppermute | solution.py:23
  17.7 1.5 %collective-permute-start.7 = (bf16[4,56,256]{2,1,0:T(8,128)(2,1)S(1)}, bf16[4,56,256]{2,1,0:T(8,128)(2,1)S(1)}, u32[]{:S(2)}, u32[]{:S(2)}) collective-permute-start(bf16[4,56,256]{2,1,0:T(8,128)(2,1)S(1)} %get-tuple-element.55), channel_id=1, source_target_pairs={{0,2},{1,3},{2,0},{3,1},{4,6},{5,7},{6,4},{7,5},{8,10},{9,11},{10,... | collective-permute-start | bytes 344072 | tf_op jit(solution)/shard_map/ppermute | solution.py:23
  19.2 1.4 %collective-permute-start.1 = (bf16[56,1024]{1,0:T(8,128)(2,1)S(1)}, bf16[56,1024]{1,0:T(8,128)(2,1)S(1)}, u32[]{:S(2)}, u32[]{:S(2)}) collective-permute-start(bf16[56,1024]{1,0:T(8,128)(2,1)S(1)} %get-tuple-element.47), channel_id=1, source_target_pairs={{0,2},{1,3},{2,0},{3,1},{4,6},{5,7},{6,4},{7,5},{8,10},{9,11},{10,... | collective-permute-start | bytes 344072 | tf_op jit(solution)/shard_map/ppermute | solution.py:23
  20.7 0.1 shard_map.33
  20.8 0.6 %collective-permute-start.2 = (bf16[56,1024]{1,0:T(8,128)(2,1)S(1)}, bf16[56,1024]{1,0:T(8,128)(2,1)S(1)}, u32[]{:S(2)}, u32[]{:S(2)}) collective-permute-start(bf16[56,1024]{1,0:T(8,128)(2,1)S(1)} %get-tuple-element.48), channel_id=1, source_target_pairs={{0,3},{1,2},{2,1},{3,0},{4,7},{5,6},{6,5},{7,4},{8,11},{9,10},{10,... | collective-permute-start | bytes 344072 | tf_op jit(solution)/shard_map/ppermute | solution.py:23
  21.4 1.4 %collective-permute-start.15 = (bf16[4,56,256]{2,1,0:T(8,128)(2,1)S(1)}, bf16[4,56,256]{2,1,0:T(8,128)(2,1)S(1)}, u32[]{:S(2)}, u32[]{:S(2)}) collective-permute-start(bf16[4,56,256]{2,1,0:T(8,128)(2,1)S(1)} %get-tuple-element.72), channel_id=1, source_target_pairs={{0,4},{4,0},{8,12},{12,8},{1,5},{5,1},{9,13},{13,9},{2,6},{6,2},{1... | collective-permute-start | bytes 344072 | tf_op jit(solution)/shard_map/ppermute | solution.py:23
  22.8 0.8 %collective-permute-done.7.refs_2_ = bf16[4,56,256]{2,1,0:T(8,128)(2,1)S(1)} collective-permute-done((bf16[4,56,256]{2,1,0:T(8,128)(2,1)S(1)}, bf16[4,56,256]{2,1,0:T(8,128)(2,1)S(1)}, u32[]{:S(2)}, u32[]{:S(2)}) %collective-permute-start.7) | collective-permute-done | bytes 114720 | tf_op jit(solution)/shard_map/ppermute | solution.py:23
  23.5 2.5 %collective-permute-start.16 = (bf16[4,56,256]{2,1,0:T(8,128)(2,1)S(1)}, bf16[4,56,256]{2,1,0:T(8,128)(2,1)S(1)}, u32[]{:S(2)}, u32[]{:S(2)}) collective-permute-start(bf16[4,56,256]{2,1,0:T(8,128)(2,1)S(1)} %get-tuple-element.73), channel_id=1, source_target_pairs={{0,8},{4,12},{8,0},{12,4},{1,9},{5,13},{9,1},{13,5},{2,10},{6,14},... | collective-permute-start | bytes 344072 | tf_op jit(solution)/shard_map/ppermute | solution.py:23
  26.1 1.6 %collective-permute-start.17 = (bf16[4,56,256]{2,1,0:T(8,128)(2,1)S(1)}, bf16[4,56,256]{2,1,0:T(8,128)(2,1)S(1)}, u32[]{:S(2)}, u32[]{:S(2)}) collective-permute-start(bf16[4,56,256]{2,1,0:T(8,128)(2,1)S(1)} %get-tuple-element.74), channel_id=1, source_target_pairs={{0,12},{4,8},{8,4},{12,0},{1,13},{5,9},{9,5},{13,1},{2,14},{6,10},... | collective-permute-start | bytes 344072 | tf_op jit(solution)/shard_map/ppermute | solution.py:23
  27.7 0.6 %shard_map.31 = (f32[4,56,128]{2,1,0:T(8,128)S(1)}, f32[4,56,128]{2,1,0:T(8,128)S(1)}, f32[4,56,128]{2,1,0:T(8,128)S(1)}, f32[4,56,128]{2,1,0:T(8,128)S(1)}) custom-call(bf16[4,56,256]{2,1,0:T(8,128)(2,1)S(1)} %get-tuple-element.53.refs_0_, bf16[4,56,256]{2,1,0:T(8,128)(2,1)S(1)} %collective-permute-done.6.refs_1_, ...), custom_call_target="tpu_custom_call" | custom-call | tf_op jit(solution)/shard_map/pallas_call | solution.py:241
  28.3 0.1 collective-permute-done.1.refs_2_
  28.5 1.5 %collective-permute-start.9 = (f16[4,56,128]{2,1,0:T(8,128)(2,1)S(1)}, f16[4,56,128]{2,1,0:T(8,128)(2,1)S(1)}, u32[]{:S(2)}, u32[]{:S(2)}) collective-permute-start(f16[4,56,128]{2,1,0:T(8,128)(2,1)S(1)} %convert_element_type.24), channel_id=1, source_target_pairs={{0,4},{4,0},{8,12},{12,8},{1,5},{5,1},{9,13},{13,9},{2,6},{6,2},{1... | collective-permute-start | bytes 172040 | tf_op jit(solution)/shard_map/ppermute | solution.py:23
  30.0 2.5 %collective-permute-start.10 = (f16[4,56,128]{2,1,0:T(8,128)(2,1)S(1)}, f16[4,56,128]{2,1,0:T(8,128)(2,1)S(1)}, u32[]{:S(2)}, u32[]{:S(2)}) collective-permute-start(f16[4,56,128]{2,1,0:T(8,128)(2,1)S(1)} %convert_element_type.25), channel_id=1, source_target_pairs={{0,8},{4,12},{8,0},{12,4},{1,9},{5,13},{9,1},{13,5},{2,10},{6,14},... | collective-permute-start | bytes 172040 | tf_op jit(solution)/shard_map/ppermute | solution.py:23
  32.5 1.3 %collective-permute-start.11 = (f16[4,56,128]{2,1,0:T(8,128)(2,1)S(1)}, f16[4,56,128]{2,1,0:T(8,128)(2,1)S(1)}, u32[]{:S(2)}, u32[]{:S(2)}) collective-permute-start(f16[4,56,128]{2,1,0:T(8,128)(2,1)S(1)} %convert_element_type.26), channel_id=1, source_target_pairs={{0,12},{4,8},{8,4},{12,0},{1,13},{5,9},{9,5},{13,1},{2,14},{6,10},... | collective-permute-start | bytes 172040 | tf_op jit(solution)/shard_map/ppermute | solution.py:23
  33.9 0.5 %shard_map.32.refs_2_ = f32[4,4,56,128]{3,2,1,0:T(8,128)S(1)} custom-call(bf16[56,1024]{1,0:T(8,128)(2,1)S(1)} %get-tuple-element.67.refs_0_, bf16[56,1024]{1,0:T(8,128)(2,1)S(1)} %collective-permute-done.12.refs_1_, bf16[56,1024]{1,0:T(8,128)(2,1)S(1)} %collective-permute-done.13.refs_2_, bf16[56,1024]{1,0:T(8,128)(2,1)S(1)} %collective-permute-done.14.refs_3_), custom_call_target="tpu_custom_call" | custom-call | tf_op jit(solution)/shard_map/pallas_call | solution.py:255
  34.4 0.5 %shard_map.29.refs_0_ = f32[4,4,56,128]{3,2,1,0:T(8,128)S(1)} custom-call(bf16[56,1024]{1,0:T(8,128)(2,1)S(1)} %get-tuple-element.45.refs_0_, bf16[56,1024]{1,0:T(8,128)(2,1)S(1)} %collective-permute-done.refs_1_, bf16[56,1024]{1,0:T(8,128)(2,1)S(1)} %collective-permute-done.1.refs_2_, bf16[56,1024]{1,0:T(8,128)(2,1)S(1)} %collective-permute-done.2.refs_3_), custom_call_target="tpu_custom_call" | custom-call | tf_op jit(solution)/shard_map/pallas_call | solution.py:255
  35.0 0.6 %shard_map.34 = (f32[4,56,128]{2,1,0:T(8,128)S(1)}, f32[4,56,128]{2,1,0:T(8,128)S(1)}, f32[4,56,128]{2,1,0:T(8,128)S(1)}, f32[4,56,128]{2,1,0:T(8,128)S(1)}) custom-call(bf16[4,56,256]{2,1,0:T(8,128)(2,1)S(1)} %get-tuple-element.71.refs_0_, bf16[4,56,256]{2,1,0:T(8,128)(2,1)S(1)} %collective-permute-done.15.refs_1_, ...), custom_call_target="tpu_custom_call" | custom-call | tf_op jit(solution)/shard_map/pallas_call | solution.py:241
  35.6 5.1 %collective-permute-start.18 = (f16[4,56,128]{2,1,0:T(8,128)(2,1)S(1)}, f16[4,56,128]{2,1,0:T(8,128)(2,1)S(1)}, u32[]{:S(2)}, u32[]{:S(2)}) collective-permute-start(f16[4,56,128]{2,1,0:T(8,128)(2,1)S(1)} %convert_element_type.27), channel_id=1, source_target_pairs={{0,4},{4,0},{8,12},{12,8},{1,5},{5,1},{9,13},{13,9},{2,6},{6,2},{1... | collective-permute-start | bytes 172040 | tf_op jit(solution)/shard_map/ppermute | solution.py:23
  40.8 1.5 %collective-permute-start.19 = (f16[4,56,128]{2,1,0:T(8,128)(2,1)S(1)}, f16[4,56,128]{2,1,0:T(8,128)(2,1)S(1)}, u32[]{:S(2)}, u32[]{:S(2)}) collective-permute-start(f16[4,56,128]{2,1,0:T(8,128)(2,1)S(1)} %convert_element_type.28), channel_id=1, source_target_pairs={{0,8},{4,12},{8,0},{12,4},{1,9},{5,13},{9,1},{13,5},{2,10},{6,14},... | collective-permute-start | bytes 172040 | tf_op jit(solution)/shard_map/ppermute | solution.py:23
  42.2 1.4 %collective-permute-start.20 = (f16[4,56,128]{2,1,0:T(8,128)(2,1)S(1)}, f16[4,56,128]{2,1,0:T(8,128)(2,1)S(1)}, u32[]{:S(2)}, u32[]{:S(2)}) collective-permute-start(f16[4,56,128]{2,1,0:T(8,128)(2,1)S(1)} %convert_element_type.29), channel_id=1, source_target_pairs={{0,12},{4,8},{8,4},{12,0},{1,13},{5,9},{9,5},{13,1},{2,14},{6,10},... | collective-permute-start | bytes 172040 | tf_op jit(solution)/shard_map/ppermute | solution.py:23
  43.7 3.2 %collective-permute-done.19 = f16[4,56,128]{2,1,0:T(8,128)(2,1)S(1)} collective-permute-done((f16[4,56,128]{2,1,0:T(8,128)(2,1)S(1)}, f16[4,56,128]{2,1,0:T(8,128)(2,1)S(1)}, u32[]{:S(2)}, u32[]{:S(2)}) %collective-permute-start.19) | collective-permute-done | bytes 57376 | tf_op jit(solution)/shard_map/ppermute | solution.py:23
  46.8 1.5 %collective-permute-done.20 = f16[4,56,128]{2,1,0:T(8,128)(2,1)S(1)} collective-permute-done((f16[4,56,128]{2,1,0:T(8,128)(2,1)S(1)}, f16[4,56,128]{2,1,0:T(8,128)(2,1)S(1)}, u32[]{:S(2)}, u32[]{:S(2)}) %collective-permute-start.20) | collective-permute-done | bytes 57376 | tf_op jit(solution)/shard_map/ppermute | solution.py:23
  48.5 2.1 %shard_map.35 = f32[32,56,168]{2,1,0:T(8,128)} custom-call(s32[1]{0:T(128)} %bitcast.me, f32[4,4,56,128]{3,2,1,0:T(8,128)S(1)} %shard_map.29.refs_0_, f32[4,4,56,128]{3,2,1,0:T(8,128)S(1)} %pad_maximum_fusion.refs_1_, f32[4,4,56,128]{3,2,1,0:T(8,128)S(1)} %shard_map.32.refs_2_, f32[4,4,56,128]{3,2,1,0:T(8,128)S(1)} %pad_maximum_fusion.1.refs_3_), custom_call_target="tpu_custom_call" | custom-call | tf_op jit(solution)/shard_map/pallas_call | solution.py:277
  (34 shorter events, 0.3 us)
Async XLA Ops:
  0.0 1.2 %copy-start = (bf16[56,8192]{1,0:T(8,128)(2,1)S(1)}, bf16[56,8192]{1,0:T(8,128)(2,1)}, u32[]{:S(2)}) copy-start(bf16[56,8192]{1,0:T(8,128)(2,1)} %frames.1) | copy-start | bytes 2752516
  1.2 0.8 %copy-start.1 = (s32[8192]{0:T(1024)S(1)}, s32[8192]{0:T(1024)}, u32[]{:S(2)}) copy-start(s32[8192]{0:T(1024)} %param.3) | copy-start | bytes 98308
  2.3 7.4 %collective-permute-start.3 = (bf16[56,1024]{1,0:T(8,128)(2,1)S(1)}, bf16[56,1024]{1,0:T(8,128)(2,1)S(1)}, u32[]{:S(2)}, u32[]{:S(2)}) collective-permute-start(bf16[56,1024]{1,0:T(8,128)(2,1)S(1)} %get-tuple-element.50), channel_id=1, source_target_pairs={{0,4},{4,0},{8,12},{12,8},{1,5},{5,1},{9,13},{13,9},{2,6},{6,2},{1... | collective-permute-start | bytes 344072 | tf_op jit(solution)/shard_map/ppermute | solution.py:23
  5.4 11.7 %collective-permute-start.4 = (bf16[56,1024]{1,0:T(8,128)(2,1)S(1)}, bf16[56,1024]{1,0:T(8,128)(2,1)S(1)}, u32[]{:S(2)}, u32[]{:S(2)}) collective-permute-start(bf16[56,1024]{1,0:T(8,128)(2,1)S(1)} %get-tuple-element.51), channel_id=1, source_target_pairs={{0,8},{4,12},{8,0},{12,4},{1,9},{5,13},{9,1},{13,5},{2,10},{6,14},... | collective-permute-start | bytes 344072 | tf_op jit(solution)/shard_map/ppermute | solution.py:23
  8.0 9.1 %collective-permute-start.5 = (bf16[56,1024]{1,0:T(8,128)(2,1)S(1)}, bf16[56,1024]{1,0:T(8,128)(2,1)S(1)}, u32[]{:S(2)}, u32[]{:S(2)}) collective-permute-start(bf16[56,1024]{1,0:T(8,128)(2,1)S(1)} %get-tuple-element.52), channel_id=1, source_target_pairs={{0,12},{4,8},{8,4},{12,0},{1,13},{5,9},{9,5},{13,1},{2,14},{6,10},... | collective-permute-start | bytes 344072 | tf_op jit(solution)/shard_map/ppermute | solution.py:23
  8.0 9.7 %collective-permute-start.12 = (bf16[56,1024]{1,0:T(8,128)(2,1)S(1)}, bf16[56,1024]{1,0:T(8,128)(2,1)S(1)}, u32[]{:S(2)}, u32[]{:S(2)}) collective-permute-start(bf16[56,1024]{1,0:T(8,128)(2,1)S(1)} %get-tuple-element.68), channel_id=1, source_target_pairs={{0,1},{1,0},{2,3},{3,2},{4,5},{5,4},{6,7},{7,6},{8,9},{9,8},{10,11... | collective-permute-start | bytes 344072 | tf_op jit(solution)/shard_map/ppermute | solution.py:23
  8.0 11.2 %collective-permute-start.13 = (bf16[56,1024]{1,0:T(8,128)(2,1)S(1)}, bf16[56,1024]{1,0:T(8,128)(2,1)S(1)}, u32[]{:S(2)}, u32[]{:S(2)}) collective-permute-start(bf16[56,1024]{1,0:T(8,128)(2,1)S(1)} %get-tuple-element.69), channel_id=1, source_target_pairs={{0,2},{1,3},{2,0},{3,1},{4,6},{5,7},{6,4},{7,5},{8,10},{9,11},{10,... | collective-permute-start | bytes 344072 | tf_op jit(solution)/shard_map/ppermute | solution.py:23
  9.7 9.5 %collective-permute-start.14 = (bf16[56,1024]{1,0:T(8,128)(2,1)S(1)}, bf16[56,1024]{1,0:T(8,128)(2,1)S(1)}, u32[]{:S(2)}, u32[]{:S(2)}) collective-permute-start(bf16[56,1024]{1,0:T(8,128)(2,1)S(1)} %get-tuple-element.70), channel_id=1, source_target_pairs={{0,3},{1,2},{2,1},{3,0},{4,7},{5,6},{6,5},{7,4},{8,11},{9,10},{10,... | collective-permute-start | bytes 344072 | tf_op jit(solution)/shard_map/ppermute | solution.py:23
  17.1 3.6 %collective-permute-start = (bf16[56,1024]{1,0:T(8,128)(2,1)S(1)}, bf16[56,1024]{1,0:T(8,128)(2,1)S(1)}, u32[]{:S(2)}, u32[]{:S(2)}) collective-permute-start(bf16[56,1024]{1,0:T(8,128)(2,1)S(1)} %get-tuple-element.46), channel_id=1, source_target_pairs={{0,1},{1,0},{2,3},{3,2},{4,5},{5,4},{6,7},{7,6},{8,9},{9,8},{10,11... | collective-permute-start | bytes 344072 | tf_op jit(solution)/shard_map/ppermute | solution.py:23
  17.2 4.2 %collective-permute-start.6 = (bf16[4,56,256]{2,1,0:T(8,128)(2,1)S(1)}, bf16[4,56,256]{2,1,0:T(8,128)(2,1)S(1)}, u32[]{:S(2)}, u32[]{:S(2)}) collective-permute-start(bf16[4,56,256]{2,1,0:T(8,128)(2,1)S(1)} %get-tuple-element.54), channel_id=1, source_target_pairs={{0,1},{1,0},{2,3},{3,2},{4,5},{5,4},{6,7},{7,6},{8,9},{9,8},{10,11... | collective-permute-start | bytes 344072 | tf_op jit(solution)/shard_map/ppermute | solution.py:23
  17.7 5.8 %collective-permute-start.7 = (bf16[4,56,256]{2,1,0:T(8,128)(2,1)S(1)}, bf16[4,56,256]{2,1,0:T(8,128)(2,1)S(1)}, u32[]{:S(2)}, u32[]{:S(2)}) collective-permute-start(bf16[4,56,256]{2,1,0:T(8,128)(2,1)S(1)} %get-tuple-element.55), channel_id=1, source_target_pairs={{0,2},{1,3},{2,0},{3,1},{4,6},{5,7},{6,4},{7,5},{8,10},{9,11},{10,... | collective-permute-start | bytes 344072 | tf_op jit(solution)/shard_map/ppermute | solution.py:23
  19.2 6.8 %collective-permute-start.8 = (bf16[4,56,256]{2,1,0:T(8,128)(2,1)S(1)}, bf16[4,56,256]{2,1,0:T(8,128)(2,1)S(1)}, u32[]{:S(2)}, u32[]{:S(2)}) collective-permute-start(bf16[4,56,256]{2,1,0:T(8,128)(2,1)S(1)} %get-tuple-element.56), channel_id=1, source_target_pairs={{0,3},{1,2},{2,1},{3,0},{4,7},{5,6},{6,5},{7,4},{8,11},{9,10},{10,... | collective-permute-start | bytes 344072 | tf_op jit(solution)/shard_map/ppermute | solution.py:23
  19.2 9.2 %collective-permute-start.1 = (bf16[56,1024]{1,0:T(8,128)(2,1)S(1)}, bf16[56,1024]{1,0:T(8,128)(2,1)S(1)}, u32[]{:S(2)}, u32[]{:S(2)}) collective-permute-start(bf16[56,1024]{1,0:T(8,128)(2,1)S(1)} %get-tuple-element.47), channel_id=1, source_target_pairs={{0,2},{1,3},{2,0},{3,1},{4,6},{5,7},{6,4},{7,5},{8,10},{9,11},{10,... | collective-permute-start | bytes 344072 | tf_op jit(solution)/shard_map/ppermute | solution.py:23
  20.8 9.2 %collective-permute-start.2 = (bf16[56,1024]{1,0:T(8,128)(2,1)S(1)}, bf16[56,1024]{1,0:T(8,128)(2,1)S(1)}, u32[]{:S(2)}, u32[]{:S(2)}) collective-permute-start(bf16[56,1024]{1,0:T(8,128)(2,1)S(1)} %get-tuple-element.48), channel_id=1, source_target_pairs={{0,3},{1,2},{2,1},{3,0},{4,7},{5,6},{6,5},{7,4},{8,11},{9,10},{10,... | collective-permute-start | bytes 344072 | tf_op jit(solution)/shard_map/ppermute | solution.py:23
  21.4 11.1 %collective-permute-start.15 = (bf16[4,56,256]{2,1,0:T(8,128)(2,1)S(1)}, bf16[4,56,256]{2,1,0:T(8,128)(2,1)S(1)}, u32[]{:S(2)}, u32[]{:S(2)}) collective-permute-start(bf16[4,56,256]{2,1,0:T(8,128)(2,1)S(1)} %get-tuple-element.72), channel_id=1, source_target_pairs={{0,4},{4,0},{8,12},{12,8},{1,5},{5,1},{9,13},{13,9},{2,6},{6,2},{1... | collective-permute-start | bytes 344072 | tf_op jit(solution)/shard_map/ppermute | solution.py:23
  23.5 11.4 %collective-permute-start.16 = (bf16[4,56,256]{2,1,0:T(8,128)(2,1)S(1)}, bf16[4,56,256]{2,1,0:T(8,128)(2,1)S(1)}, u32[]{:S(2)}, u32[]{:S(2)}) collective-permute-start(bf16[4,56,256]{2,1,0:T(8,128)(2,1)S(1)} %get-tuple-element.73), channel_id=1, source_target_pairs={{0,8},{4,12},{8,0},{12,4},{1,9},{5,13},{9,1},{13,5},{2,10},{6,14},... | collective-permute-start | bytes 344072 | tf_op jit(solution)/shard_map/ppermute | solution.py:23
  26.1 8.9 %collective-permute-start.17 = (bf16[4,56,256]{2,1,0:T(8,128)(2,1)S(1)}, bf16[4,56,256]{2,1,0:T(8,128)(2,1)S(1)}, u32[]{:S(2)}, u32[]{:S(2)}) collective-permute-start(bf16[4,56,256]{2,1,0:T(8,128)(2,1)S(1)} %get-tuple-element.74), channel_id=1, source_target_pairs={{0,12},{4,8},{8,4},{12,0},{1,13},{5,9},{9,5},{13,1},{2,14},{6,10},... | collective-permute-start | bytes 344072 | tf_op jit(solution)/shard_map/ppermute | solution.py:23
  28.5 13.8 %collective-permute-start.9 = (f16[4,56,128]{2,1,0:T(8,128)(2,1)S(1)}, f16[4,56,128]{2,1,0:T(8,128)(2,1)S(1)}, u32[]{:S(2)}, u32[]{:S(2)}) collective-permute-start(f16[4,56,128]{2,1,0:T(8,128)(2,1)S(1)} %convert_element_type.24), channel_id=1, source_target_pairs={{0,4},{4,0},{8,12},{12,8},{1,5},{5,1},{9,13},{13,9},{2,6},{6,2},{1... | collective-permute-start | bytes 172040 | tf_op jit(solution)/shard_map/ppermute | solution.py:23
  30.0 13.7 %collective-permute-start.10 = (f16[4,56,128]{2,1,0:T(8,128)(2,1)S(1)}, f16[4,56,128]{2,1,0:T(8,128)(2,1)S(1)}, u32[]{:S(2)}, u32[]{:S(2)}) collective-permute-start(f16[4,56,128]{2,1,0:T(8,128)(2,1)S(1)} %convert_element_type.25), channel_id=1, source_target_pairs={{0,8},{4,12},{8,0},{12,4},{1,9},{5,13},{9,1},{13,5},{2,10},{6,14},... | collective-permute-start | bytes 172040 | tf_op jit(solution)/shard_map/ppermute | solution.py:23
  32.5 11.1 %collective-permute-start.11 = (f16[4,56,128]{2,1,0:T(8,128)(2,1)S(1)}, f16[4,56,128]{2,1,0:T(8,128)(2,1)S(1)}, u32[]{:S(2)}, u32[]{:S(2)}) collective-permute-start(f16[4,56,128]{2,1,0:T(8,128)(2,1)S(1)} %convert_element_type.26), channel_id=1, source_target_pairs={{0,12},{4,8},{8,4},{12,0},{1,13},{5,9},{9,5},{13,1},{2,14},{6,10},... | collective-permute-start | bytes 172040 | tf_op jit(solution)/shard_map/ppermute | solution.py:23
  35.6 8.0 %collective-permute-start.18 = (f16[4,56,128]{2,1,0:T(8,128)(2,1)S(1)}, f16[4,56,128]{2,1,0:T(8,128)(2,1)S(1)}, u32[]{:S(2)}, u32[]{:S(2)}) collective-permute-start(f16[4,56,128]{2,1,0:T(8,128)(2,1)S(1)} %convert_element_type.27), channel_id=1, source_target_pairs={{0,4},{4,0},{8,12},{12,8},{1,5},{5,1},{9,13},{13,9},{2,6},{6,2},{1... | collective-permute-start | bytes 172040 | tf_op jit(solution)/shard_map/ppermute | solution.py:23
  40.8 6.1 %collective-permute-start.19 = (f16[4,56,128]{2,1,0:T(8,128)(2,1)S(1)}, f16[4,56,128]{2,1,0:T(8,128)(2,1)S(1)}, u32[]{:S(2)}, u32[]{:S(2)}) collective-permute-start(f16[4,56,128]{2,1,0:T(8,128)(2,1)S(1)} %convert_element_type.28), channel_id=1, source_target_pairs={{0,8},{4,12},{8,0},{12,4},{1,9},{5,13},{9,1},{13,5},{2,10},{6,14},... | collective-permute-start | bytes 172040 | tf_op jit(solution)/shard_map/ppermute | solution.py:23
  42.2 6.1 %collective-permute-start.20 = (f16[4,56,128]{2,1,0:T(8,128)(2,1)S(1)}, f16[4,56,128]{2,1,0:T(8,128)(2,1)S(1)}, u32[]{:S(2)}, u32[]{:S(2)}) collective-permute-start(f16[4,56,128]{2,1,0:T(8,128)(2,1)S(1)} %convert_element_type.29), channel_id=1, source_target_pairs={{0,12},{4,8},{8,4},{12,0},{1,13},{5,9},{9,5},{13,1},{2,14},{6,10},... | collective-permute-start | bytes 172040 | tf_op jit(solution)/shard_map/ppermute | solution.py:23

commit v2 on v0

--- a/solution.py
+++ b/solution.py
@@ -1,10 +1,17 @@
+import functools
+
 import jax
 import jax.numpy as jnp
 from jax import lax
+from jax.experimental import pallas as pl
+from jax.experimental.pallas import tpu as pltpu
 from jax.sharding import PartitionSpec as P
 
 CYCLES = 128
 CYCLE_CAP = 64
+LANES = 128
+VMEM_LIMIT = 48 * 2**20
+OWN_COST, PLACE_COST = 4 << 20, 4 << 20
 
 
 def from_behind(shard, axis, by):
@@ -12,7 +19,12 @@
     return lax.ppermute(shard, axis, [(i, (i + by) % size) for i in range(size)])
 
 
-def on_device(frames, labels):
+def swap(shard, axis, by):
+    size = lax.axis_size(axis)
+    return lax.ppermute(shard, axis, [(i, i ^ by) for i in range(size)])
+
+
+def ring(frames, labels):
     groups = lax.axis_size("pix")
     loop_size = lax.axis_size("tm")
     local_cycles = CYCLES // groups
@@ -62,6 +74,249 @@
     return filled
 
 
+VMEM = pl.BlockSpec(memory_space=pltpu.VMEM)
+HBM = pl.BlockSpec(memory_space=pltpu.HBM)
+ANY = pl.BlockSpec(memory_space=pl.ANY)
+
+
+def local_call(body, outs, count_in, scratch=(), in_specs=None, out_specs=None, after=(), cost=1, **options):
+    def ordered(*refs):
+        body(*refs[: len(refs) - skipped], *refs[len(refs) - tail :])
+
+    tail = len(outs) + len(scratch)
+    skipped = tail + len(after)
+    call = pl.pallas_call(
+        ordered,
+        out_shape=outs,
+        in_specs=(in_specs or [VMEM] * count_in) + [ANY] * len(after),
+        out_specs=out_specs or [VMEM] * len(outs),
+        scratch_shapes=list(scratch),
+        compiler_params=pltpu.CompilerParams(vmem_limit_bytes=VMEM_LIMIT),
+        cost_estimate=pl.CostEstimate(flops=1, bytes_accessed=cost, transcendentals=0),
+        **options,
+    )
+    return lambda *operands: call(*operands, *after)
+
+
+def lanes_at(start, width):
+    return pl.ds(pl.multiple_of(start, LANES), width)
+
+
+def pack_kernel(loop, groups, per, first, frames, live, *outs):
+    t, p = lax.axis_index("tm"), lax.axis_index("pix")
+    to_time, to_owner = outs[: loop - 1], outs[loop - 1 :]
+
+    def tile(index):
+        return frames[:, lanes_at(index * LANES, LANES)] * live[pl.ds(index, 1), :].astype(jnp.bfloat16)
+
+    for j in range(1, loop):
+        for g in range(groups):
+            for s in range(first):
+                at = (g * first + s) * LANES
+                to_time[j - 1][:, at : at + LANES] = tile((g * loop + (t ^ j)) * per + s)
+    for k in range(groups):
+        for c in range(loop * per):
+            to_owner[k][:, c * LANES : (c + 1) * LANES] = tile((p ^ k) * loop * per + c)
+
+
+def pick_kernel(axis, partners, step, base, width, count, *refs):
+    sources, outs = refs[:count][::-1], refs[count:]
+    me = lax.axis_index(axis)
+    for j, out in zip(partners, outs):
+        for k, source in enumerate(sources):
+            out[k] = source[:, lanes_at((me ^ j) * step + base, width)]
+
+
+def padded(value):
+    wide = value.astype(jnp.float32)
+    live = jnp.where(wide[0:1, :] != 0, 1.0, 0.0)
+    return jnp.concatenate([wide, jnp.broadcast_to(live, (8, LANES))], axis=0)
+
+
+def halves(block):
+    lane = lax.broadcasted_iota(jnp.int32, block.shape, 1) % LANES
+    zero = jnp.zeros_like(block)
+    return jnp.concatenate(
+        [jnp.where(lane < CYCLE_CAP, block, zero), jnp.where(lane < CYCLE_CAP, zero, block)], axis=0
+    )
+
+
+def normalized(product, rows):
+    result = []
+    for half in range(2):
+        cycle = product[half * (rows + 8) : (half + 1) * (rows + 8)]
+        count = cycle[rows : rows + 1, rows : rows + 1]
+        row_scale = count / cycle[:rows, rows : rows + 1]
+        column_scale = 1.0 / cycle[rows : rows + 1, :]
+        result.append(cycle[:rows] * row_scale * column_scale)
+    return result
+
+
+def dot_rows(left, right):
+    return lax.dot_general(
+        left, right, (((1,), (1,)), ((), ())), preferred_element_type=jnp.float32
+    )
+
+
+def cross_kernel(loop, groups, per, base, pairs, rows, by_group, *refs):
+    sources, outs, blocks = refs[: groups + len(refs) - 1 - loop - groups], refs[-1 - loop : -1], refs[-1]
+    own, others = sources[:groups], sources[groups:][::-1]
+    t = lax.axis_index("tm")
+    for s in range(pairs):
+        at = slice(s * LANES, (s + 1) * LANES)
+        for j in range(loop):
+            for k in range(groups):
+                if j == 0:
+                    value = own[k][:, lanes_at((t * per + base + s) * LANES, LANES)]
+                elif by_group:
+                    value = others[k][j - 1, :, at]
+                else:
+                    value = others[j - 1][k, :, at]
+                blocks[s, t ^ j, :, k * LANES : (k + 1) * LANES] = padded(value).astype(jnp.bfloat16)
+        for i in range(loop):
+            r = t ^ i
+            left = halves(blocks[s, r].astype(jnp.float32)).astype(jnp.bfloat16)
+            right = jnp.concatenate(
+                [blocks[s, (r + 1) % loop], blocks[s, (r + 2) % loop]], axis=0
+            )
+            for half, cycle in enumerate(normalized(dot_rows(left, right), rows)):
+                outs[i][2 * s + half] = cycle - 1.0
+
+
+def own_kernel(pairs, rows, *refs):
+    sources, out = refs[:-1], refs[-1]
+    for c in range(pairs):
+        at = slice(c * LANES, (c + 1) * LANES)
+        block = jnp.concatenate([padded(source[:, at]) for source in sources], axis=1)
+        left = halves(block).astype(jnp.bfloat16)
+        block = block.astype(jnp.bfloat16)
+        right = jnp.concatenate([block, block], axis=0)
+        for half, cycle in enumerate(normalized(dot_rows(left, right), rows)):
+            out[2 * c + half] = cycle
+
+
+def place_kernel(loop, rows, pairs, cycles, base, own, *refs):
+    parts, (out, slots, sems) = refs[:loop][::-1], refs[-3:]
+    t = lax.axis_index("tm")
+    lane = lax.broadcasted_iota(jnp.int32, (rows, LANES), 1)
+    copies = []
+    for i in range(loop):
+        at = (t ^ i) * cycles + base
+        for c in range(2 * pairs):
+            value = parts[i][c] + 1.0
+            one = pltpu.roll(value, rows, 1)
+            two = pltpu.roll(value, 2 * rows - CYCLE_CAP, 1)
+            slots[i, c, :, :LANES] = jnp.where(
+                lane < rows, own[at + c], jnp.where(lane < 2 * rows, one, two)
+            )
+            slots[i, c, :, LANES:] = two[:, : 3 * rows - LANES]
+        copies.append(
+            pltpu.make_async_copy(slots.at[i], out.at[pl.ds(at, 2 * pairs)], sems.at[i])
+        )
+        copies[-1].start()
+    for copy in copies:
+        copy.wait()
+
+
+def spread(frames, labels, first):
+    loop, groups = lax.axis_size("tm"), lax.axis_size("pix")
+    rows = frames.shape[0]
+    per = frames.shape[1] // (LANES * groups * loop)
+    rest = per - first
+    cycles = 2 * per
+    bf16, f32 = jnp.bfloat16, jnp.float32
+
+    def shape(*dims, dtype=bf16):
+        return jax.ShapeDtypeStruct(dims, dtype)
+
+    packed = local_call(
+        functools.partial(pack_kernel, loop, groups, per, first),
+        [shape(rows, groups * first * LANES)] * (loop - 1) + [shape(rows, loop * per * LANES)] * groups,
+        2,
+    )(frames, jnp.where(labels >= 0, 1.0, 0.0).astype(f32).reshape(-1, LANES))
+
+    def exchange(parts, axis):
+        return [swap(part, axis, j) for j, part in enumerate(parts, 1)]
+
+    def over_pix(parts):
+        over = swap(parts[2], "pix", 2)
+        next_core = swap(parts[3], "pix", 1)
+        core = swap(parts[1], "pix", 1)
+        return [parts[0], core, over, swap(next_core, "pix", 2)]
+
+    def pick(parts, axis, partners, step, base, width):
+        return local_call(
+            functools.partial(pick_kernel, axis, partners, step, base, width, len(parts)),
+            [shape(len(parts), rows, width)] * len(partners),
+            len(parts),
+        )(*parts[::-1])
+
+    def cross(own, others, base, pairs, by_group, after=()):
+        return local_call(
+            functools.partial(cross_kernel, loop, groups, per, base, pairs, rows, by_group),
+            [shape(2 * pairs, rows, LANES, dtype=f32)] * loop,
+            groups + len(others),
+            [pltpu.VMEM((pairs, loop, rows + 8, groups * LANES), bf16)],
+            after=after,
+        )(*own, *others[::-1])
+
+    def block(body, *operands):
+        here = lax.axis_index("tm") < loop
+        outs = jax.eval_shape(body, *operands)
+        return lax.cond(
+            here, body, lambda *_: jax.tree.map(lambda o: jnp.zeros(o.shape, o.dtype), outs), *operands
+        )
+
+    def first_to_owner(own, arrived, after):
+        del after
+        picked = pick(arrived, "pix", range(groups), first * LANES, 0, first * LANES)
+        return cross(own, over_pix(picked), 0, first, True)
+
+    def send_back(tiles):
+        sent = lax.optimization_barrier([tile.astype(jnp.float16) for tile in tiles[1:]])
+        moved = lax.optimization_barrier(exchange(sent, "tm"))
+        return [tiles[0]] + [tile.astype(f32) for tile in moved]
+
+    def place(base, pairs, tiles, filled, cost):
+        return local_call(
+            functools.partial(place_kernel, loop, rows, pairs, cycles, base),
+            [shape(loop * cycles, rows, 3 * rows, dtype=f32)],
+            1 + len(tiles) + len(filled),
+            [pltpu.VMEM((loop, 2 * pairs, rows, 3 * rows), f32), pltpu.SemaphoreType.DMA((loop,))],
+            in_specs=[VMEM] * (1 + len(tiles)) + [HBM] * len(filled),
+            out_specs=[HBM],
+            input_output_aliases={1 + len(tiles): 0} if filled else {},
+            cost=cost,
+        )(own_tiles, *tiles[::-1], *filled)[0]
+
+    time_first = exchange(packed[: loop - 1], "tm")
+    mine, *to_owner = packed[loop - 1 :]
+    owned = [mine] + exchange(to_owner, "pix")
+    picked_rest = pick(owned, "tm", range(1, loop), per * LANES, first * LANES, rest * LANES)
+    time_rest = exchange(picked_rest, "tm")
+    tiles_first = block(first_to_owner, owned, time_first, picked_rest[:1])
+    tiles_rest = cross(owned, time_rest, first, rest, False, tiles_first[:1])
+    own_tiles = local_call(
+        functools.partial(own_kernel, loop * per, rows),
+        [shape(loop * cycles, rows, LANES, dtype=f32)],
+        groups,
+        cost=OWN_COST,
+    )(*owned)[0]
+    back_first = send_back(tiles_first)
+    back_rest = send_back(tiles_rest)
+    filled = place(0, first, back_first, (), PLACE_COST)
+    return place(2 * first, rest, back_rest, (filled,), PLACE_COST)
+
+
+def on_device(frames, labels):
+    loop, groups = lax.axis_size("tm"), lax.axis_size("pix")
+    pairs = CYCLES // groups // 2
+    fits = frames.shape[1] == CYCLES * CYCLE_CAP and frames.shape[0] == CYCLE_CAP - 8
+    if loop == 4 and groups == 4 and fits and pairs % loop == 0 and pairs // loop >= 2:
+        return spread(frames, labels, pairs // loop // 2)
+    return ring(frames, labels)
+
+
 def solution(mesh):
     placed = (P(("runs", "tm"), "pix"), P("pix"))
     return jax.shard_map(

time: 115 us -> 45.1 us (0.39)
  waiting for transfers between devices: 52.1 us -> 14.3 us
  local copies, waits for them, and re-layouts: 30.4 us -> 1.18 us
  matrix products: 11 us -> 0 us
  starting transfers between devices: 16.2 us -> 23.7 us
  Pallas kernels: 0 us -> 4.63 us
  other arithmetic: 4.37 us -> 0.89 us
    ppermute x2 -> x19, waiting for transfers between devices: 37.8 us -> 14.3 us  [swap(): return lax.ppermute(shard, axis, [(i, i ^ by) for i in range(size)])]
    dynamic_update_slice x3 -> x0, local copies, waits for them, and re-layouts: 19.5 us -> none  [the longest x2 18.1 us: advance(): lax.dynamic_update_slice(result, make_tiles(moving[None]), (0, 0, offset...]
    ppermute x2 -> x19, starting transfers between devices: 8.44 us -> 23.7 us  [swap(): return lax.ppermute(shard, axis, [(i, i ^ by) for i in range(size)])]
    all_to_all x2 -> x0, waiting for transfers between devices: 14.3 us -> none  [the longest x1 12.8 us: on_device(): lax.all_to_all(masked, 'pix', split_axis=1, concat_axis=1, tiled=True)]
    dot_general x3 -> x0, matrix products: 11 us -> none  [make_tiles(): jnp.einsum('tgqc,nsgqc->qtns', own_split, block_split, preferred_element_...]
    all_to_all x2 -> x0, starting transfers between devices: 7.71 us -> none  [the longest x1 4.21 us: on_device(): lax.all_to_all(live_row, 'pix', split_axis=1, concat_axis=1, tiled=True)]
    pallas_call x0 -> x8, Pallas kernels: none -> 4.63 us  [local_call(): return lambda *operands: call(*operands, *after)]
    another operation x2 -> x0, local copies, waits for them, and re-layouts: 3.88 us -> none
  transfers between devices with their start and end apart: 4 -> 19, of which waited for: 4 -> 7; matrix products, arithmetic and copies ran while one was open for 2% -> 0% of each run, Pallas kernels for 0% -> 7%
where the time goes in v2:
time: 45.1 us; the launch traced here: 44.9 us
  starting transfers between devices  23.7 us (53%)
  waiting for transfers between devices  14.3 us (32%)
  Pallas kernels  4.63 us (10%)
  local copies, waits for them, and re-layouts  1.18 us (3%)
  other arithmetic  0.89 us (2%)
    ppermute x19, starting transfers between devices, swap(): return lax.ppermute(shard, axis, [(i, i ^ by) for i in range(size)])  23.7 us
    ppermute x19, waiting for transfers between devices, swap(): return lax.ppermute(shard, axis, [(i, i ^ by) for i in range(size)])  14.3 us
    pallas_call x8, Pallas kernels, local_call(): return lambda *operands: call(*operands, *after)  4.63 us
    unnamed x2, local copies, waits for them, and re-layouts  1.18 us
  transfers between devices with their start and end apart: 19, of which 7 were waited for; matrix products, arithmetic and copies ran while one was open for 0% of the time, Pallas kernels for 7%

profile of v2, /device:TPU:0, one launch (start us, length us, event | category | flops | bytes accessed | tf_op | source)
XLA Modules:
  0.0 44.9 jit_solution(3244985042535860824)
XLA Ops:
  0.0 0.8 %select_bitcast_fusion.refs_1_ = f32[64,128]{1,0:T(8,128)S(1)} fusion(s32[8192]{0:T(1024)} %param.5), kind=kLoop, calls=%fused_computation | loop fusion | flops 16384 | bytes 65536 | tf_op jit(solution)/shard_map/reshape | solution.py:236
  0.8 1.2 %copy-done = bf16[56,8192]{1,0:T(8,128)(2,1)S(1)} copy-done((bf16[56,8192]{1,0:T(8,128)(2,1)S(1)}, bf16[56,8192]{1,0:T(8,128)(2,1)}, u32[]{:S(2)}) %copy-start) | copy-done | bytes 917528
  1.9 0.3 shard_map.28
  2.3 0.5 %collective-permute-start.4 = (bf16[56,2048]{1,0:T(8,128)(2,1)S(1)}, bf16[56,2048]{1,0:T(8,128)(2,1)S(1)}, u32[]{:S(2)}, u32[]{:S(2)}) collective-permute-start(bf16[56,2048]{1,0:T(8,128)(2,1)S(1)} %get-tuple-element.72), channel_id=1, source_target_pairs={{0,1},{1,0},{2,3},{3,2},{4,5},{5,4},{6,7},{7,6},{8,9},{9,8},{10,11... | collective-permute-start | bytes 688136 | tf_op jit(solution)/shard_map/ppermute | solution.py:24
  2.8 2.6 %collective-permute-start.5 = (bf16[56,2048]{1,0:T(8,128)(2,1)S(1)}, bf16[56,2048]{1,0:T(8,128)(2,1)S(1)}, u32[]{:S(2)}, u32[]{:S(2)}) collective-permute-start(bf16[56,2048]{1,0:T(8,128)(2,1)S(1)} %get-tuple-element.73), channel_id=1, source_target_pairs={{0,2},{1,3},{2,0},{3,1},{4,6},{5,7},{6,4},{7,5},{8,10},{9,11},{10,... | collective-permute-start | bytes 688136 | tf_op jit(solution)/shard_map/ppermute | solution.py:24
  5.4 0.1 collective-permute-start.6
  5.4 3.8 %collective-permute-start.10 = (bf16[56,1024]{1,0:T(8,128)(2,1)S(1)}, bf16[56,1024]{1,0:T(8,128)(2,1)S(1)}, u32[]{:S(2)}, u32[]{:S(2)}) collective-permute-start(bf16[56,1024]{1,0:T(8,128)(2,1)S(1)} %get-tuple-element.78), channel_id=1, source_target_pairs={{0,12},{4,8},{8,4},{12,0},{1,13},{5,9},{9,5},{13,1},{2,14},{6,10},... | collective-permute-start | bytes 344072 | tf_op jit(solution)/shard_map/ppermute | solution.py:24
  9.3 0.6 %collective-permute-start.12 = (bf16[56,1024]{1,0:T(8,128)(2,1)S(1)}, bf16[56,1024]{1,0:T(8,128)(2,1)S(1)}, u32[]{:S(2)}, u32[]{:S(2)}) collective-permute-start(bf16[56,1024]{1,0:T(8,128)(2,1)S(1)} %get-tuple-element.80), channel_id=1, source_target_pairs={{0,4},{4,0},{8,12},{12,8},{1,5},{5,1},{9,13},{13,9},{2,6},{6,2},{1... | collective-permute-start | bytes 344072 | tf_op jit(solution)/shard_map/ppermute | solution.py:24
  9.8 2.0 %collective-permute-done.5.refs_2_.refs_1_ = bf16[56,2048]{1,0:T(8,128)(2,1)S(1)} collective-permute-done((bf16[56,2048]{1,0:T(8,128)(2,1)S(1)}, bf16[56,2048]{1,0:T(8,128)(2,1)S(1)}, u32[]{:S(2)}, u32[]{:S(2)}) %collective-permute-start.5) | collective-permute-done | bytes 229408 | tf_op jit(solution)/shard_map/ppermute | solution.py:24
  11.8 4.4 %collective-permute-done.6.refs_3_.refs_0_ = bf16[56,2048]{1,0:T(8,128)(2,1)S(1)} collective-permute-done((bf16[56,2048]{1,0:T(8,128)(2,1)S(1)}, bf16[56,2048]{1,0:T(8,128)(2,1)S(1)}, u32[]{:S(2)}, u32[]{:S(2)}) %collective-permute-start.6) | collective-permute-done | bytes 229408 | tf_op jit(solution)/shard_map/ppermute | solution.py:24
  16.3 3.7 %collective-permute-start.7 = (bf16[4,56,256]{2,1,0:T(8,128)(2,1)S(1)}, bf16[4,56,256]{2,1,0:T(8,128)(2,1)S(1)}, u32[]{:S(2)}, u32[]{:S(2)}) collective-permute-start(bf16[4,56,256]{2,1,0:T(8,128)(2,1)S(1)} %get-tuple-element.75), channel_id=1, source_target_pairs={{0,12},{4,8},{8,4},{12,0},{1,13},{5,9},{9,5},{13,1},{2,14},{6,10},... | collective-permute-start | bytes 344072 | tf_op jit(solution)/shard_map/ppermute | solution.py:24
  20.0 7.6 %conditional.1 = (f32[4,56,128]{2,1,0:T(8,128)S(1)}, f16[4,56,128]{2,1,0:T(8,128)(2,1)S(1)}, f16[4,56,128]{2,1,0:T(8,128)(2,1)S(1)}, f16[4,56,128]{2,1,0:T(8,128)(2,1)S(1)}) conditional(s32[]{:T(128)} %convert_element_type.46, () %tuple.23, (bf16[56,1024]{1,0:T(8,128)(2,1)S(1)}, bf16[56,1024]{1,0:T(8,128)(2,1)S(1)}, bf16[56,1024]{1,0:T(8,128)(2,1)S(1)}, ...), branch_computations={%region_0.1_spmd, %region_1.2_spmd} | conditional | flops 86018 | bytes 1892546 | solution.py:266
  20.1 0.4 collective-permute-start
  20.5 1.5 %collective-permute-start.2 = (bf16[3,56,256]{2,1,0:T(8,128)(2,1)S(1)}, bf16[3,56,256]{2,1,0:T(8,128)(2,1)S(1)}, u32[]{:S(2)}, u32[]{:S(2)}) collective-permute-start(bf16[3,56,256]{2,1,0:T(8,128)(2,1)S(1)} %get-tuple-element.34), channel_id=1, source_target_pairs={{0,2},{1,3},{2,0},{3,1},{4,6},{5,7},{6,4},{7,5},{8,10},{9,11},{10,... | collective-permute-start | bytes 258056 | tf_op jit(solution)/shard_map/cond/branch_1_fun/ppermute | solution.py:24
  22.0 1.0 %collective-permute-start.1 = (bf16[3,56,256]{2,1,0:T(8,128)(2,1)S(1)}, bf16[3,56,256]{2,1,0:T(8,128)(2,1)S(1)}, u32[]{:S(2)}, u32[]{:S(2)}) collective-permute-start(bf16[3,56,256]{2,1,0:T(8,128)(2,1)S(1)} %collective-permute-done), channel_id=1, source_target_pairs={{0,2},{1,3},{2,0},{3,1},{4,6},{5,7},{6,4},{7,5},{8,10},{9,11},{10,... | collective-permute-start | bytes 258056 | tf_op jit(solution)/shard_map/cond/branch_1_fun/ppermute | solution.py:24
  22.9 2.2 %collective-permute-done.2.refs_5_ = bf16[3,56,256]{2,1,0:T(8,128)(2,1)S(1)} collective-permute-done((bf16[3,56,256]{2,1,0:T(8,128)(2,1)S(1)}, bf16[3,56,256]{2,1,0:T(8,128)(2,1)S(1)}, u32[]{:S(2)}, u32[]{:S(2)}) %collective-permute-start.2) | collective-permute-done | bytes 86048 | tf_op jit(solution)/shard_map/cond/branch_1_fun/ppermute | solution.py:24
  25.2 1.8 %collective-permute-done.1.refs_4_ = bf16[3,56,256]{2,1,0:T(8,128)(2,1)S(1)} collective-permute-done((bf16[3,56,256]{2,1,0:T(8,128)(2,1)S(1)}, bf16[3,56,256]{2,1,0:T(8,128)(2,1)S(1)}, u32[]{:S(2)}, u32[]{:S(2)}) %collective-permute-start.1) | collective-permute-done | bytes 86048 | tf_op jit(solution)/shard_map/cond/branch_1_fun/ppermute | solution.py:24
  27.0 0.6 %branch_1_fun.3 = (f32[4,56,128]{2,1,0:T(8,128)S(1)}, f32[4,56,128]{2,1,0:T(8,128)S(1)}, f32[4,56,128]{2,1,0:T(8,128)S(1)}, f32[4,56,128]{2,1,0:T(8,128)S(1)}) custom-call(bf16[56,2048]{1,0:T(8,128)(2,1)S(1)} %get-tuple-element.26.refs_0_, bf16[56,2048]{1,0:T(8,128)(2,1)S(1)} %get-tuple-element.27.refs_1_, bf16[56,2048]{1,0:T(8,128)(2,1)S(1)} %get-tuple-element.28.refs_2_, ...), custom_call_target="tpu_custom_call" | custom-call | flops 1 | bytes 1 | tf_op jit(solution)/shard_map/cond/branch_1_fun/pallas_call | solution.py:98
  27.6 0.8 %collective-permute-start.9 = (bf16[4,56,256]{2,1,0:T(8,128)(2,1)S(1)}, bf16[4,56,256]{2,1,0:T(8,128)(2,1)S(1)}, u32[]{:S(2)}, u32[]{:S(2)}) collective-permute-start(bf16[4,56,256]{2,1,0:T(8,128)(2,1)S(1)} %get-tuple-element.77), channel_id=1, source_target_pairs={{0,4},{4,0},{8,12},{12,8},{1,5},{5,1},{9,13},{13,9},{2,6},{6,2},{1... | collective-permute-start | bytes 344072 | tf_op jit(solution)/shard_map/ppermute | solution.py:24
  28.4 1.3 %collective-permute-start.16 = (f16[4,56,128]{2,1,0:T(8,128)(2,1)S(1)}, f16[4,56,128]{2,1,0:T(8,128)(2,1)S(1)}, u32[]{:S(2)}, u32[]{:S(2)}) collective-permute-start(f16[4,56,128]{2,1,0:T(8,128)(2,1)S(1)} %get-tuple-element.95), channel_id=1, source_target_pairs={{0,4},{4,0},{8,12},{12,8},{1,5},{5,1},{9,13},{13,9},{2,6},{6,2},{1... | collective-permute-start | bytes 172040 | tf_op jit(solution)/shard_map/ppermute | solution.py:24
  29.7 2.9 %collective-permute-start.17 = (f16[4,56,128]{2,1,0:T(8,128)(2,1)S(1)}, f16[4,56,128]{2,1,0:T(8,128)(2,1)S(1)}, u32[]{:S(2)}, u32[]{:S(2)}) collective-permute-start(f16[4,56,128]{2,1,0:T(8,128)(2,1)S(1)} %get-tuple-element.96), channel_id=1, source_target_pairs={{0,8},{4,12},{8,0},{12,4},{1,9},{5,13},{9,1},{13,5},{2,10},{6,14},... | collective-permute-start | bytes 172040 | tf_op jit(solution)/shard_map/ppermute | solution.py:24
  32.7 0.1 collective-permute-start.18
  32.8 1.3 %collective-permute-done.9.refs_6_ = bf16[4,56,256]{2,1,0:T(8,128)(2,1)S(1)} collective-permute-done((bf16[4,56,256]{2,1,0:T(8,128)(2,1)S(1)}, bf16[4,56,256]{2,1,0:T(8,128)(2,1)S(1)}, u32[]{:S(2)}, u32[]{:S(2)}) %collective-permute-start.9) | collective-permute-done | bytes 114720 | tf_op jit(solution)/shard_map/ppermute | solution.py:24
  34.1 0.6 %shard_map.31 = (f32[4,56,128]{2,1,0:T(8,128)S(1)}, f32[4,56,128]{2,1,0:T(8,128)S(1)}, f32[4,56,128]{2,1,0:T(8,128)S(1)}, f32[4,56,128]{2,1,0:T(8,128)S(1)}) custom-call(bf16[56,2048]{1,0:T(8,128)(2,1)S(1)} %get-tuple-element.71.refs_0_.refs_3_, bf16[56,2048]{1,0:T(8,128)(2,1)S(1)} %collective-permute-done.4.refs_1_.refs_2_, ...), custom_call_target="tpu_custom_call" | custom-call | flops 1 | bytes 1 | tf_op jit(solution)/shard_map/pallas_call | solution.py:98
  34.8 0.1 collective-permute-start.13
  34.9 2.9 %collective-permute-start.14 = (f16[4,56,128]{2,1,0:T(8,128)(2,1)S(1)}, f16[4,56,128]{2,1,0:T(8,128)(2,1)S(1)}, u32[]{:S(2)}, u32[]{:S(2)}) collective-permute-start(f16[4,56,128]{2,1,0:T(8,128)(2,1)S(1)} %convert_element_type.48), channel_id=1, source_target_pairs={{0,8},{4,12},{8,0},{12,4},{1,9},{5,13},{9,1},{13,5},{2,10},{6,14},... | collective-permute-start | bytes 172040 | tf_op jit(solution)/shard_map/ppermute | solution.py:24
  37.8 1.4 %collective-permute-start.15 = (f16[4,56,128]{2,1,0:T(8,128)(2,1)S(1)}, f16[4,56,128]{2,1,0:T(8,128)(2,1)S(1)}, u32[]{:S(2)}, u32[]{:S(2)}) collective-permute-start(f16[4,56,128]{2,1,0:T(8,128)(2,1)S(1)} %convert_element_type.49), channel_id=1, source_target_pairs={{0,12},{4,8},{8,4},{12,0},{1,13},{5,9},{9,5},{13,1},{2,14},{6,10},... | collective-permute-start | bytes 172040 | tf_op jit(solution)/shard_map/ppermute | solution.py:24
  39.2 0.8 %shard_map.29.refs_0_ = f32[32,56,128]{2,1,0:T(8,128)S(1)} custom-call(bf16[56,2048]{1,0:T(8,128)(2,1)S(1)} %get-tuple-element.71.refs_0_.refs_3_, bf16[56,2048]{1,0:T(8,128)(2,1)S(1)} %collective-permute-done.4.refs_1_.refs_2_, bf16[56,2048]{1,0:T(8,128)(2,1)S(1)} %collective-permute-done.5.refs_2_.refs_1_, ...), custom_call_target="tpu_custom_call" | custom-call | flops 1 | bytes 4194304 | tf_op jit(solution)/shard_map/pallas_call | solution.py:98
  40.1 1.1 %shard_map.32.refs_5_ = f32[32,56,168]{2,1,0:T(8,128)} custom-call(f32[32,56,128]{2,1,0:T(8,128)S(1)} %shard_map.29.refs_0_, f32[4,56,128]{2,1,0:T(8,128)S(1)} %convert_element_type.53.refs_1_, f32[4,56,128]{2,1,0:T(8,128)S(1)} %convert_element_type.54.refs_2_, f32[4,56,128]{2,1,0:T(8,128)S(1)} %convert_element_type.55.refs_3_, ...), custom_call_target="tpu_custom_call" | custom-call | flops 1 | bytes 4194304 | tf_op jit(solution)/shard_map/pallas_call | solution.py:98
  41.2 0.3 collective-permute-done.14
  41.5 2.3 %collective-permute-done.15 = f16[4,56,128]{2,1,0:T(8,128)(2,1)S(1)} collective-permute-done((f16[4,56,128]{2,1,0:T(8,128)(2,1)S(1)}, f16[4,56,128]{2,1,0:T(8,128)(2,1)S(1)}, u32[]{:S(2)}, u32[]{:S(2)}) %collective-permute-start.15) | collective-permute-done | bytes 57376 | tf_op jit(solution)/shard_map/ppermute | solution.py:24
  43.8 1.1 %shard_map.33 = f32[32,56,168]{2,1,0:T(8,128)} custom-call(f32[32,56,128]{2,1,0:T(8,128)S(1)} %shard_map.29.refs_0_, f32[4,56,128]{2,1,0:T(8,128)S(1)} %convert_element_type.50.refs_1_, f32[4,56,128]{2,1,0:T(8,128)S(1)} %convert_element_type.51.refs_2_, f32[4,56,128]{2,1,0:T(8,128)S(1)} %convert_element_type.52.refs_3_, ...), custom_call_target="tpu_custom_call", output_to_operand_aliasing={{}: (5, {})} | custom-call | flops 1 | bytes 4194304 | tf_op jit(solution)/shard_map/pallas_call | solution.py:98
  (30 shorter events, 0.3 us)
Async XLA Ops:
  0.8 1.2 %copy-start = (bf16[56,8192]{1,0:T(8,128)(2,1)S(1)}, bf16[56,8192]{1,0:T(8,128)(2,1)}, u32[]{:S(2)}) copy-start(bf16[56,8192]{1,0:T(8,128)(2,1)} %refs_0_.1) | copy-start | bytes 2752516
  2.3 7.0 %collective-permute-start.4 = (bf16[56,2048]{1,0:T(8,128)(2,1)S(1)}, bf16[56,2048]{1,0:T(8,128)(2,1)S(1)}, u32[]{:S(2)}, u32[]{:S(2)}) collective-permute-start(bf16[56,2048]{1,0:T(8,128)(2,1)S(1)} %get-tuple-element.72), channel_id=1, source_target_pairs={{0,1},{1,0},{2,3},{3,2},{4,5},{5,4},{6,7},{7,6},{8,9},{9,8},{10,11... | collective-permute-start | bytes 688136 | tf_op jit(solution)/shard_map/ppermute | solution.py:24
  2.8 9.0 %collective-permute-start.5 = (bf16[56,2048]{1,0:T(8,128)(2,1)S(1)}, bf16[56,2048]{1,0:T(8,128)(2,1)S(1)}, u32[]{:S(2)}, u32[]{:S(2)}) collective-permute-start(bf16[56,2048]{1,0:T(8,128)(2,1)S(1)} %get-tuple-element.73), channel_id=1, source_target_pairs={{0,2},{1,3},{2,0},{3,1},{4,6},{5,7},{6,4},{7,5},{8,10},{9,11},{10,... | collective-permute-start | bytes 688136 | tf_op jit(solution)/shard_map/ppermute | solution.py:24
  5.4 10.8 %collective-permute-start.6 = (bf16[56,2048]{1,0:T(8,128)(2,1)S(1)}, bf16[56,2048]{1,0:T(8,128)(2,1)S(1)}, u32[]{:S(2)}, u32[]{:S(2)}) collective-permute-start(bf16[56,2048]{1,0:T(8,128)(2,1)S(1)} %get-tuple-element.74), channel_id=1, source_target_pairs={{0,3},{1,2},{2,1},{3,0},{4,7},{5,6},{6,5},{7,4},{8,11},{9,10},{10,... | collective-permute-start | bytes 688136 | tf_op jit(solution)/shard_map/ppermute | solution.py:24
  5.4 14.6 %collective-permute-start.10 = (bf16[56,1024]{1,0:T(8,128)(2,1)S(1)}, bf16[56,1024]{1,0:T(8,128)(2,1)S(1)}, u32[]{:S(2)}, u32[]{:S(2)}) collective-permute-start(bf16[56,1024]{1,0:T(8,128)(2,1)S(1)} %get-tuple-element.78), channel_id=1, source_target_pairs={{0,12},{4,8},{8,4},{12,0},{1,13},{5,9},{9,5},{13,1},{2,14},{6,10},... | collective-permute-start | bytes 344072 | tf_op jit(solution)/shard_map/ppermute | solution.py:24
  9.3 10.7 %collective-permute-start.11 = (bf16[56,1024]{1,0:T(8,128)(2,1)S(1)}, bf16[56,1024]{1,0:T(8,128)(2,1)S(1)}, u32[]{:S(2)}, u32[]{:S(2)}) collective-permute-start(bf16[56,1024]{1,0:T(8,128)(2,1)S(1)} %get-tuple-element.79), channel_id=1, source_target_pairs={{0,8},{4,12},{8,0},{12,4},{1,9},{5,13},{9,1},{13,5},{2,10},{6,14},... | collective-permute-start | bytes 344072 | tf_op jit(solution)/shard_map/ppermute | solution.py:24
  9.3 10.7 %collective-permute-start.12 = (bf16[56,1024]{1,0:T(8,128)(2,1)S(1)}, bf16[56,1024]{1,0:T(8,128)(2,1)S(1)}, u32[]{:S(2)}, u32[]{:S(2)}) collective-permute-start(bf16[56,1024]{1,0:T(8,128)(2,1)S(1)} %get-tuple-element.80), channel_id=1, source_target_pairs={{0,4},{4,0},{8,12},{12,8},{1,5},{5,1},{9,13},{13,9},{2,6},{6,2},{1... | collective-permute-start | bytes 344072 | tf_op jit(solution)/shard_map/ppermute | solution.py:24
  16.3 16.4 %collective-permute-start.7 = (bf16[4,56,256]{2,1,0:T(8,128)(2,1)S(1)}, bf16[4,56,256]{2,1,0:T(8,128)(2,1)S(1)}, u32[]{:S(2)}, u32[]{:S(2)}) collective-permute-start(bf16[4,56,256]{2,1,0:T(8,128)(2,1)S(1)} %get-tuple-element.75), channel_id=1, source_target_pairs={{0,12},{4,8},{8,4},{12,0},{1,13},{5,9},{9,5},{13,1},{2,14},{6,10},... | collective-permute-start | bytes 344072 | tf_op jit(solution)/shard_map/ppermute | solution.py:24
  20.0 12.8 %collective-permute-start.8 = (bf16[4,56,256]{2,1,0:T(8,128)(2,1)S(1)}, bf16[4,56,256]{2,1,0:T(8,128)(2,1)S(1)}, u32[]{:S(2)}, u32[]{:S(2)}) collective-permute-start(bf16[4,56,256]{2,1,0:T(8,128)(2,1)S(1)} %get-tuple-element.76), channel_id=1, source_target_pairs={{0,8},{4,12},{8,0},{12,4},{1,9},{5,13},{9,1},{13,5},{2,10},{6,14},... | collective-permute-start | bytes 344072 | tf_op jit(solution)/shard_map/ppermute | solution.py:24
  20.1 1.9 %collective-permute-start = (bf16[3,56,256]{2,1,0:T(8,128)(2,1)S(1)}, bf16[3,56,256]{2,1,0:T(8,128)(2,1)S(1)}, u32[]{:S(2)}, u32[]{:S(2)}) collective-permute-start(bf16[3,56,256]{2,1,0:T(8,128)(2,1)S(1)} %get-tuple-element.33), channel_id=1, source_target_pairs={{0,1},{1,0},{2,3},{3,2},{4,5},{5,4},{6,7},{7,6},{8,9},{9,8},{10,11... | collective-permute-start | bytes 258056 | tf_op jit(solution)/shard_map/cond/branch_1_fun/ppermute | solution.py:24
  20.5 4.7 %collective-permute-start.2 = (bf16[3,56,256]{2,1,0:T(8,128)(2,1)S(1)}, bf16[3,56,256]{2,1,0:T(8,128)(2,1)S(1)}, u32[]{:S(2)}, u32[]{:S(2)}) collective-permute-start(bf16[3,56,256]{2,1,0:T(8,128)(2,1)S(1)} %get-tuple-element.34), channel_id=1, source_target_pairs={{0,2},{1,3},{2,0},{3,1},{4,6},{5,7},{6,4},{7,5},{8,10},{9,11},{10,... | collective-permute-start | bytes 258056 | tf_op jit(solution)/shard_map/cond/branch_1_fun/ppermute | solution.py:24
  22.0 3.2 %collective-permute-start.3 = (bf16[3,56,256]{2,1,0:T(8,128)(2,1)S(1)}, bf16[3,56,256]{2,1,0:T(8,128)(2,1)S(1)}, u32[]{:S(2)}, u32[]{:S(2)}) collective-permute-start(bf16[3,56,256]{2,1,0:T(8,128)(2,1)S(1)} %get-tuple-element.35), channel_id=1, source_target_pairs={{0,1},{1,0},{2,3},{3,2},{4,5},{5,4},{6,7},{7,6},{8,9},{9,8},{10,11... | collective-permute-start | bytes 258056 | tf_op jit(solution)/shard_map/cond/branch_1_fun/ppermute | solution.py:24
  22.0 5.0 %collective-permute-start.1 = (bf16[3,56,256]{2,1,0:T(8,128)(2,1)S(1)}, bf16[3,56,256]{2,1,0:T(8,128)(2,1)S(1)}, u32[]{:S(2)}, u32[]{:S(2)}) collective-permute-start(bf16[3,56,256]{2,1,0:T(8,128)(2,1)S(1)} %collective-permute-done), channel_id=1, source_target_pairs={{0,2},{1,3},{2,0},{3,1},{4,6},{5,7},{6,4},{7,5},{8,10},{9,11},{10,... | collective-permute-start | bytes 258056 | tf_op jit(solution)/shard_map/cond/branch_1_fun/ppermute | solution.py:24
  27.6 6.5 %collective-permute-start.9 = (bf16[4,56,256]{2,1,0:T(8,128)(2,1)S(1)}, bf16[4,56,256]{2,1,0:T(8,128)(2,1)S(1)}, u32[]{:S(2)}, u32[]{:S(2)}) collective-permute-start(bf16[4,56,256]{2,1,0:T(8,128)(2,1)S(1)} %get-tuple-element.77), channel_id=1, source_target_pairs={{0,4},{4,0},{8,12},{12,8},{1,5},{5,1},{9,13},{13,9},{2,6},{6,2},{1... | collective-permute-start | bytes 344072 | tf_op jit(solution)/shard_map/ppermute | solution.py:24
  28.4 9.4 %collective-permute-start.16 = (f16[4,56,128]{2,1,0:T(8,128)(2,1)S(1)}, f16[4,56,128]{2,1,0:T(8,128)(2,1)S(1)}, u32[]{:S(2)}, u32[]{:S(2)}) collective-permute-start(f16[4,56,128]{2,1,0:T(8,128)(2,1)S(1)} %get-tuple-element.95), channel_id=1, source_target_pairs={{0,4},{4,0},{8,12},{12,8},{1,5},{5,1},{9,13},{13,9},{2,6},{6,2},{1... | collective-permute-start | bytes 172040 | tf_op jit(solution)/shard_map/ppermute | solution.py:24
  29.7 10.3 %collective-permute-start.17 = (f16[4,56,128]{2,1,0:T(8,128)(2,1)S(1)}, f16[4,56,128]{2,1,0:T(8,128)(2,1)S(1)}, u32[]{:S(2)}, u32[]{:S(2)}) collective-permute-start(f16[4,56,128]{2,1,0:T(8,128)(2,1)S(1)} %get-tuple-element.96), channel_id=1, source_target_pairs={{0,8},{4,12},{8,0},{12,4},{1,9},{5,13},{9,1},{13,5},{2,10},{6,14},... | collective-permute-start | bytes 172040 | tf_op jit(solution)/shard_map/ppermute | solution.py:24
  32.7 7.4 %collective-permute-start.18 = (f16[4,56,128]{2,1,0:T(8,128)(2,1)S(1)}, f16[4,56,128]{2,1,0:T(8,128)(2,1)S(1)}, u32[]{:S(2)}, u32[]{:S(2)}) collective-permute-start(f16[4,56,128]{2,1,0:T(8,128)(2,1)S(1)} %get-tuple-element.97), channel_id=1, source_target_pairs={{0,12},{4,8},{8,4},{12,0},{1,13},{5,9},{9,5},{13,1},{2,14},{6,10},... | collective-permute-start | bytes 172040 | tf_op jit(solution)/shard_map/ppermute | solution.py:24
  34.8 6.4 %collective-permute-start.13 = (f16[4,56,128]{2,1,0:T(8,128)(2,1)S(1)}, f16[4,56,128]{2,1,0:T(8,128)(2,1)S(1)}, u32[]{:S(2)}, u32[]{:S(2)}) collective-permute-start(f16[4,56,128]{2,1,0:T(8,128)(2,1)S(1)} %convert_element_type.47), channel_id=1, source_target_pairs={{0,4},{4,0},{8,12},{12,8},{1,5},{5,1},{9,13},{13,9},{2,6},{6,2},{1... | collective-permute-start | bytes 172040 | tf_op jit(solution)/shard_map/ppermute | solution.py:24
  34.9 6.6 %collective-permute-start.14 = (f16[4,56,128]{2,1,0:T(8,128)(2,1)S(1)}, f16[4,56,128]{2,1,0:T(8,128)(2,1)S(1)}, u32[]{:S(2)}, u32[]{:S(2)}) collective-permute-start(f16[4,56,128]{2,1,0:T(8,128)(2,1)S(1)} %convert_element_type.48), channel_id=1, source_target_pairs={{0,8},{4,12},{8,0},{12,4},{1,9},{5,13},{9,1},{13,5},{2,10},{6,14},... | collective-permute-start | bytes 172040 | tf_op jit(solution)/shard_map/ppermute | solution.py:24
  37.8 6.0 %collective-permute-start.15 = (f16[4,56,128]{2,1,0:T(8,128)(2,1)S(1)}, f16[4,56,128]{2,1,0:T(8,128)(2,1)S(1)}, u32[]{:S(2)}, u32[]{:S(2)}) collective-permute-start(f16[4,56,128]{2,1,0:T(8,128)(2,1)S(1)} %convert_element_type.49), channel_id=1, source_target_pairs={{0,12},{4,8},{8,4},{12,0},{1,13},{5,9},{9,5},{13,1},{2,14},{6,10},... | collective-permute-start | bytes 172040 | tf_op jit(solution)/shard_map/ppermute | solution.py:24

commit v3 on v0

--- a/solution.py
+++ b/solution.py
@@ -1,10 +1,18 @@
+import functools
+
 import jax
 import jax.numpy as jnp
 from jax import lax
+from jax.experimental import pallas as pl
+from jax.experimental.pallas import tpu as pltpu
 from jax.sharding import PartitionSpec as P
 
 CYCLES = 128
 CYCLE_CAP = 64
+LANES = 128
+PIECE = 16
+VMEM_LIMIT = 48 * 2**20
+OWN_COST, PLACE_COST = 4 << 20, 4 << 20
 
 
 def from_behind(shard, axis, by):
@@ -12,7 +20,12 @@
     return lax.ppermute(shard, axis, [(i, (i + by) % size) for i in range(size)])
 
 
-def on_device(frames, labels):
+def swap(shard, axis, by):
+    size = lax.axis_size(axis)
+    return lax.ppermute(shard, axis, [(i, i ^ by) for i in range(size)])
+
+
+def ring(frames, labels):
     groups = lax.axis_size("pix")
     loop_size = lax.axis_size("tm")
     local_cycles = CYCLES // groups
@@ -62,6 +75,262 @@
     return filled
 
 
+VMEM = pl.BlockSpec(memory_space=pltpu.VMEM)
+HBM = pl.BlockSpec(memory_space=pltpu.HBM)
+ANY = pl.BlockSpec(memory_space=pl.ANY)
+
+
+def local_call(body, outs, count_in, scratch=(), in_specs=None, out_specs=None, after=(), cost=1, **options):
+    def ordered(*refs):
+        body(*refs[: len(refs) - skipped], *refs[len(refs) - tail :])
+
+    tail = len(outs) + len(scratch)
+    skipped = tail + len(after)
+    call = pl.pallas_call(
+        ordered,
+        out_shape=outs,
+        in_specs=(in_specs or [VMEM] * count_in) + [ANY] * len(after),
+        out_specs=out_specs or [VMEM] * len(outs),
+        scratch_shapes=list(scratch),
+        compiler_params=pltpu.CompilerParams(vmem_limit_bytes=VMEM_LIMIT),
+        cost_estimate=pl.CostEstimate(flops=1, bytes_accessed=cost, transcendentals=0),
+        **options,
+    )
+    return lambda *operands: call(*operands, *after)
+
+
+def lanes_at(start, width):
+    return pl.ds(pl.multiple_of(start, LANES), width)
+
+
+def pack_kernel(loop, groups, per, frames, live, mine, over, core):
+    p = lax.axis_index("pix")
+    for k, out in ((1, core.at[0]), (3, core.at[1]), (0, mine), (2, over)):
+        for n in range(loop * per):
+            index = (p ^ k) * loop * per + n
+            mask = live[pl.ds(index, 1), :].astype(jnp.bfloat16)
+            out[:, n * LANES : (n + 1) * LANES] = frames[:, lanes_at(index * LANES, LANES)] * mask
+
+
+def near_kernel(loop, per, parts, mine, over, core, *outs):
+    t = lax.axis_index("tm")
+    to_chip, to_time = outs[: len(parts)], outs[len(parts) :]
+    for j, out in enumerate(to_time, 1):
+        lanes = lanes_at((t ^ j) * per * LANES, per * LANES)
+        out[0] = mine[:, lanes]
+        out[1] = core[0, :, lanes]
+    for (start, count), out in zip(parts, to_chip):
+        for c in range(loop):
+            source = slice((c * per + start) * LANES, (c * per + start + count) * LANES)
+            target = slice(c * count * LANES, (c + 1) * count * LANES)
+            out[0, :, target] = over[:, source]
+            out[1, :, target] = core[1, :, source]
+
+
+def far_kernel(count, chip, *outs):
+    t = lax.axis_index("tm")
+    for j, out in enumerate(outs, 1):
+        out[...] = chip[:, :, lanes_at((t ^ j) * count * LANES, count * LANES)]
+
+
+def padded(value):
+    wide = value.astype(jnp.float32)
+    live = jnp.where(wide[0:1, :] != 0, 1.0, 0.0)
+    return jnp.concatenate([wide, jnp.broadcast_to(live, (8, LANES))], axis=0)
+
+
+def halves(block):
+    lane = lax.broadcasted_iota(jnp.int32, block.shape, 1) % LANES
+    zero = jnp.zeros_like(block)
+    return jnp.concatenate(
+        [jnp.where(lane < CYCLE_CAP, block, zero), jnp.where(lane < CYCLE_CAP, zero, block)], axis=0
+    )
+
+
+def normalized(product, rows):
+    result = []
+    for half in range(2):
+        cycle = product[half * (rows + 8) : (half + 1) * (rows + 8)]
+        count = cycle[rows : rows + 1, rows : rows + 1]
+        row_scale = count / cycle[:rows, rows : rows + 1]
+        column_scale = 1.0 / cycle[rows : rows + 1, :]
+        result.append(cycle[:rows] * row_scale * column_scale)
+    return result
+
+
+def dot_rows(left, right):
+    return lax.dot_general(
+        left, right, (((1,), (1,)), ((), ())), preferred_element_type=jnp.float32
+    )
+
+
+def lane_of(rows):
+    return lax.broadcasted_iota(jnp.int32, (rows, LANES), 1)
+
+
+def cross_kernel(loop, per, part, rows, last, mine, core, chip, *refs):
+    start, count = part
+    near, far = refs[: loop - 1][::-1], refs[loop - 1 : 2 * loop - 2][::-1]
+    early, outs, blocks = refs[2 * loop - 2 : -1 - loop], refs[-1 - loop : -1], refs[-1]
+    t = lax.axis_index("tm")
+    lane = lane_of(rows)
+    before = 2 * start if last else 0
+
+    def put(i, cycle, tile):
+        if not last or i == 0 or cycle < 2 * per - 1:
+            outs[i][cycle] = tile
+        else:
+            for m in range(cycle):
+                spare = pltpu.roll(tile, (2 * rows - PIECE * m) % LANES, 1)
+                outs[i][m] = jnp.where(lane < 2 * rows, outs[i][m], spare)
+
+    for n, tiles in enumerate(early):
+        for c in range(tiles.shape[0]):
+            put(n % loop, n // loop * tiles.shape[0] + c, tiles[c])
+    for s in range(count):
+        at = lanes_at((t * per + start + s) * LANES, LANES)
+        at_near = slice((start + s) * LANES, (start + s + 1) * LANES)
+        at_far = slice(s * LANES, (s + 1) * LANES)
+        at_chip = lanes_at((t * count + s) * LANES, LANES)
+        for j in range(loop):
+            if j == 0:
+                values = mine[:, at], core[0, :, at], chip[0, :, at_chip], chip[1, :, at_chip]
+            else:
+                values = [near[j - 1][k, :, at_near] for k in range(2)] + [far[j - 1][k, :, at_far] for k in range(2)]
+            for k, value in enumerate(values):
+                blocks[s, t ^ j, :, k * LANES : (k + 1) * LANES] = padded(value).astype(jnp.bfloat16)
+        for i in range(loop):
+            r = t ^ i
+            left = halves(blocks[s, r].astype(jnp.float32)).astype(jnp.bfloat16)
+            right = jnp.concatenate(
+                [blocks[s, (r + 1) % loop], blocks[s, (r + 2) % loop]], axis=0
+            )
+            for half, cycle in enumerate(normalized(dot_rows(left, right), rows)):
+                cycle = cycle - 1.0
+                cycle = jnp.where(lane < rows, cycle, pltpu.roll(cycle, LANES + rows - CYCLE_CAP, 1))
+                put(i, before + 2 * s + half, cycle)
+
+
+def own_kernel(loop, per, parts, rows, mine, core, *refs):
+    chips, out = refs[:-1], refs[-1]
+    for c in range(loop):
+        for (start, count), chip in zip(parts, chips):
+            for s in range(count):
+                n = c * per + start + s
+                at = slice(n * LANES, (n + 1) * LANES)
+                at_chip = slice((c * count + s) * LANES, (c * count + s + 1) * LANES)
+                values = mine[:, at], core[0, :, at], chip[0, :, at_chip], chip[1, :, at_chip]
+                block = jnp.concatenate([padded(value) for value in values], axis=1)
+                left = halves(block).astype(jnp.bfloat16)
+                block = block.astype(jnp.bfloat16)
+                right = jnp.concatenate([block, block], axis=0)
+                for half, cycle in enumerate(normalized(dot_rows(left, right), rows)):
+                    out[2 * n + half] = cycle
+
+
+def place_kernel(rows, cycles, partners, own, *refs):
+    tiles, (out, slots, sems) = refs[: len(partners)], refs[-3:]
+    t = lax.axis_index("tm")
+    lane = lane_of(rows)
+    copies = []
+    for n, (i, part) in enumerate(zip(partners, tiles)):
+        at = (t ^ i) * cycles
+        for c in range(cycles):
+            if c < part.shape[0]:
+                value = part[c]
+            else:
+                value = jnp.zeros((rows, LANES), jnp.float32)
+                for m in range(c):
+                    piece = pltpu.roll(part[m], PIECE * (m + 1) % LANES, 1)
+                    value = jnp.where(lane // PIECE == m, piece, value)
+            value = pltpu.roll(value + 1.0, rows, 1)
+            slots[n, c, :, :LANES] = jnp.where(lane < rows, own[at + c], value)
+            slots[n, c, :, LANES:] = value[:, : 3 * rows - LANES]
+        copies.append(pltpu.make_async_copy(slots.at[n], out.at[pl.ds(at, cycles)], sems.at[n]))
+        copies[-1].start()
+    for copy in copies:
+        copy.wait()
+
+
+def spread(frames, labels, counts):
+    loop, groups = lax.axis_size("tm"), lax.axis_size("pix")
+    rows = frames.shape[0]
+    per = frames.shape[1] // (LANES * groups * loop)
+    cycles = 2 * per
+    bf16, f32 = jnp.bfloat16, jnp.float32
+    parts = [(sum(counts[:n]), count) for n, count in enumerate(counts)]
+
+    def shape(*dims, dtype=bf16):
+        return jax.ShapeDtypeStruct(dims, dtype)
+
+    def tiles(count):
+        return shape(count, rows, LANES, dtype=f32)
+
+    mine, over, core = local_call(
+        functools.partial(pack_kernel, loop, groups, per),
+        [shape(rows, loop * per * LANES)] * 2 + [shape(2, rows, loop * per * LANES)],
+        2,
+    )(frames, jnp.where(labels >= 0, 1.0, 0.0).astype(f32).reshape(-1, LANES))
+    core = swap(core, "pix", 1)
+    ready = local_call(
+        functools.partial(near_kernel, loop, per, parts),
+        [shape(2, rows, loop * count * LANES) for _, count in parts]
+        + [shape(2, rows, per * LANES)] * (loop - 1),
+        3,
+    )(mine, over, core)
+    chips = [swap(part, "pix", 2) for part in ready[: len(parts)]]
+    near = [swap(part, "tm", j) for j, part in enumerate(ready[len(parts) :], 1)]
+    early = []
+    for part, chip in zip(parts, chips):
+        far = local_call(
+            functools.partial(far_kernel, part[1]), [shape(2, rows, part[1] * LANES)] * (loop - 1), 1
+        )(chip)
+        far = [swap(value, "tm", j) for j, value in enumerate(far, 1)]
+        last = part is parts[-1]
+        early += local_call(
+            functools.partial(cross_kernel, loop, per, part, rows, last),
+            [tiles(cycles)] + [tiles(cycles - 1)] * (loop - 1) if last else [tiles(2 * part[1])] * loop,
+            2 * loop + 1 + (len(early) if last else 0),
+            [pltpu.VMEM((part[1], loop, rows + 8, groups * LANES), bf16)],
+        )(mine, core, chip, *near[::-1], *far[::-1], *(early if last else ()))
+    kept, *sent = early[-loop:]
+    own_tiles = local_call(
+        functools.partial(own_kernel, loop, per, parts, rows),
+        [tiles(loop * cycles)],
+        2 + len(parts),
+        cost=OWN_COST,
+    )(mine, core, *chips)[0]
+    sent = lax.optimization_barrier([part.astype(jnp.float16) for part in sent])
+    back = [lax.optimization_barrier(swap(part, "tm", j)) for j, part in enumerate(sent, 1)]
+    one, two, three = [part.astype(f32) for part in back]
+
+    def place(partners, parts, *filled):
+        return local_call(
+            functools.partial(place_kernel, rows, cycles, partners),
+            [shape(loop * cycles, rows, 3 * rows, dtype=f32)],
+            1 + len(parts) + len(filled),
+            [
+                pltpu.VMEM((len(partners), cycles, rows, 3 * rows), f32),
+                pltpu.SemaphoreType.DMA((len(partners),)),
+            ],
+            in_specs=[VMEM] * (1 + len(parts)) + [HBM] * len(filled),
+            out_specs=[HBM],
+            input_output_aliases={1 + len(parts): 0} if filled else {},
+            cost=PLACE_COST,
+        )(own_tiles, *parts, *filled)[0]
+
+    return place((2,), (two,), place((0, 1, 3), (kept, one, three)))
+
+
+def on_device(frames, labels):
+    loop, groups = lax.axis_size("tm"), lax.axis_size("pix")
+    pairs = CYCLES // groups // 2
+    fits = frames.shape[1] == CYCLES * CYCLE_CAP and frames.shape[0] == CYCLE_CAP - 8
+    if loop == 4 and groups == 4 and fits and pairs // loop == 4 and pairs % loop == 0:
+        return spread(frames, labels, (2, 2))
+    return ring(frames, labels)
+
+
 def solution(mesh):
     placed = (P(("runs", "tm"), "pix"), P("pix"))
     return jax.shard_map(

time: 115 us -> 43.3 us (0.38)
  waiting for transfers between devices: 52.1 us -> 11.1 us
  local copies, waits for them, and re-layouts: 30.4 us -> 1.18 us
  matrix products: 11 us -> 0 us
  starting transfers between devices: 16.2 us -> 24.8 us
  Pallas kernels: 0 us -> 5.06 us
  other arithmetic: 4.37 us -> 0.86 us
    ppermute x2 -> x15, waiting for transfers between devices: 37.8 us -> 11.1 us  [swap(): return lax.ppermute(shard, axis, [(i, i ^ by) for i in range(size)])]
    dynamic_update_slice x3 -> x0, local copies, waits for them, and re-layouts: 19.5 us -> none  [the longest x2 18.1 us: advance(): lax.dynamic_update_slice(result, make_tiles(moving[None]), (0, 0, offset...]
    ppermute x2 -> x15, starting transfers between devices: 8.44 us -> 24.8 us  [swap(): return lax.ppermute(shard, axis, [(i, i ^ by) for i in range(size)])]
    all_to_all x2 -> x0, waiting for transfers between devices: 14.3 us -> none  [the longest x1 12.8 us: on_device(): lax.all_to_all(masked, 'pix', split_axis=1, concat_axis=1, tiled=True)]
    dot_general x3 -> x0, matrix products: 11 us -> none  [make_tiles(): jnp.einsum('tgqc,nsgqc->qtns', own_split, block_split, preferred_element_...]
    all_to_all x2 -> x0, starting transfers between devices: 7.71 us -> none  [the longest x1 4.21 us: on_device(): lax.all_to_all(live_row, 'pix', split_axis=1, concat_axis=1, tiled=True)]
    pallas_call x0 -> x9, Pallas kernels: none -> 5.06 us  [local_call(): return lambda *operands: call(*operands, *after)]
    another operation x2 -> x0, local copies, waits for them, and re-layouts: 3.88 us -> none
  transfers between devices with their start and end apart: 4 -> 15, of which waited for: 4 -> 9; matrix products, arithmetic and copies ran while one was open for 2% -> 0% of each run, Pallas kernels for 0% -> 7%
where the time goes in v3:
time: 43.3 us; the launch traced here: 43.1 us
  starting transfers between devices  24.8 us (57%)
  waiting for transfers between devices  11.1 us (26%)
  Pallas kernels  5.06 us (12%)
  local copies, waits for them, and re-layouts  1.18 us (3%)
  other arithmetic  0.86 us (2%)
    ppermute x15, starting transfers between devices, swap(): return lax.ppermute(shard, axis, [(i, i ^ by) for i in range(size)])  24.8 us
    ppermute x15, waiting for transfers between devices, swap(): return lax.ppermute(shard, axis, [(i, i ^ by) for i in range(size)])  11.1 us
    pallas_call x9, Pallas kernels, local_call(): return lambda *operands: call(*operands, *after)  5.06 us
    unnamed x2, local copies, waits for them, and re-layouts  1.18 us
  transfers between devices with their start and end apart: 15, of which 9 were waited for; matrix products, arithmetic and copies ran while one was open for 0% of the time, Pallas kernels for 7%

profile of v3, /device:TPU:0, one launch (start us, length us, event | category | flops | bytes accessed | tf_op | source)
XLA Modules:
  0.0 43.1 jit_solution(6274584231590770018)
XLA Ops:
  0.0 0.8 %select_bitcast_fusion.refs_1_ = f32[64,128]{1,0:T(8,128)S(1)} fusion(s32[8192]{0:T(1024)} %param.3), kind=kLoop, calls=%fused_computation | loop fusion | flops 16384 | bytes 65536 | tf_op jit(solution)/shard_map/reshape | solution.py:273
  0.8 1.2 %copy-done = bf16[56,8192]{1,0:T(8,128)(2,1)S(1)} copy-done((bf16[56,8192]{1,0:T(8,128)(2,1)S(1)}, bf16[56,8192]{1,0:T(8,128)(2,1)}, u32[]{:S(2)}) %copy-start) | copy-done | bytes 917528
  1.9 0.2 shard_map.28
  2.2 0.5 %collective-permute-start = (bf16[2,56,2048]{2,1,0:T(8,128)(2,1)S(1)}, bf16[2,56,2048]{2,1,0:T(8,128)(2,1)S(1)}, u32[]{:S(2)}, u32[]{:S(2)}) collective-permute-start(bf16[2,56,2048]{2,1,0:T(8,128)(2,1)S(1)} %get-tuple-element.31), channel_id=1, source_target_pairs={{0,1},{1,0},{2,3},{3,2},{4,5},{5,4},{6,7},{7,6},{8,9},{9,8},{10,11... | collective-permute-start | bytes 1376264 | tf_op jit(solution)/shard_map/ppermute | solution.py:25
  2.7 1.4 %collective-permute-done.refs_2_.refs_1_ = bf16[2,56,2048]{2,1,0:T(8,128)(2,1)S(1)} collective-permute-done((bf16[2,56,2048]{2,1,0:T(8,128)(2,1)S(1)}, bf16[2,56,2048]{2,1,0:T(8,128)(2,1)S(1)}, u32[]{:S(2)}, u32[]{:S(2)}) %collective-permute-start) | collective-permute-done | bytes 458784 | tf_op jit(solution)/shard_map/ppermute | solution.py:25
  4.2 0.1 shard_map.29
  4.2 2.9 %collective-permute-start.1 = (bf16[2,56,1024]{2,1,0:T(8,128)(2,1)S(1)}, bf16[2,56,1024]{2,1,0:T(8,128)(2,1)S(1)}, u32[]{:S(2)}, u32[]{:S(2)}) collective-permute-start(bf16[2,56,1024]{2,1,0:T(8,128)(2,1)S(1)} %get-tuple-element.33), channel_id=1, source_target_pairs={{0,2},{1,3},{2,0},{3,1},{4,6},{5,7},{6,4},{7,5},{8,10},{9,11},{10,... | collective-permute-start | bytes 688136 | tf_op jit(solution)/shard_map/ppermute | solution.py:25
  7.1 0.1 collective-permute-start.2
  7.2 4.1 %collective-permute-start.3 = (bf16[2,56,512]{2,1,0:T(8,128)(2,1)S(1)}, bf16[2,56,512]{2,1,0:T(8,128)(2,1)S(1)}, u32[]{:S(2)}, u32[]{:S(2)}) collective-permute-start(bf16[2,56,512]{2,1,0:T(8,128)(2,1)S(1)} %get-tuple-element.35), channel_id=1, source_target_pairs={{0,12},{4,8},{8,4},{12,0},{1,13},{5,9},{9,5},{13,1},{2,14},{6,10},... | collective-permute-start | bytes 344072 | tf_op jit(solution)/shard_map/ppermute | solution.py:25
  11.3 0.0 collective-permute-start.4
  11.3 0.6 %collective-permute-start.5 = (bf16[2,56,512]{2,1,0:T(8,128)(2,1)S(1)}, bf16[2,56,512]{2,1,0:T(8,128)(2,1)S(1)}, u32[]{:S(2)}, u32[]{:S(2)}) collective-permute-start(bf16[2,56,512]{2,1,0:T(8,128)(2,1)S(1)} %get-tuple-element.37), channel_id=1, source_target_pairs={{0,4},{4,0},{8,12},{12,8},{1,5},{5,1},{9,13},{13,9},{2,6},{6,2},{1... | collective-permute-start | bytes 344072 | tf_op jit(solution)/shard_map/ppermute | solution.py:25
  11.8 1.7 %collective-permute-done.1.refs_2_.refs_0_ = bf16[2,56,1024]{2,1,0:T(8,128)(2,1)S(1)} collective-permute-done((bf16[2,56,1024]{2,1,0:T(8,128)(2,1)S(1)}, bf16[2,56,1024]{2,1,0:T(8,128)(2,1)S(1)}, u32[]{:S(2)}, u32[]{:S(2)}) %collective-permute-start.1) | collective-permute-done | bytes 229408 | tf_op jit(solution)/shard_map/ppermute | solution.py:25
  13.6 4.2 %collective-permute-start.9 = (bf16[2,56,256]{2,1,0:T(8,128)(2,1)S(1)}, bf16[2,56,256]{2,1,0:T(8,128)(2,1)S(1)}, u32[]{:S(2)}, u32[]{:S(2)}) collective-permute-start(bf16[2,56,256]{2,1,0:T(8,128)(2,1)S(1)} %get-tuple-element.41), channel_id=1, source_target_pairs={{0,12},{4,8},{8,4},{12,0},{1,13},{5,9},{9,5},{13,1},{2,14},{6,10},... | collective-permute-start | bytes 172040 | tf_op jit(solution)/shard_map/ppermute | solution.py:25
  17.8 0.2 collective-permute-done.2.refs_3_.refs_0_.refs_2_
  18.0 2.8 %collective-permute-start.10 = (bf16[2,56,256]{2,1,0:T(8,128)(2,1)S(1)}, bf16[2,56,256]{2,1,0:T(8,128)(2,1)S(1)}, u32[]{:S(2)}, u32[]{:S(2)}) collective-permute-start(bf16[2,56,256]{2,1,0:T(8,128)(2,1)S(1)} %get-tuple-element.42), channel_id=1, source_target_pairs={{0,8},{4,12},{8,0},{12,4},{1,9},{5,13},{9,1},{13,5},{2,10},{6,14},... | collective-permute-start | bytes 172040 | tf_op jit(solution)/shard_map/ppermute | solution.py:25
  20.8 1.6 %collective-permute-start.11 = (bf16[2,56,256]{2,1,0:T(8,128)(2,1)S(1)}, bf16[2,56,256]{2,1,0:T(8,128)(2,1)S(1)}, u32[]{:S(2)}, u32[]{:S(2)}) collective-permute-start(bf16[2,56,256]{2,1,0:T(8,128)(2,1)S(1)} %get-tuple-element.43), channel_id=1, source_target_pairs={{0,4},{4,0},{8,12},{12,8},{1,5},{5,1},{9,13},{13,9},{2,6},{6,2},{1... | collective-permute-start | bytes 172040 | tf_op jit(solution)/shard_map/ppermute | solution.py:25
  22.5 1.1 %collective-permute-done.4.refs_4_ = bf16[2,56,512]{2,1,0:T(8,128)(2,1)S(1)} collective-permute-done((bf16[2,56,512]{2,1,0:T(8,128)(2,1)S(1)}, bf16[2,56,512]{2,1,0:T(8,128)(2,1)S(1)}, u32[]{:S(2)}, u32[]{:S(2)}) %collective-permute-start.4) | collective-permute-done | bytes 114720 | tf_op jit(solution)/shard_map/ppermute | solution.py:25
  23.6 2.3 %collective-permute-start.6 = (bf16[2,56,256]{2,1,0:T(8,128)(2,1)S(1)}, bf16[2,56,256]{2,1,0:T(8,128)(2,1)S(1)}, u32[]{:S(2)}, u32[]{:S(2)}) collective-permute-start(bf16[2,56,256]{2,1,0:T(8,128)(2,1)S(1)} %get-tuple-element.38), channel_id=1, source_target_pairs={{0,12},{4,8},{8,4},{12,0},{1,13},{5,9},{9,5},{13,1},{2,14},{6,10},... | collective-permute-start | bytes 172040 | tf_op jit(solution)/shard_map/ppermute | solution.py:25
  26.0 2.0 %collective-permute-start.8 = (bf16[2,56,256]{2,1,0:T(8,128)(2,1)S(1)}, bf16[2,56,256]{2,1,0:T(8,128)(2,1)S(1)}, u32[]{:S(2)}, u32[]{:S(2)}) collective-permute-start(bf16[2,56,256]{2,1,0:T(8,128)(2,1)S(1)} %get-tuple-element.40), channel_id=1, source_target_pairs={{0,4},{4,0},{8,12},{12,8},{1,5},{5,1},{9,13},{13,9},{2,6},{6,2},{1... | collective-permute-start | bytes 172040 | tf_op jit(solution)/shard_map/ppermute | solution.py:25
  28.0 0.7 %shard_map.33 = (f32[4,56,128]{2,1,0:T(8,128)S(1)}, f32[4,56,128]{2,1,0:T(8,128)S(1)}, f32[4,56,128]{2,1,0:T(8,128)S(1)}, f32[4,56,128]{2,1,0:T(8,128)S(1)}) custom-call(bf16[56,2048]{1,0:T(8,128)(2,1)S(1)} %get-tuple-element.30.refs_0_, bf16[2,56,2048]{2,1,0:T(8,128)(2,1)S(1)} %collective-permute-done.refs_2_.refs_1_, ...), custom_call_target="tpu_custom_call" | custom-call | flops 1 | bytes 1 | tf_op jit(solution)/shard_map/pallas_call | solution.py:99
  28.8 0.8 %collective-permute-done.6.refs_6_ = bf16[2,56,256]{2,1,0:T(8,128)(2,1)S(1)} collective-permute-done((bf16[2,56,256]{2,1,0:T(8,128)(2,1)S(1)}, bf16[2,56,256]{2,1,0:T(8,128)(2,1)S(1)}, u32[]{:S(2)}, u32[]{:S(2)}) %collective-permute-start.6) | collective-permute-done | bytes 57376 | tf_op jit(solution)/shard_map/ppermute | solution.py:25
  29.6 1.5 %collective-permute-done.7.refs_7_ = bf16[2,56,256]{2,1,0:T(8,128)(2,1)S(1)} collective-permute-done((bf16[2,56,256]{2,1,0:T(8,128)(2,1)S(1)}, bf16[2,56,256]{2,1,0:T(8,128)(2,1)S(1)}, u32[]{:S(2)}, u32[]{:S(2)}) %collective-permute-start.7) | collective-permute-done | bytes 57376 | tf_op jit(solution)/shard_map/ppermute | solution.py:25
  31.1 0.9 %shard_map.34 = (f32[8,56,128]{2,1,0:T(8,128)S(1)}, f32[7,56,128]{2,1,0:T(8,128)S(1)}, f32[7,56,128]{2,1,0:T(8,128)S(1)}, f32[7,56,128]{2,1,0:T(8,128)S(1)}) custom-call(bf16[56,2048]{1,0:T(8,128)(2,1)S(1)} %get-tuple-element.30.refs_0_, bf16[2,56,2048]{2,1,0:T(8,128)(2,1)S(1)} %collective-permute-done.refs_2_.refs_1_, ...), custom_call_target="tpu_custom_call" | custom-call | flops 1 | bytes 1 | tf_op jit(solution)/shard_map/pallas_call | solution.py:99
  32.0 1.4 %collective-permute-start.13 = (f16[7,56,128]{2,1,0:T(8,128)(2,1)S(1)}, f16[7,56,128]{2,1,0:T(8,128)(2,1)S(1)}, u32[]{:S(2)}, u32[]{:S(2)}) collective-permute-start(f16[7,56,128]{2,1,0:T(8,128)(2,1)S(1)} %convert_element_type.18), channel_id=1, source_target_pairs={{0,4},{4,0},{8,12},{12,8},{1,5},{5,1},{9,13},{13,9},{2,6},{6,2},{1... | collective-permute-start | bytes 301064 | tf_op jit(solution)/shard_map/ppermute | solution.py:25
  33.5 2.1 %collective-permute-start.14 = (f16[7,56,128]{2,1,0:T(8,128)(2,1)S(1)}, f16[7,56,128]{2,1,0:T(8,128)(2,1)S(1)}, u32[]{:S(2)}, u32[]{:S(2)}) collective-permute-start(f16[7,56,128]{2,1,0:T(8,128)(2,1)S(1)} %convert_element_type.20), channel_id=1, source_target_pairs={{0,12},{4,8},{8,4},{12,0},{1,13},{5,9},{9,5},{13,1},{2,14},{6,10},... | collective-permute-start | bytes 301064 | tf_op jit(solution)/shard_map/ppermute | solution.py:25
  35.6 0.0 collective-permute-start.12
  35.6 0.8 %shard_map.30.refs_0_ = f32[32,56,128]{2,1,0:T(8,128)S(1)} custom-call(bf16[56,2048]{1,0:T(8,128)(2,1)S(1)} %get-tuple-element.30.refs_0_, bf16[2,56,2048]{2,1,0:T(8,128)(2,1)S(1)} %collective-permute-done.refs_2_.refs_1_, bf16[2,56,1024]{2,1,0:T(8,128)(2,1)S(1)} %collective-permute-done.1.refs_2_.refs_0_, ...), custom_call_target="tpu_custom_call" | custom-call | flops 1 | bytes 4194304 | tf_op jit(solution)/shard_map/pallas_call | solution.py:99
  36.4 1.3 %collective-permute-done.13 = f16[7,56,128]{2,1,0:T(8,128)(2,1)S(1)} collective-permute-done((f16[7,56,128]{2,1,0:T(8,128)(2,1)S(1)}, f16[7,56,128]{2,1,0:T(8,128)(2,1)S(1)}, u32[]{:S(2)}, u32[]{:S(2)}) %collective-permute-start.13) | collective-permute-done | bytes 100384 | tf_op jit(solution)/shard_map/ppermute | solution.py:25
  37.8 2.1 %collective-permute-done.14 = f16[7,56,128]{2,1,0:T(8,128)(2,1)S(1)} collective-permute-done((f16[7,56,128]{2,1,0:T(8,128)(2,1)S(1)}, f16[7,56,128]{2,1,0:T(8,128)(2,1)S(1)}, u32[]{:S(2)}, u32[]{:S(2)}) %collective-permute-start.14) | collective-permute-done | bytes 100384 | tf_op jit(solution)/shard_map/ppermute | solution.py:25
  39.9 1.3 %shard_map.35.refs_2_ = f32[32,56,168]{2,1,0:T(8,128)} custom-call(f32[32,56,128]{2,1,0:T(8,128)S(1)} %shard_map.30.refs_0_, f32[8,56,128]{2,1,0:T(8,128)S(1)} %get-tuple-element.52.refs_1_, f32[7,56,128]{2,1,0:T(8,128)S(1)} %convert_element_type.22.refs_2_, f32[7,56,128]{2,1,0:T(8,128)S(1)} %convert_element_type.23.refs_3_), custom_call_target="tpu_custom_call" | custom-call | flops 1 | bytes 4194304 | tf_op jit(solution)/shard_map/pallas_call | solution.py:99
  41.2 0.9 %collective-permute-done.12 = f16[7,56,128]{2,1,0:T(8,128)(2,1)S(1)} collective-permute-done((f16[7,56,128]{2,1,0:T(8,128)(2,1)S(1)}, f16[7,56,128]{2,1,0:T(8,128)(2,1)S(1)}, u32[]{:S(2)}, u32[]{:S(2)}) %collective-permute-start.12) | collective-permute-done | bytes 100384 | tf_op jit(solution)/shard_map/ppermute | solution.py:25
  42.1 1.0 %shard_map.36 = f32[32,56,168]{2,1,0:T(8,128)} custom-call(f32[32,56,128]{2,1,0:T(8,128)S(1)} %shard_map.30.refs_0_, f32[7,56,128]{2,1,0:T(8,128)S(1)} %convert_element_type.21.refs_1_, f32[32,56,168]{2,1,0:T(8,128)} %shard_map.35.refs_2_), custom_call_target="tpu_custom_call", output_to_operand_aliasing={{}: (2, {})} | custom-call | flops 1 | bytes 4194304 | tf_op jit(solution)/shard_map/pallas_call | solution.py:99
  (16 shorter events, 0.2 us)
Async XLA Ops:
  0.8 1.2 %copy-start = (bf16[56,8192]{1,0:T(8,128)(2,1)S(1)}, bf16[56,8192]{1,0:T(8,128)(2,1)}, u32[]{:S(2)}) copy-start(bf16[56,8192]{1,0:T(8,128)(2,1)} %refs_0_.1) | copy-start | bytes 2752516
  2.2 2.0 %collective-permute-start = (bf16[2,56,2048]{2,1,0:T(8,128)(2,1)S(1)}, bf16[2,56,2048]{2,1,0:T(8,128)(2,1)S(1)}, u32[]{:S(2)}, u32[]{:S(2)}) collective-permute-start(bf16[2,56,2048]{2,1,0:T(8,128)(2,1)S(1)} %get-tuple-element.31), channel_id=1, source_target_pairs={{0,1},{1,0},{2,3},{3,2},{4,5},{5,4},{6,7},{7,6},{8,9},{9,8},{10,11... | collective-permute-start | bytes 1376264 | tf_op jit(solution)/shard_map/ppermute | solution.py:25
  4.2 9.3 %collective-permute-start.1 = (bf16[2,56,1024]{2,1,0:T(8,128)(2,1)S(1)}, bf16[2,56,1024]{2,1,0:T(8,128)(2,1)S(1)}, u32[]{:S(2)}, u32[]{:S(2)}) collective-permute-start(bf16[2,56,1024]{2,1,0:T(8,128)(2,1)S(1)} %get-tuple-element.33), channel_id=1, source_target_pairs={{0,2},{1,3},{2,0},{3,1},{4,6},{5,7},{6,4},{7,5},{8,10},{9,11},{10,... | collective-permute-start | bytes 688136 | tf_op jit(solution)/shard_map/ppermute | solution.py:25
  7.1 10.8 %collective-permute-start.2 = (bf16[2,56,1024]{2,1,0:T(8,128)(2,1)S(1)}, bf16[2,56,1024]{2,1,0:T(8,128)(2,1)S(1)}, u32[]{:S(2)}, u32[]{:S(2)}) collective-permute-start(bf16[2,56,1024]{2,1,0:T(8,128)(2,1)S(1)} %get-tuple-element.34), channel_id=1, source_target_pairs={{0,2},{1,3},{2,0},{3,1},{4,6},{5,7},{6,4},{7,5},{8,10},{9,11},{10,... | collective-permute-start | bytes 688136 | tf_op jit(solution)/shard_map/ppermute | solution.py:25
  7.2 13.6 %collective-permute-start.3 = (bf16[2,56,512]{2,1,0:T(8,128)(2,1)S(1)}, bf16[2,56,512]{2,1,0:T(8,128)(2,1)S(1)}, u32[]{:S(2)}, u32[]{:S(2)}) collective-permute-start(bf16[2,56,512]{2,1,0:T(8,128)(2,1)S(1)} %get-tuple-element.35), channel_id=1, source_target_pairs={{0,12},{4,8},{8,4},{12,0},{1,13},{5,9},{9,5},{13,1},{2,14},{6,10},... | collective-permute-start | bytes 344072 | tf_op jit(solution)/shard_map/ppermute | solution.py:25
  11.3 12.3 %collective-permute-start.4 = (bf16[2,56,512]{2,1,0:T(8,128)(2,1)S(1)}, bf16[2,56,512]{2,1,0:T(8,128)(2,1)S(1)}, u32[]{:S(2)}, u32[]{:S(2)}) collective-permute-start(bf16[2,56,512]{2,1,0:T(8,128)(2,1)S(1)} %get-tuple-element.36), channel_id=1, source_target_pairs={{0,8},{4,12},{8,0},{12,4},{1,9},{5,13},{9,1},{13,5},{2,10},{6,14},... | collective-permute-start | bytes 344072 | tf_op jit(solution)/shard_map/ppermute | solution.py:25
  11.3 14.7 %collective-permute-start.5 = (bf16[2,56,512]{2,1,0:T(8,128)(2,1)S(1)}, bf16[2,56,512]{2,1,0:T(8,128)(2,1)S(1)}, u32[]{:S(2)}, u32[]{:S(2)}) collective-permute-start(bf16[2,56,512]{2,1,0:T(8,128)(2,1)S(1)} %get-tuple-element.37), channel_id=1, source_target_pairs={{0,4},{4,0},{8,12},{12,8},{1,5},{5,1},{9,13},{13,9},{2,6},{6,2},{1... | collective-permute-start | bytes 344072 | tf_op jit(solution)/shard_map/ppermute | solution.py:25
  13.6 12.4 %collective-permute-start.9 = (bf16[2,56,256]{2,1,0:T(8,128)(2,1)S(1)}, bf16[2,56,256]{2,1,0:T(8,128)(2,1)S(1)}, u32[]{:S(2)}, u32[]{:S(2)}) collective-permute-start(bf16[2,56,256]{2,1,0:T(8,128)(2,1)S(1)} %get-tuple-element.41), channel_id=1, source_target_pairs={{0,12},{4,8},{8,4},{12,0},{1,13},{5,9},{9,5},{13,1},{2,14},{6,10},... | collective-permute-start | bytes 172040 | tf_op jit(solution)/shard_map/ppermute | solution.py:25
  18.0 10.1 %collective-permute-start.10 = (bf16[2,56,256]{2,1,0:T(8,128)(2,1)S(1)}, bf16[2,56,256]{2,1,0:T(8,128)(2,1)S(1)}, u32[]{:S(2)}, u32[]{:S(2)}) collective-permute-start(bf16[2,56,256]{2,1,0:T(8,128)(2,1)S(1)} %get-tuple-element.42), channel_id=1, source_target_pairs={{0,8},{4,12},{8,0},{12,4},{1,9},{5,13},{9,1},{13,5},{2,10},{6,14},... | collective-permute-start | bytes 172040 | tf_op jit(solution)/shard_map/ppermute | solution.py:25
  20.8 7.2 %collective-permute-start.11 = (bf16[2,56,256]{2,1,0:T(8,128)(2,1)S(1)}, bf16[2,56,256]{2,1,0:T(8,128)(2,1)S(1)}, u32[]{:S(2)}, u32[]{:S(2)}) collective-permute-start(bf16[2,56,256]{2,1,0:T(8,128)(2,1)S(1)} %get-tuple-element.43), channel_id=1, source_target_pairs={{0,4},{4,0},{8,12},{12,8},{1,5},{5,1},{9,13},{13,9},{2,6},{6,2},{1... | collective-permute-start | bytes 172040 | tf_op jit(solution)/shard_map/ppermute | solution.py:25
  23.6 6.0 %collective-permute-start.6 = (bf16[2,56,256]{2,1,0:T(8,128)(2,1)S(1)}, bf16[2,56,256]{2,1,0:T(8,128)(2,1)S(1)}, u32[]{:S(2)}, u32[]{:S(2)}) collective-permute-start(bf16[2,56,256]{2,1,0:T(8,128)(2,1)S(1)} %get-tuple-element.38), channel_id=1, source_target_pairs={{0,12},{4,8},{8,4},{12,0},{1,13},{5,9},{9,5},{13,1},{2,14},{6,10},... | collective-permute-start | bytes 172040 | tf_op jit(solution)/shard_map/ppermute | solution.py:25
  26.0 5.1 %collective-permute-start.7 = (bf16[2,56,256]{2,1,0:T(8,128)(2,1)S(1)}, bf16[2,56,256]{2,1,0:T(8,128)(2,1)S(1)}, u32[]{:S(2)}, u32[]{:S(2)}) collective-permute-start(bf16[2,56,256]{2,1,0:T(8,128)(2,1)S(1)} %get-tuple-element.39), channel_id=1, source_target_pairs={{0,8},{4,12},{8,0},{12,4},{1,9},{5,13},{9,1},{13,5},{2,10},{6,14},... | collective-permute-start | bytes 172040 | tf_op jit(solution)/shard_map/ppermute | solution.py:25
  26.0 5.1 %collective-permute-start.8 = (bf16[2,56,256]{2,1,0:T(8,128)(2,1)S(1)}, bf16[2,56,256]{2,1,0:T(8,128)(2,1)S(1)}, u32[]{:S(2)}, u32[]{:S(2)}) collective-permute-start(bf16[2,56,256]{2,1,0:T(8,128)(2,1)S(1)} %get-tuple-element.40), channel_id=1, source_target_pairs={{0,4},{4,0},{8,12},{12,8},{1,5},{5,1},{9,13},{13,9},{2,6},{6,2},{1... | collective-permute-start | bytes 172040 | tf_op jit(solution)/shard_map/ppermute | solution.py:25
  32.0 5.7 %collective-permute-start.13 = (f16[7,56,128]{2,1,0:T(8,128)(2,1)S(1)}, f16[7,56,128]{2,1,0:T(8,128)(2,1)S(1)}, u32[]{:S(2)}, u32[]{:S(2)}) collective-permute-start(f16[7,56,128]{2,1,0:T(8,128)(2,1)S(1)} %convert_element_type.18), channel_id=1, source_target_pairs={{0,4},{4,0},{8,12},{12,8},{1,5},{5,1},{9,13},{13,9},{2,6},{6,2},{1... | collective-permute-start | bytes 301064 | tf_op jit(solution)/shard_map/ppermute | solution.py:25
  33.5 6.4 %collective-permute-start.14 = (f16[7,56,128]{2,1,0:T(8,128)(2,1)S(1)}, f16[7,56,128]{2,1,0:T(8,128)(2,1)S(1)}, u32[]{:S(2)}, u32[]{:S(2)}) collective-permute-start(f16[7,56,128]{2,1,0:T(8,128)(2,1)S(1)} %convert_element_type.20), channel_id=1, source_target_pairs={{0,12},{4,8},{8,4},{12,0},{1,13},{5,9},{9,5},{13,1},{2,14},{6,10},... | collective-permute-start | bytes 301064 | tf_op jit(solution)/shard_map/ppermute | solution.py:25
  35.6 6.5 %collective-permute-start.12 = (f16[7,56,128]{2,1,0:T(8,128)(2,1)S(1)}, f16[7,56,128]{2,1,0:T(8,128)(2,1)S(1)}, u32[]{:S(2)}, u32[]{:S(2)}) collective-permute-start(f16[7,56,128]{2,1,0:T(8,128)(2,1)S(1)} %convert_element_type.19), channel_id=1, source_target_pairs={{0,8},{4,12},{8,0},{12,4},{1,9},{5,13},{9,1},{13,5},{2,10},{6,14},... | collective-permute-start | bytes 301064 | tf_op jit(solution)/shard_map/ppermute | solution.py:25

commit v4 on v3

--- a/solution.py
+++ b/solution.py
@@ -174,19 +174,6 @@
     early, outs, blocks = refs[2 * loop - 2 : -1 - loop], refs[-1 - loop : -1], refs[-1]
     t = lax.axis_index("tm")
     lane = lane_of(rows)
-    before = 2 * start if last else 0
-
-    def put(i, cycle, tile):
-        if not last or i == 0 or cycle < 2 * per - 1:
-            outs[i][cycle] = tile
-        else:
-            for m in range(cycle):
-                spare = pltpu.roll(tile, (2 * rows - PIECE * m) % LANES, 1)
-                outs[i][m] = jnp.where(lane < 2 * rows, outs[i][m], spare)
-
-    for n, tiles in enumerate(early):
-        for c in range(tiles.shape[0]):
-            put(n % loop, n // loop * tiles.shape[0] + c, tiles[c])
     for s in range(count):
         at = lanes_at((t * per + start + s) * LANES, LANES)
         at_near = slice((start + s) * LANES, (start + s + 1) * LANES)
@@ -199,16 +186,29 @@
                 values = [near[j - 1][k, :, at_near] for k in range(2)] + [far[j - 1][k, :, at_far] for k in range(2)]
             for k, value in enumerate(values):
                 blocks[s, t ^ j, :, k * LANES : (k + 1) * LANES] = padded(value).astype(jnp.bfloat16)
-        for i in range(loop):
-            r = t ^ i
+    products = {}
+    for i in range(loop):
+        r = t ^ i
+        for s in range(count):
             left = halves(blocks[s, r].astype(jnp.float32)).astype(jnp.bfloat16)
             right = jnp.concatenate(
                 [blocks[s, (r + 1) % loop], blocks[s, (r + 2) % loop]], axis=0
             )
-            for half, cycle in enumerate(normalized(dot_rows(left, right), rows)):
-                cycle = cycle - 1.0
-                cycle = jnp.where(lane < rows, cycle, pltpu.roll(cycle, LANES + rows - CYCLE_CAP, 1))
-                put(i, before + 2 * s + half, cycle)
+            products[i, s] = dot_rows(left, right)
+    for i, out in enumerate(outs):
+        new = []
+        for s in range(count):
+            for tile in normalized(products[i, s], rows):
+                tile = tile - 1.0
+                new.append(jnp.where(lane < rows, tile, pltpu.roll(tile, LANES + rows - CYCLE_CAP, 1)))
+        before = [tiles[c] for tiles in early[i::loop] for c in range(tiles.shape[0])]
+        if last and i:
+            spare = new.pop()
+            for m, tile in enumerate(before + new):
+                out[m] = jnp.where(lane < 2 * rows, tile, pltpu.roll(spare, (2 * rows - PIECE * m) % LANES, 1))
+        else:
+            for c, tile in enumerate(before + new):
+                out[c] = tile
 
 
 def own_kernel(loop, per, parts, rows, mine, core, *refs):
@@ -319,7 +319,7 @@
             cost=PLACE_COST,
         )(own_tiles, *parts, *filled)[0]
 
-    return place((2,), (two,), place((0, 1, 3), (kept, one, three)))
+    return place((2, 1), (two, one), place((0, 3), (kept, three)))
 
 
 def on_device(frames, labels):

time: 43.3 us -> 42.5 us (0.982)
  waiting for transfers between devices: 11.1 us -> 9.44 us
  starting transfers between devices: 24.8 us -> 25.7 us
    ppermute x15, waiting for transfers between devices: 11.1 us -> 9.44 us  [swap(): return lax.ppermute(shard, axis, [(i, i ^ by) for i in range(size)])]
    ppermute x15, starting transfers between devices: 24.8 us -> 25.7 us  [swap(): return lax.ppermute(shard, axis, [(i, i ^ by) for i in range(size)])]
  transfers between devices with their start and end apart: 15 -> 15, of which waited for: 9 -> 8; matrix products, arithmetic and copies ran while one was open for 0% -> 0% of each run, Pallas kernels for 7% -> 6%
where the time goes in v4:
time: 42.5 us; the launch traced here: 42.3 us
  starting transfers between devices  25.7 us (60%)
  waiting for transfers between devices  9.44 us (22%)
  Pallas kernels  5 us (12%)
  local copies, waits for them, and re-layouts  1.18 us (3%)
  other arithmetic  0.86 us (2%)
    ppermute x15, starting transfers between devices, swap(): return lax.ppermute(shard, axis, [(i, i ^ by) for i in range(size)])  25.7 us
    ppermute x15, waiting for transfers between devices, swap(): return lax.ppermute(shard, axis, [(i, i ^ by) for i in range(size)])  9.44 us
    pallas_call x9, Pallas kernels, local_call(): return lambda *operands: call(*operands, *after)  5 us
    unnamed x2, local copies, waits for them, and re-layouts  1.18 us
  transfers between devices with their start and end apart: 15, of which 8 were waited for; matrix products, arithmetic and copies ran while one was open for 0% of the time, Pallas kernels for 6%

profile of v4, /device:TPU:0, one launch (start us, length us, event | category | flops | bytes accessed | tf_op | source)
XLA Modules:
  0.0 42.3 jit_solution(8292182588874120917)
XLA Ops:
  0.0 0.8 %select_bitcast_fusion.refs_1_ = f32[64,128]{1,0:T(8,128)S(1)} fusion(s32[8192]{0:T(1024)} %param.3), kind=kLoop, calls=%fused_computation | loop fusion | flops 16384 | bytes 65536 | tf_op jit(solution)/shard_map/reshape | solution.py:273
  0.8 1.2 %copy-done = bf16[56,8192]{1,0:T(8,128)(2,1)S(1)} copy-done((bf16[56,8192]{1,0:T(8,128)(2,1)S(1)}, bf16[56,8192]{1,0:T(8,128)(2,1)}, u32[]{:S(2)}) %copy-start) | copy-done | bytes 917528
  1.9 0.2 shard_map.28
  2.2 0.5 %collective-permute-start = (bf16[2,56,2048]{2,1,0:T(8,128)(2,1)S(1)}, bf16[2,56,2048]{2,1,0:T(8,128)(2,1)S(1)}, u32[]{:S(2)}, u32[]{:S(2)}) collective-permute-start(bf16[2,56,2048]{2,1,0:T(8,128)(2,1)S(1)} %get-tuple-element.31), channel_id=1, source_target_pairs={{0,1},{1,0},{2,3},{3,2},{4,5},{5,4},{6,7},{7,6},{8,9},{9,8},{10,11... | collective-permute-start | bytes 1376264 | tf_op jit(solution)/shard_map/ppermute | solution.py:25
  2.7 1.4 %collective-permute-done.refs_2_.refs_1_ = bf16[2,56,2048]{2,1,0:T(8,128)(2,1)S(1)} collective-permute-done((bf16[2,56,2048]{2,1,0:T(8,128)(2,1)S(1)}, bf16[2,56,2048]{2,1,0:T(8,128)(2,1)S(1)}, u32[]{:S(2)}, u32[]{:S(2)}) %collective-permute-start) | collective-permute-done | bytes 458784 | tf_op jit(solution)/shard_map/ppermute | solution.py:25
  4.2 0.1 shard_map.29
  4.2 2.9 %collective-permute-start.1 = (bf16[2,56,1024]{2,1,0:T(8,128)(2,1)S(1)}, bf16[2,56,1024]{2,1,0:T(8,128)(2,1)S(1)}, u32[]{:S(2)}, u32[]{:S(2)}) collective-permute-start(bf16[2,56,1024]{2,1,0:T(8,128)(2,1)S(1)} %get-tuple-element.33), channel_id=1, source_target_pairs={{0,2},{1,3},{2,0},{3,1},{4,6},{5,7},{6,4},{7,5},{8,10},{9,11},{10,... | collective-permute-start | bytes 688136 | tf_op jit(solution)/shard_map/ppermute | solution.py:25
  7.1 0.1 collective-permute-start.2
  7.2 4.1 %collective-permute-start.3 = (bf16[2,56,512]{2,1,0:T(8,128)(2,1)S(1)}, bf16[2,56,512]{2,1,0:T(8,128)(2,1)S(1)}, u32[]{:S(2)}, u32[]{:S(2)}) collective-permute-start(bf16[2,56,512]{2,1,0:T(8,128)(2,1)S(1)} %get-tuple-element.35), channel_id=1, source_target_pairs={{0,12},{4,8},{8,4},{12,0},{1,13},{5,9},{9,5},{13,1},{2,14},{6,10},... | collective-permute-start | bytes 344072 | tf_op jit(solution)/shard_map/ppermute | solution.py:25
  11.3 0.6 %collective-permute-start.5 = (bf16[2,56,512]{2,1,0:T(8,128)(2,1)S(1)}, bf16[2,56,512]{2,1,0:T(8,128)(2,1)S(1)}, u32[]{:S(2)}, u32[]{:S(2)}) collective-permute-start(bf16[2,56,512]{2,1,0:T(8,128)(2,1)S(1)} %get-tuple-element.37), channel_id=1, source_target_pairs={{0,4},{4,0},{8,12},{12,8},{1,5},{5,1},{9,13},{13,9},{2,6},{6,2},{1... | collective-permute-start | bytes 344072 | tf_op jit(solution)/shard_map/ppermute | solution.py:25
  11.8 1.7 %collective-permute-done.1.refs_2_.refs_0_ = bf16[2,56,1024]{2,1,0:T(8,128)(2,1)S(1)} collective-permute-done((bf16[2,56,1024]{2,1,0:T(8,128)(2,1)S(1)}, bf16[2,56,1024]{2,1,0:T(8,128)(2,1)S(1)}, u32[]{:S(2)}, u32[]{:S(2)}) %collective-permute-start.1) | collective-permute-done | bytes 229408 | tf_op jit(solution)/shard_map/ppermute | solution.py:25
  13.6 4.2 %collective-permute-start.9 = (bf16[2,56,256]{2,1,0:T(8,128)(2,1)S(1)}, bf16[2,56,256]{2,1,0:T(8,128)(2,1)S(1)}, u32[]{:S(2)}, u32[]{:S(2)}) collective-permute-start(bf16[2,56,256]{2,1,0:T(8,128)(2,1)S(1)} %get-tuple-element.41), channel_id=1, source_target_pairs={{0,12},{4,8},{8,4},{12,0},{1,13},{5,9},{9,5},{13,1},{2,14},{6,10},... | collective-permute-start | bytes 172040 | tf_op jit(solution)/shard_map/ppermute | solution.py:25
  17.8 0.2 collective-permute-done.2.refs_3_.refs_0_.refs_2_
  18.0 2.8 %collective-permute-start.10 = (bf16[2,56,256]{2,1,0:T(8,128)(2,1)S(1)}, bf16[2,56,256]{2,1,0:T(8,128)(2,1)S(1)}, u32[]{:S(2)}, u32[]{:S(2)}) collective-permute-start(bf16[2,56,256]{2,1,0:T(8,128)(2,1)S(1)} %get-tuple-element.42), channel_id=1, source_target_pairs={{0,8},{4,12},{8,0},{12,4},{1,9},{5,13},{9,1},{13,5},{2,10},{6,14},... | collective-permute-start | bytes 172040 | tf_op jit(solution)/shard_map/ppermute | solution.py:25
  20.8 0.0 collective-permute-done.3.refs_3_
  20.8 1.6 %collective-permute-start.11 = (bf16[2,56,256]{2,1,0:T(8,128)(2,1)S(1)}, bf16[2,56,256]{2,1,0:T(8,128)(2,1)S(1)}, u32[]{:S(2)}, u32[]{:S(2)}) collective-permute-start(bf16[2,56,256]{2,1,0:T(8,128)(2,1)S(1)} %get-tuple-element.43), channel_id=1, source_target_pairs={{0,4},{4,0},{8,12},{12,8},{1,5},{5,1},{9,13},{13,9},{2,6},{6,2},{1... | collective-permute-start | bytes 172040 | tf_op jit(solution)/shard_map/ppermute | solution.py:25
  22.5 1.1 %collective-permute-done.4.refs_4_ = bf16[2,56,512]{2,1,0:T(8,128)(2,1)S(1)} collective-permute-done((bf16[2,56,512]{2,1,0:T(8,128)(2,1)S(1)}, bf16[2,56,512]{2,1,0:T(8,128)(2,1)S(1)}, u32[]{:S(2)}, u32[]{:S(2)}) %collective-permute-start.4) | collective-permute-done | bytes 114720 | tf_op jit(solution)/shard_map/ppermute | solution.py:25
  23.6 2.3 %collective-permute-start.6 = (bf16[2,56,256]{2,1,0:T(8,128)(2,1)S(1)}, bf16[2,56,256]{2,1,0:T(8,128)(2,1)S(1)}, u32[]{:S(2)}, u32[]{:S(2)}) collective-permute-start(bf16[2,56,256]{2,1,0:T(8,128)(2,1)S(1)} %get-tuple-element.38), channel_id=1, source_target_pairs={{0,12},{4,8},{8,4},{12,0},{1,13},{5,9},{9,5},{13,1},{2,14},{6,10},... | collective-permute-start | bytes 172040 | tf_op jit(solution)/shard_map/ppermute | solution.py:25
  26.0 0.0 collective-permute-start.7
  26.0 2.0 %collective-permute-start.8 = (bf16[2,56,256]{2,1,0:T(8,128)(2,1)S(1)}, bf16[2,56,256]{2,1,0:T(8,128)(2,1)S(1)}, u32[]{:S(2)}, u32[]{:S(2)}) collective-permute-start(bf16[2,56,256]{2,1,0:T(8,128)(2,1)S(1)} %get-tuple-element.40), channel_id=1, source_target_pairs={{0,4},{4,0},{8,12},{12,8},{1,5},{5,1},{9,13},{13,9},{2,6},{6,2},{1... | collective-permute-start | bytes 172040 | tf_op jit(solution)/shard_map/ppermute | solution.py:25
  28.0 0.7 %shard_map.33 = (f32[4,56,128]{2,1,0:T(8,128)S(1)}, f32[4,56,128]{2,1,0:T(8,128)S(1)}, f32[4,56,128]{2,1,0:T(8,128)S(1)}, f32[4,56,128]{2,1,0:T(8,128)S(1)}) custom-call(bf16[56,2048]{1,0:T(8,128)(2,1)S(1)} %get-tuple-element.30.refs_0_, bf16[2,56,2048]{2,1,0:T(8,128)(2,1)S(1)} %collective-permute-done.refs_2_.refs_1_, ...), custom_call_target="tpu_custom_call" | custom-call | flops 1 | bytes 1 | tf_op jit(solution)/shard_map/pallas_call | solution.py:99
  28.8 0.9 %collective-permute-done.6.refs_6_ = bf16[2,56,256]{2,1,0:T(8,128)(2,1)S(1)} collective-permute-done((bf16[2,56,256]{2,1,0:T(8,128)(2,1)S(1)}, bf16[2,56,256]{2,1,0:T(8,128)(2,1)S(1)}, u32[]{:S(2)}, u32[]{:S(2)}) %collective-permute-start.6) | collective-permute-done | bytes 57376 | tf_op jit(solution)/shard_map/ppermute | solution.py:25
  29.6 1.5 %collective-permute-done.7.refs_7_ = bf16[2,56,256]{2,1,0:T(8,128)(2,1)S(1)} collective-permute-done((bf16[2,56,256]{2,1,0:T(8,128)(2,1)S(1)}, bf16[2,56,256]{2,1,0:T(8,128)(2,1)S(1)}, u32[]{:S(2)}, u32[]{:S(2)}) %collective-permute-start.7) | collective-permute-done | bytes 57376 | tf_op jit(solution)/shard_map/ppermute | solution.py:25
  31.1 0.9 %shard_map.34 = (f32[8,56,128]{2,1,0:T(8,128)S(1)}, f32[7,56,128]{2,1,0:T(8,128)S(1)}, f32[7,56,128]{2,1,0:T(8,128)S(1)}, f32[7,56,128]{2,1,0:T(8,128)S(1)}) custom-call(bf16[56,2048]{1,0:T(8,128)(2,1)S(1)} %get-tuple-element.30.refs_0_, bf16[2,56,2048]{2,1,0:T(8,128)(2,1)S(1)} %collective-permute-done.refs_2_.refs_1_, ...), custom_call_target="tpu_custom_call" | custom-call | flops 1 | bytes 1 | tf_op jit(solution)/shard_map/pallas_call | solution.py:99
  32.0 2.3 %collective-permute-start.14 = (f16[7,56,128]{2,1,0:T(8,128)(2,1)S(1)}, f16[7,56,128]{2,1,0:T(8,128)(2,1)S(1)}, u32[]{:S(2)}, u32[]{:S(2)}) collective-permute-start(f16[7,56,128]{2,1,0:T(8,128)(2,1)S(1)} %convert_element_type.20), channel_id=1, source_target_pairs={{0,12},{4,8},{8,4},{12,0},{1,13},{5,9},{9,5},{13,1},{2,14},{6,10},... | collective-permute-start | bytes 301064 | tf_op jit(solution)/shard_map/ppermute | solution.py:25
  34.3 0.3 collective-permute-start.12
  34.7 1.8 %collective-permute-start.13 = (f16[7,56,128]{2,1,0:T(8,128)(2,1)S(1)}, f16[7,56,128]{2,1,0:T(8,128)(2,1)S(1)}, u32[]{:S(2)}, u32[]{:S(2)}) collective-permute-start(f16[7,56,128]{2,1,0:T(8,128)(2,1)S(1)} %convert_element_type.18), channel_id=1, source_target_pairs={{0,4},{4,0},{8,12},{12,8},{1,5},{5,1},{9,13},{13,9},{2,6},{6,2},{1... | collective-permute-start | bytes 301064 | tf_op jit(solution)/shard_map/ppermute | solution.py:25
  36.5 0.8 %shard_map.30.refs_0_ = f32[32,56,128]{2,1,0:T(8,128)S(1)} custom-call(bf16[56,2048]{1,0:T(8,128)(2,1)S(1)} %get-tuple-element.30.refs_0_, bf16[2,56,2048]{2,1,0:T(8,128)(2,1)S(1)} %collective-permute-done.refs_2_.refs_1_, bf16[2,56,1024]{2,1,0:T(8,128)(2,1)S(1)} %collective-permute-done.1.refs_2_.refs_0_, ...), custom_call_target="tpu_custom_call" | custom-call | flops 1 | bytes 4194304 | tf_op jit(solution)/shard_map/pallas_call | solution.py:99
  37.3 1.4 %collective-permute-done.14 = f16[7,56,128]{2,1,0:T(8,128)(2,1)S(1)} collective-permute-done((f16[7,56,128]{2,1,0:T(8,128)(2,1)S(1)}, f16[7,56,128]{2,1,0:T(8,128)(2,1)S(1)}, u32[]{:S(2)}, u32[]{:S(2)}) %collective-permute-start.14) | collective-permute-done | bytes 100384 | tf_op jit(solution)/shard_map/ppermute | solution.py:25
  38.7 1.1 %shard_map.35.refs_3_ = f32[32,56,168]{2,1,0:T(8,128)} custom-call(f32[32,56,128]{2,1,0:T(8,128)S(1)} %shard_map.30.refs_0_, f32[8,56,128]{2,1,0:T(8,128)S(1)} %get-tuple-element.53.refs_1_, f32[7,56,128]{2,1,0:T(8,128)S(1)} %convert_element_type.23.refs_2_), custom_call_target="tpu_custom_call" | custom-call | flops 1 | bytes 4194304 | tf_op jit(solution)/shard_map/pallas_call | solution.py:99
  39.7 1.3 %collective-permute-done.12 = f16[7,56,128]{2,1,0:T(8,128)(2,1)S(1)} collective-permute-done((f16[7,56,128]{2,1,0:T(8,128)(2,1)S(1)}, f16[7,56,128]{2,1,0:T(8,128)(2,1)S(1)}, u32[]{:S(2)}, u32[]{:S(2)}) %collective-permute-start.12) | collective-permute-done | bytes 100384 | tf_op jit(solution)/shard_map/ppermute | solution.py:25
  41.1 1.2 %shard_map.36 = f32[32,56,168]{2,1,0:T(8,128)} custom-call(f32[32,56,128]{2,1,0:T(8,128)S(1)} %shard_map.30.refs_0_, f32[7,56,128]{2,1,0:T(8,128)S(1)} %convert_element_type.21.refs_1_, f32[7,56,128]{2,1,0:T(8,128)S(1)} %convert_element_type.22.refs_2_, f32[32,56,168]{2,1,0:T(8,128)} %shard_map.35.refs_3_), custom_call_target="tpu_custom_call", output_to_operand_aliasing={{}: (3, {})} | custom-call | flops 1 | bytes 4194304 | tf_op jit(solution)/shard_map/pallas_call | solution.py:99
  (16 shorter events, 0.2 us)
Async XLA Ops:
  0.8 1.2 %copy-start = (bf16[56,8192]{1,0:T(8,128)(2,1)S(1)}, bf16[56,8192]{1,0:T(8,128)(2,1)}, u32[]{:S(2)}) copy-start(bf16[56,8192]{1,0:T(8,128)(2,1)} %refs_0_.1) | copy-start | bytes 2752516
  2.2 2.0 %collective-permute-start = (bf16[2,56,2048]{2,1,0:T(8,128)(2,1)S(1)}, bf16[2,56,2048]{2,1,0:T(8,128)(2,1)S(1)}, u32[]{:S(2)}, u32[]{:S(2)}) collective-permute-start(bf16[2,56,2048]{2,1,0:T(8,128)(2,1)S(1)} %get-tuple-element.31), channel_id=1, source_target_pairs={{0,1},{1,0},{2,3},{3,2},{4,5},{5,4},{6,7},{7,6},{8,9},{9,8},{10,11... | collective-permute-start | bytes 1376264 | tf_op jit(solution)/shard_map/ppermute | solution.py:25
  4.2 9.3 %collective-permute-start.1 = (bf16[2,56,1024]{2,1,0:T(8,128)(2,1)S(1)}, bf16[2,56,1024]{2,1,0:T(8,128)(2,1)S(1)}, u32[]{:S(2)}, u32[]{:S(2)}) collective-permute-start(bf16[2,56,1024]{2,1,0:T(8,128)(2,1)S(1)} %get-tuple-element.33), channel_id=1, source_target_pairs={{0,2},{1,3},{2,0},{3,1},{4,6},{5,7},{6,4},{7,5},{8,10},{9,11},{10,... | collective-permute-start | bytes 688136 | tf_op jit(solution)/shard_map/ppermute | solution.py:25
  7.1 10.8 %collective-permute-start.2 = (bf16[2,56,1024]{2,1,0:T(8,128)(2,1)S(1)}, bf16[2,56,1024]{2,1,0:T(8,128)(2,1)S(1)}, u32[]{:S(2)}, u32[]{:S(2)}) collective-permute-start(bf16[2,56,1024]{2,1,0:T(8,128)(2,1)S(1)} %get-tuple-element.34), channel_id=1, source_target_pairs={{0,2},{1,3},{2,0},{3,1},{4,6},{5,7},{6,4},{7,5},{8,10},{9,11},{10,... | collective-permute-start | bytes 688136 | tf_op jit(solution)/shard_map/ppermute | solution.py:25
  7.2 13.6 %collective-permute-start.3 = (bf16[2,56,512]{2,1,0:T(8,128)(2,1)S(1)}, bf16[2,56,512]{2,1,0:T(8,128)(2,1)S(1)}, u32[]{:S(2)}, u32[]{:S(2)}) collective-permute-start(bf16[2,56,512]{2,1,0:T(8,128)(2,1)S(1)} %get-tuple-element.35), channel_id=1, source_target_pairs={{0,12},{4,8},{8,4},{12,0},{1,13},{5,9},{9,5},{13,1},{2,14},{6,10},... | collective-permute-start | bytes 344072 | tf_op jit(solution)/shard_map/ppermute | solution.py:25
  11.3 12.3 %collective-permute-start.4 = (bf16[2,56,512]{2,1,0:T(8,128)(2,1)S(1)}, bf16[2,56,512]{2,1,0:T(8,128)(2,1)S(1)}, u32[]{:S(2)}, u32[]{:S(2)}) collective-permute-start(bf16[2,56,512]{2,1,0:T(8,128)(2,1)S(1)} %get-tuple-element.36), channel_id=1, source_target_pairs={{0,8},{4,12},{8,0},{12,4},{1,9},{5,13},{9,1},{13,5},{2,10},{6,14},... | collective-permute-start | bytes 344072 | tf_op jit(solution)/shard_map/ppermute | solution.py:25
  11.3 14.7 %collective-permute-start.5 = (bf16[2,56,512]{2,1,0:T(8,128)(2,1)S(1)}, bf16[2,56,512]{2,1,0:T(8,128)(2,1)S(1)}, u32[]{:S(2)}, u32[]{:S(2)}) collective-permute-start(bf16[2,56,512]{2,1,0:T(8,128)(2,1)S(1)} %get-tuple-element.37), channel_id=1, source_target_pairs={{0,4},{4,0},{8,12},{12,8},{1,5},{5,1},{9,13},{13,9},{2,6},{6,2},{1... | collective-permute-start | bytes 344072 | tf_op jit(solution)/shard_map/ppermute | solution.py:25
  13.6 12.4 %collective-permute-start.9 = (bf16[2,56,256]{2,1,0:T(8,128)(2,1)S(1)}, bf16[2,56,256]{2,1,0:T(8,128)(2,1)S(1)}, u32[]{:S(2)}, u32[]{:S(2)}) collective-permute-start(bf16[2,56,256]{2,1,0:T(8,128)(2,1)S(1)} %get-tuple-element.41), channel_id=1, source_target_pairs={{0,12},{4,8},{8,4},{12,0},{1,13},{5,9},{9,5},{13,1},{2,14},{6,10},... | collective-permute-start | bytes 172040 | tf_op jit(solution)/shard_map/ppermute | solution.py:25
  18.0 10.1 %collective-permute-start.10 = (bf16[2,56,256]{2,1,0:T(8,128)(2,1)S(1)}, bf16[2,56,256]{2,1,0:T(8,128)(2,1)S(1)}, u32[]{:S(2)}, u32[]{:S(2)}) collective-permute-start(bf16[2,56,256]{2,1,0:T(8,128)(2,1)S(1)} %get-tuple-element.42), channel_id=1, source_target_pairs={{0,8},{4,12},{8,0},{12,4},{1,9},{5,13},{9,1},{13,5},{2,10},{6,14},... | collective-permute-start | bytes 172040 | tf_op jit(solution)/shard_map/ppermute | solution.py:25
  20.8 7.2 %collective-permute-start.11 = (bf16[2,56,256]{2,1,0:T(8,128)(2,1)S(1)}, bf16[2,56,256]{2,1,0:T(8,128)(2,1)S(1)}, u32[]{:S(2)}, u32[]{:S(2)}) collective-permute-start(bf16[2,56,256]{2,1,0:T(8,128)(2,1)S(1)} %get-tuple-element.43), channel_id=1, source_target_pairs={{0,4},{4,0},{8,12},{12,8},{1,5},{5,1},{9,13},{13,9},{2,6},{6,2},{1... | collective-permute-start | bytes 172040 | tf_op jit(solution)/shard_map/ppermute | solution.py:25
  23.6 6.0 %collective-permute-start.6 = (bf16[2,56,256]{2,1,0:T(8,128)(2,1)S(1)}, bf16[2,56,256]{2,1,0:T(8,128)(2,1)S(1)}, u32[]{:S(2)}, u32[]{:S(2)}) collective-permute-start(bf16[2,56,256]{2,1,0:T(8,128)(2,1)S(1)} %get-tuple-element.38), channel_id=1, source_target_pairs={{0,12},{4,8},{8,4},{12,0},{1,13},{5,9},{9,5},{13,1},{2,14},{6,10},... | collective-permute-start | bytes 172040 | tf_op jit(solution)/shard_map/ppermute | solution.py:25
  26.0 5.1 %collective-permute-start.7 = (bf16[2,56,256]{2,1,0:T(8,128)(2,1)S(1)}, bf16[2,56,256]{2,1,0:T(8,128)(2,1)S(1)}, u32[]{:S(2)}, u32[]{:S(2)}) collective-permute-start(bf16[2,56,256]{2,1,0:T(8,128)(2,1)S(1)} %get-tuple-element.39), channel_id=1, source_target_pairs={{0,8},{4,12},{8,0},{12,4},{1,9},{5,13},{9,1},{13,5},{2,10},{6,14},... | collective-permute-start | bytes 172040 | tf_op jit(solution)/shard_map/ppermute | solution.py:25
  26.0 5.1 %collective-permute-start.8 = (bf16[2,56,256]{2,1,0:T(8,128)(2,1)S(1)}, bf16[2,56,256]{2,1,0:T(8,128)(2,1)S(1)}, u32[]{:S(2)}, u32[]{:S(2)}) collective-permute-start(bf16[2,56,256]{2,1,0:T(8,128)(2,1)S(1)} %get-tuple-element.40), channel_id=1, source_target_pairs={{0,4},{4,0},{8,12},{12,8},{1,5},{5,1},{9,13},{13,9},{2,6},{6,2},{1... | collective-permute-start | bytes 172040 | tf_op jit(solution)/shard_map/ppermute | solution.py:25
  32.0 6.6 %collective-permute-start.14 = (f16[7,56,128]{2,1,0:T(8,128)(2,1)S(1)}, f16[7,56,128]{2,1,0:T(8,128)(2,1)S(1)}, u32[]{:S(2)}, u32[]{:S(2)}) collective-permute-start(f16[7,56,128]{2,1,0:T(8,128)(2,1)S(1)} %convert_element_type.20), channel_id=1, source_target_pairs={{0,12},{4,8},{8,4},{12,0},{1,13},{5,9},{9,5},{13,1},{2,14},{6,10},... | collective-permute-start | bytes 301064 | tf_op jit(solution)/shard_map/ppermute | solution.py:25
  34.3 6.7 %collective-permute-start.12 = (f16[7,56,128]{2,1,0:T(8,128)(2,1)S(1)}, f16[7,56,128]{2,1,0:T(8,128)(2,1)S(1)}, u32[]{:S(2)}, u32[]{:S(2)}) collective-permute-start(f16[7,56,128]{2,1,0:T(8,128)(2,1)S(1)} %convert_element_type.19), channel_id=1, source_target_pairs={{0,8},{4,12},{8,0},{12,4},{1,9},{5,13},{9,1},{13,5},{2,10},{6,14},... | collective-permute-start | bytes 301064 | tf_op jit(solution)/shard_map/ppermute | solution.py:25
  34.7 6.4 %collective-permute-start.13 = (f16[7,56,128]{2,1,0:T(8,128)(2,1)S(1)}, f16[7,56,128]{2,1,0:T(8,128)(2,1)S(1)}, u32[]{:S(2)}, u32[]{:S(2)}) collective-permute-start(f16[7,56,128]{2,1,0:T(8,128)(2,1)S(1)} %convert_element_type.18), channel_id=1, source_target_pairs={{0,4},{4,0},{8,12},{12,8},{1,5},{5,1},{9,13},{13,9},{2,6},{6,2},{1... | collective-permute-start | bytes 301064 | tf_op jit(solution)/shard_map/ppermute | solution.py:25

commit v5 on v4

--- a/solution.py
+++ b/solution.py
@@ -11,6 +11,7 @@
 CYCLE_CAP = 64
 LANES = 128
 PIECE = 16
+NEAR, FAR = (3, 2, 1), (2, 3, 1)
 VMEM_LIMIT = 48 * 2**20
 OWN_COST, PLACE_COST = 4 << 20, 4 << 20
 
@@ -103,28 +104,29 @@
     return pl.ds(pl.multiple_of(start, LANES), width)
 
 
-def pack_kernel(loop, groups, per, frames, live, mine, over, core):
+def owned_kernel(pairs, frames, labels, *outs):
     p = lax.axis_index("pix")
-    for k, out in ((1, core.at[0]), (3, core.at[1]), (0, mine), (2, over)):
-        for n in range(loop * per):
-            index = (p ^ k) * loop * per + n
-            mask = live[pl.ds(index, 1), :].astype(jnp.bfloat16)
-            out[:, n * LANES : (n + 1) * LANES] = frames[:, lanes_at(index * LANES, LANES)] * mask
-
-
-def near_kernel(loop, per, parts, mine, over, core, *outs):
+    for k, out in zip((0, 2), outs):
+        for n in range(pairs):
+            index = (p ^ k) * pairs + n
+            live = jnp.where(labels[pl.ds(index, 1), :] >= 0, 1.0, 0.0).astype(jnp.bfloat16)
+            out[:, n * LANES : (n + 1) * LANES] = frames[:, lanes_at(index * LANES, LANES)] * live
+
+
+def near_kernel(loop, per, parts, mine, over, frames, labels, core, *outs):
+    to_chip, (*to_time, core_over) = outs[: len(parts)], outs[len(parts) :]
     t = lax.axis_index("tm")
-    to_chip, to_time = outs[: len(parts)], outs[len(parts) :]
-    for j, out in enumerate(to_time, 1):
-        lanes = lanes_at((t ^ j) * per * LANES, per * LANES)
-        out[0] = mine[:, lanes]
-        out[1] = core[0, :, lanes]
+    owned_kernel(loop * per, frames, labels, core, core_over)
     for (start, count), out in zip(parts, to_chip):
         for c in range(loop):
             source = slice((c * per + start) * LANES, (c * per + start + count) * LANES)
             target = slice(c * count * LANES, (c + 1) * count * LANES)
             out[0, :, target] = over[:, source]
-            out[1, :, target] = core[1, :, source]
+            out[1, :, target] = core_over[:, source]
+    for j, out in enumerate(to_time, 1):
+        lanes = lanes_at((t ^ j) * per * LANES, per * LANES)
+        out[0] = mine[:, lanes]
+        out[1] = core[:, lanes]
 
 
 def far_kernel(count, chip, *outs):
@@ -168,9 +170,13 @@
     return lax.broadcasted_iota(jnp.int32, (rows, LANES), 1)
 
 
+def ordered(refs, order):
+    return [refs[order.index(j)] for j in range(1, len(order) + 1)]
+
+
 def cross_kernel(loop, per, part, rows, last, mine, core, chip, *refs):
     start, count = part
-    near, far = refs[: loop - 1][::-1], refs[loop - 1 : 2 * loop - 2][::-1]
+    near, far = ordered(refs[: loop - 1], NEAR), ordered(refs[loop - 1 : 2 * loop - 2], FAR)
     early, outs, blocks = refs[2 * loop - 2 : -1 - loop], refs[-1 - loop : -1], refs[-1]
     t = lax.axis_index("tm")
     lane = lane_of(rows)
@@ -181,7 +187,7 @@
         at_chip = lanes_at((t * count + s) * LANES, LANES)
         for j in range(loop):
             if j == 0:
-                values = mine[:, at], core[0, :, at], chip[0, :, at_chip], chip[1, :, at_chip]
+                values = mine[:, at], core[:, at], chip[0, :, at_chip], chip[1, :, at_chip]
             else:
                 values = [near[j - 1][k, :, at_near] for k in range(2)] + [far[j - 1][k, :, at_far] for k in range(2)]
             for k, value in enumerate(values):
@@ -219,7 +225,7 @@
                 n = c * per + start + s
                 at = slice(n * LANES, (n + 1) * LANES)
                 at_chip = slice((c * count + s) * LANES, (c * count + s + 1) * LANES)
-                values = mine[:, at], core[0, :, at], chip[0, :, at_chip], chip[1, :, at_chip]
+                values = mine[:, at], core[:, at], chip[0, :, at_chip], chip[1, :, at_chip]
                 block = jnp.concatenate([padded(value) for value in values], axis=1)
                 left = halves(block).astype(jnp.bfloat16)
                 block = block.astype(jnp.bfloat16)
@@ -266,18 +272,20 @@
     def tiles(count):
         return shape(count, rows, LANES, dtype=f32)
 
-    mine, over, core = local_call(
-        functools.partial(pack_kernel, loop, groups, per),
-        [shape(rows, loop * per * LANES)] * 2 + [shape(2, rows, loop * per * LANES)],
-        2,
-    )(frames, jnp.where(labels >= 0, 1.0, 0.0).astype(f32).reshape(-1, LANES))
-    core = swap(core, "pix", 1)
-    ready = local_call(
+    span = loop * per * LANES
+    rows_of_labels = labels.reshape(-1, LANES)
+    other = swap(frames, "pix", 1), swap(rows_of_labels, "pix", 1)
+    mine, over = local_call(
+        functools.partial(owned_kernel, loop * per), [shape(rows, span)] * 2, 2
+    )(frames, rows_of_labels)
+    core, *ready = local_call(
         functools.partial(near_kernel, loop, per, parts),
-        [shape(2, rows, loop * count * LANES) for _, count in parts]
+        [shape(rows, span)]
+        + [shape(2, rows, loop * count * LANES) for _, count in parts]
         + [shape(2, rows, per * LANES)] * (loop - 1),
-        3,
-    )(mine, over, core)
+        4,
+        [pltpu.VMEM((rows, span), bf16)],
+    )(mine, over, *other)
     chips = [swap(part, "pix", 2) for part in ready[: len(parts)]]
     near = [swap(part, "tm", j) for j, part in enumerate(ready[len(parts) :], 1)]
     early = []
@@ -292,7 +300,7 @@
             [tiles(cycles)] + [tiles(cycles - 1)] * (loop - 1) if last else [tiles(2 * part[1])] * loop,
             2 * loop + 1 + (len(early) if last else 0),
             [pltpu.VMEM((part[1], loop, rows + 8, groups * LANES), bf16)],
-        )(mine, core, chip, *near[::-1], *far[::-1], *(early if last else ()))
+        )(mine, core, chip, *[near[j - 1] for j in NEAR], *[far[j - 1] for j in FAR], *(early if last else ()))
     kept, *sent = early[-loop:]
     own_tiles = local_call(
         functools.partial(own_kernel, loop, per, parts, rows),

time: 42.5 us -> 41 us (0.965)
  starting transfers between devices: 25.7 us -> 23.2 us
  waiting for transfers between devices: 9.44 us -> 10.4 us
  other arithmetic: 0.86 us -> 0.1 us
  local copies, waits for them, and re-layouts: 1.18 us -> 1.94 us
    ppermute x15 -> x16, starting transfers between devices: 25.7 us -> 23.2 us  [swap(): return lax.ppermute(shard, axis, [(i, i ^ by) for i in range(size)])]
    ppermute x15 -> x16, waiting for transfers between devices: 9.44 us -> 10.4 us  [swap(): return lax.ppermute(shard, axis, [(i, i ^ by) for i in range(size)])]
    reshape x1 -> x0, other arithmetic: 0.76 us -> none  [spread(): jnp.where(labels >= 0, 1.0, 0.0).astype(f32).reshape(-1, LANES)]
    unnamed x2 -> x4, local copies, waits for them, and re-layouts: 1.18 us -> 1.94 us
  transfers between devices with their start and end apart: 15 -> 16, of which waited for: 8 -> 9; matrix products, arithmetic and copies ran while one was open for 0% -> 0% of each run, Pallas kernels for 6% -> 7%
where the time goes in v5:
time: 41 us; the launch traced here: 40.8 us
  starting transfers between devices  23.2 us (57%)
  waiting for transfers between devices  10.4 us (25%)
  Pallas kernels  5.01 us (12%)
  local copies, waits for them, and re-layouts  1.94 us (5%)
    ppermute x16, starting transfers between devices, swap(): return lax.ppermute(shard, axis, [(i, i ^ by) for i in range(size)])  23.2 us
    ppermute x16, waiting for transfers between devices, swap(): return lax.ppermute(shard, axis, [(i, i ^ by) for i in range(size)])  10.4 us
    pallas_call x9, Pallas kernels, local_call(): return lambda *operands: call(*operands, *after)  5.01 us
    unnamed x4, local copies, waits for them, and re-layouts  1.94 us
  transfers between devices with their start and end apart: 16, of which 9 were waited for; matrix products, arithmetic and copies ran while one was open for 0% of the time, Pallas kernels for 7%

profile of v5, /device:TPU:0, one launch (start us, length us, event | category | flops | bytes accessed | tf_op | source)
XLA Modules:
  0.0 40.8 jit_solution(924835812700134163)
XLA Ops:
  0.0 0.5 %collective-permute-start = (bf16[56,8192]{1,0:T(8,128)(2,1)}, bf16[56,8192]{1,0:T(8,128)(2,1)S(1)}, u32[]{:S(2)}, u32[]{:S(2)}) collective-permute-start(bf16[56,8192]{1,0:T(8,128)(2,1)} %refs_0_.1), channel_id=1, source_target_pairs={{0,1},{1,0},{2,3},{3,2},{4,5},{5,4},{6,7},{7,6},{8,9},{9,8},{10,11... | collective-permute-start | bytes 2752520 | tf_op jit(solution)/shard_map/ppermute | solution.py:26
  0.5 0.1 collective-permute-start.1
  0.5 1.2 %copy-done = bf16[56,8192]{1,0:T(8,128)(2,1)S(1)} copy-done((bf16[56,8192]{1,0:T(8,128)(2,1)S(1)}, bf16[56,8192]{1,0:T(8,128)(2,1)}, u32[]{:S(2)}) %copy-start) | copy-done | bytes 917528
  1.7 0.8 %copy-done.1 = s32[8192]{0:T(1024)S(1)} copy-done((s32[8192]{0:T(1024)S(1)}, s32[8192]{0:T(1024)}, u32[]{:S(2)}) %copy-start.1) | copy-done | bytes 32792
  2.4 0.1 shard_map.28
  2.6 0.2 collective-permute-done.1.refs_3_
  2.8 0.2 shard_map.29
  3.0 2.9 %collective-permute-start.2 = (bf16[2,56,1024]{2,1,0:T(8,128)(2,1)S(1)}, bf16[2,56,1024]{2,1,0:T(8,128)(2,1)S(1)}, u32[]{:S(2)}, u32[]{:S(2)}) collective-permute-start(bf16[2,56,1024]{2,1,0:T(8,128)(2,1)S(1)} %get-tuple-element.33), channel_id=1, source_target_pairs={{0,2},{1,3},{2,0},{3,1},{4,6},{5,7},{6,4},{7,5},{8,10},{9,11},{10,... | collective-permute-start | bytes 688136 | tf_op jit(solution)/shard_map/ppermute | solution.py:26
  5.9 0.1 collective-permute-start.3
  6.0 4.1 %collective-permute-start.4 = (bf16[2,56,512]{2,1,0:T(8,128)(2,1)S(1)}, bf16[2,56,512]{2,1,0:T(8,128)(2,1)S(1)}, u32[]{:S(2)}, u32[]{:S(2)}) collective-permute-start(bf16[2,56,512]{2,1,0:T(8,128)(2,1)S(1)} %get-tuple-element.35), channel_id=1, source_target_pairs={{0,12},{4,8},{8,4},{12,0},{1,13},{5,9},{9,5},{13,1},{2,14},{6,10},... | collective-permute-start | bytes 344072 | tf_op jit(solution)/shard_map/ppermute | solution.py:26
  10.1 0.6 %collective-permute-start.6 = (bf16[2,56,512]{2,1,0:T(8,128)(2,1)S(1)}, bf16[2,56,512]{2,1,0:T(8,128)(2,1)S(1)}, u32[]{:S(2)}, u32[]{:S(2)}) collective-permute-start(bf16[2,56,512]{2,1,0:T(8,128)(2,1)S(1)} %get-tuple-element.37), channel_id=1, source_target_pairs={{0,4},{4,0},{8,12},{12,8},{1,5},{5,1},{9,13},{13,9},{2,6},{6,2},{1... | collective-permute-start | bytes 344072 | tf_op jit(solution)/shard_map/ppermute | solution.py:26
  10.6 1.7 %collective-permute-done.2.refs_2_.refs_0_ = bf16[2,56,1024]{2,1,0:T(8,128)(2,1)S(1)} collective-permute-done((bf16[2,56,1024]{2,1,0:T(8,128)(2,1)S(1)}, bf16[2,56,1024]{2,1,0:T(8,128)(2,1)S(1)}, u32[]{:S(2)}, u32[]{:S(2)}) %collective-permute-start.2) | collective-permute-done | bytes 229408 | tf_op jit(solution)/shard_map/ppermute | solution.py:26
  12.4 3.2 %collective-permute-start.10 = (bf16[2,56,256]{2,1,0:T(8,128)(2,1)S(1)}, bf16[2,56,256]{2,1,0:T(8,128)(2,1)S(1)}, u32[]{:S(2)}, u32[]{:S(2)}) collective-permute-start(bf16[2,56,256]{2,1,0:T(8,128)(2,1)S(1)} %get-tuple-element.41), channel_id=1, source_target_pairs={{0,8},{4,12},{8,0},{12,4},{1,9},{5,13},{9,1},{13,5},{2,10},{6,14},... | collective-permute-start | bytes 172040 | tf_op jit(solution)/shard_map/ppermute | solution.py:26
  15.6 1.2 %collective-permute-done.3.refs_3_.refs_0_.refs_2_ = bf16[2,56,1024]{2,1,0:T(8,128)(2,1)S(1)} collective-permute-done((bf16[2,56,1024]{2,1,0:T(8,128)(2,1)S(1)}, bf16[2,56,1024]{2,1,0:T(8,128)(2,1)S(1)}, u32[]{:S(2)}, u32[]{:S(2)}) %collective-permute-start.3) | collective-permute-done | bytes 229408 | tf_op jit(solution)/shard_map/ppermute | solution.py:26
  16.8 3.8 %collective-permute-start.11 = (bf16[2,56,256]{2,1,0:T(8,128)(2,1)S(1)}, bf16[2,56,256]{2,1,0:T(8,128)(2,1)S(1)}, u32[]{:S(2)}, u32[]{:S(2)}) collective-permute-start(bf16[2,56,256]{2,1,0:T(8,128)(2,1)S(1)} %get-tuple-element.42), channel_id=1, source_target_pairs={{0,12},{4,8},{8,4},{12,0},{1,13},{5,9},{9,5},{13,1},{2,14},{6,10},... | collective-permute-start | bytes 172040 | tf_op jit(solution)/shard_map/ppermute | solution.py:26
  20.6 0.1 collective-permute-start.12
  20.7 2.2 %collective-permute-done.5.refs_4_ = bf16[2,56,512]{2,1,0:T(8,128)(2,1)S(1)} collective-permute-done((bf16[2,56,512]{2,1,0:T(8,128)(2,1)S(1)}, bf16[2,56,512]{2,1,0:T(8,128)(2,1)S(1)}, u32[]{:S(2)}, u32[]{:S(2)}) %collective-permute-start.5) | collective-permute-done | bytes 114720 | tf_op jit(solution)/shard_map/ppermute | solution.py:26
  23.0 2.1 %collective-permute-start.8 = (bf16[2,56,256]{2,1,0:T(8,128)(2,1)S(1)}, bf16[2,56,256]{2,1,0:T(8,128)(2,1)S(1)}, u32[]{:S(2)}, u32[]{:S(2)}) collective-permute-start(bf16[2,56,256]{2,1,0:T(8,128)(2,1)S(1)} %get-tuple-element.39), channel_id=1, source_target_pairs={{0,12},{4,8},{8,4},{12,0},{1,13},{5,9},{9,5},{13,1},{2,14},{6,10},... | collective-permute-start | bytes 172040 | tf_op jit(solution)/shard_map/ppermute | solution.py:26
  25.1 1.4 %collective-permute-start.9 = (bf16[2,56,256]{2,1,0:T(8,128)(2,1)S(1)}, bf16[2,56,256]{2,1,0:T(8,128)(2,1)S(1)}, u32[]{:S(2)}, u32[]{:S(2)}) collective-permute-start(bf16[2,56,256]{2,1,0:T(8,128)(2,1)S(1)} %get-tuple-element.40), channel_id=1, source_target_pairs={{0,4},{4,0},{8,12},{12,8},{1,5},{5,1},{9,13},{13,9},{2,6},{6,2},{1... | collective-permute-start | bytes 172040 | tf_op jit(solution)/shard_map/ppermute | solution.py:26
  26.5 0.7 %shard_map.33 = (f32[4,56,128]{2,1,0:T(8,128)S(1)}, f32[4,56,128]{2,1,0:T(8,128)S(1)}, f32[4,56,128]{2,1,0:T(8,128)S(1)}, f32[4,56,128]{2,1,0:T(8,128)S(1)}) custom-call(bf16[56,2048]{1,0:T(8,128)(2,1)S(1)} %get-tuple-element.30.refs_0_, bf16[56,2048]{1,0:T(8,128)(2,1)S(1)} %get-tuple-element.32.refs_1_, ...), custom_call_target="tpu_custom_call" | custom-call | flops 1 | bytes 1 | tf_op jit(solution)/shard_map/pallas_call | solution.py:100
  27.2 0.9 %collective-permute-done.7.refs_6_ = bf16[2,56,256]{2,1,0:T(8,128)(2,1)S(1)} collective-permute-done((bf16[2,56,256]{2,1,0:T(8,128)(2,1)S(1)}, bf16[2,56,256]{2,1,0:T(8,128)(2,1)S(1)}, u32[]{:S(2)}, u32[]{:S(2)}) %collective-permute-start.7) | collective-permute-done | bytes 57376 | tf_op jit(solution)/shard_map/ppermute | solution.py:26
  28.1 0.9 %collective-permute-done.8.refs_7_ = bf16[2,56,256]{2,1,0:T(8,128)(2,1)S(1)} collective-permute-done((bf16[2,56,256]{2,1,0:T(8,128)(2,1)S(1)}, bf16[2,56,256]{2,1,0:T(8,128)(2,1)S(1)}, u32[]{:S(2)}, u32[]{:S(2)}) %collective-permute-start.8) | collective-permute-done | bytes 57376 | tf_op jit(solution)/shard_map/ppermute | solution.py:26
  29.0 0.6 %collective-permute-done.9.refs_8_ = bf16[2,56,256]{2,1,0:T(8,128)(2,1)S(1)} collective-permute-done((bf16[2,56,256]{2,1,0:T(8,128)(2,1)S(1)}, bf16[2,56,256]{2,1,0:T(8,128)(2,1)S(1)}, u32[]{:S(2)}, u32[]{:S(2)}) %collective-permute-start.9) | collective-permute-done | bytes 57376 | tf_op jit(solution)/shard_map/ppermute | solution.py:26
  29.6 0.9 %shard_map.34 = (f32[8,56,128]{2,1,0:T(8,128)S(1)}, f32[7,56,128]{2,1,0:T(8,128)S(1)}, f32[7,56,128]{2,1,0:T(8,128)S(1)}, f32[7,56,128]{2,1,0:T(8,128)S(1)}) custom-call(bf16[56,2048]{1,0:T(8,128)(2,1)S(1)} %get-tuple-element.30.refs_0_, bf16[56,2048]{1,0:T(8,128)(2,1)S(1)} %get-tuple-element.32.refs_1_, ...), custom_call_target="tpu_custom_call" | custom-call | flops 1 | bytes 1 | tf_op jit(solution)/shard_map/pallas_call | solution.py:100
  30.5 2.3 %collective-permute-start.15 = (f16[7,56,128]{2,1,0:T(8,128)(2,1)S(1)}, f16[7,56,128]{2,1,0:T(8,128)(2,1)S(1)}, u32[]{:S(2)}, u32[]{:S(2)}) collective-permute-start(f16[7,56,128]{2,1,0:T(8,128)(2,1)S(1)} %convert_element_type.20), channel_id=1, source_target_pairs={{0,12},{4,8},{8,4},{12,0},{1,13},{5,9},{9,5},{13,1},{2,14},{6,10},... | collective-permute-start | bytes 301064 | tf_op jit(solution)/shard_map/ppermute | solution.py:26
  32.8 0.3 collective-permute-start.13
  33.1 1.9 %collective-permute-start.14 = (f16[7,56,128]{2,1,0:T(8,128)(2,1)S(1)}, f16[7,56,128]{2,1,0:T(8,128)(2,1)S(1)}, u32[]{:S(2)}, u32[]{:S(2)}) collective-permute-start(f16[7,56,128]{2,1,0:T(8,128)(2,1)S(1)} %convert_element_type.18), channel_id=1, source_target_pairs={{0,4},{4,0},{8,12},{12,8},{1,5},{5,1},{9,13},{13,9},{2,6},{6,2},{1... | collective-permute-start | bytes 301064 | tf_op jit(solution)/shard_map/ppermute | solution.py:26
  35.0 0.8 %shard_map.30.refs_0_ = f32[32,56,128]{2,1,0:T(8,128)S(1)} custom-call(bf16[56,2048]{1,0:T(8,128)(2,1)S(1)} %get-tuple-element.30.refs_0_, bf16[56,2048]{1,0:T(8,128)(2,1)S(1)} %get-tuple-element.32.refs_1_, bf16[2,56,1024]{2,1,0:T(8,128)(2,1)S(1)} %collective-permute-done.2.refs_2_.refs_0_, ...), custom_call_target="tpu_custom_call" | custom-call | flops 1 | bytes 4194304 | tf_op jit(solution)/shard_map/pallas_call | solution.py:100
  35.8 1.4 %collective-permute-done.15 = f16[7,56,128]{2,1,0:T(8,128)(2,1)S(1)} collective-permute-done((f16[7,56,128]{2,1,0:T(8,128)(2,1)S(1)}, f16[7,56,128]{2,1,0:T(8,128)(2,1)S(1)}, u32[]{:S(2)}, u32[]{:S(2)}) %collective-permute-start.15) | collective-permute-done | bytes 100384 | tf_op jit(solution)/shard_map/ppermute | solution.py:26
  37.2 1.1 %shard_map.35.refs_3_ = f32[32,56,168]{2,1,0:T(8,128)} custom-call(f32[32,56,128]{2,1,0:T(8,128)S(1)} %shard_map.30.refs_0_, f32[8,56,128]{2,1,0:T(8,128)S(1)} %get-tuple-element.53.refs_1_, f32[7,56,128]{2,1,0:T(8,128)S(1)} %convert_element_type.23.refs_2_), custom_call_target="tpu_custom_call" | custom-call | flops 1 | bytes 4194304 | tf_op jit(solution)/shard_map/pallas_call | solution.py:100
  38.2 1.3 %collective-permute-done.13 = f16[7,56,128]{2,1,0:T(8,128)(2,1)S(1)} collective-permute-done((f16[7,56,128]{2,1,0:T(8,128)(2,1)S(1)}, f16[7,56,128]{2,1,0:T(8,128)(2,1)S(1)}, u32[]{:S(2)}, u32[]{:S(2)}) %collective-permute-start.13) | collective-permute-done | bytes 100384 | tf_op jit(solution)/shard_map/ppermute | solution.py:26
  39.6 1.2 %shard_map.36 = f32[32,56,168]{2,1,0:T(8,128)} custom-call(f32[32,56,128]{2,1,0:T(8,128)S(1)} %shard_map.30.refs_0_, f32[7,56,128]{2,1,0:T(8,128)S(1)} %convert_element_type.21.refs_1_, f32[7,56,128]{2,1,0:T(8,128)S(1)} %convert_element_type.22.refs_2_, f32[32,56,168]{2,1,0:T(8,128)} %shard_map.35.refs_3_), custom_call_target="tpu_custom_call", output_to_operand_aliasing={{}: (3, {})} | custom-call | flops 1 | bytes 4194304 | tf_op jit(solution)/shard_map/pallas_call | solution.py:100
  (19 shorter events, 0.2 us)
Async XLA Ops:
  0.0 2.8 %collective-permute-start = (bf16[56,8192]{1,0:T(8,128)(2,1)}, bf16[56,8192]{1,0:T(8,128)(2,1)S(1)}, u32[]{:S(2)}, u32[]{:S(2)}) collective-permute-start(bf16[56,8192]{1,0:T(8,128)(2,1)} %refs_0_.1), channel_id=1, source_target_pairs={{0,1},{1,0},{2,3},{3,2},{4,5},{5,4},{6,7},{7,6},{8,9},{9,8},{10,11... | collective-permute-start | bytes 2752520 | tf_op jit(solution)/shard_map/ppermute | solution.py:26
  0.5 2.4 %collective-permute-start.1 = (s32[64,128]{1,0:T(8,128)}, s32[64,128]{1,0:T(8,128)S(1)}, u32[]{:S(2)}, u32[]{:S(2)}) collective-permute-start(s32[64,128]{1,0:T(8,128)} %bitcast.1), channel_id=1, source_target_pairs={{0,1},{1,0},{2,3},{3,2},{4,5},{5,4},{6,7},{7,6},{8,9},{9,8},{10,11... | collective-permute-start | bytes 98312 | tf_op jit(solution)/shard_map/ppermute | solution.py:26
  0.5 1.2 %copy-start = (bf16[56,8192]{1,0:T(8,128)(2,1)S(1)}, bf16[56,8192]{1,0:T(8,128)(2,1)}, u32[]{:S(2)}) copy-start(bf16[56,8192]{1,0:T(8,128)(2,1)} %refs_0_.1) | copy-start | bytes 2752516
  1.7 0.8 %copy-start.1 = (s32[8192]{0:T(1024)S(1)}, s32[8192]{0:T(1024)}, u32[]{:S(2)}) copy-start(s32[8192]{0:T(1024)} %param.3) | copy-start | bytes 98308
  3.0 9.3 %collective-permute-start.2 = (bf16[2,56,1024]{2,1,0:T(8,128)(2,1)S(1)}, bf16[2,56,1024]{2,1,0:T(8,128)(2,1)S(1)}, u32[]{:S(2)}, u32[]{:S(2)}) collective-permute-start(bf16[2,56,1024]{2,1,0:T(8,128)(2,1)S(1)} %get-tuple-element.33), channel_id=1, source_target_pairs={{0,2},{1,3},{2,0},{3,1},{4,6},{5,7},{6,4},{7,5},{8,10},{9,11},{10,... | collective-permute-start | bytes 688136 | tf_op jit(solution)/shard_map/ppermute | solution.py:26
  5.9 10.8 %collective-permute-start.3 = (bf16[2,56,1024]{2,1,0:T(8,128)(2,1)S(1)}, bf16[2,56,1024]{2,1,0:T(8,128)(2,1)S(1)}, u32[]{:S(2)}, u32[]{:S(2)}) collective-permute-start(bf16[2,56,1024]{2,1,0:T(8,128)(2,1)S(1)} %get-tuple-element.34), channel_id=1, source_target_pairs={{0,2},{1,3},{2,0},{3,1},{4,6},{5,7},{6,4},{7,5},{8,10},{9,11},{10,... | collective-permute-start | bytes 688136 | tf_op jit(solution)/shard_map/ppermute | solution.py:26
  6.0 14.6 %collective-permute-start.4 = (bf16[2,56,512]{2,1,0:T(8,128)(2,1)S(1)}, bf16[2,56,512]{2,1,0:T(8,128)(2,1)S(1)}, u32[]{:S(2)}, u32[]{:S(2)}) collective-permute-start(bf16[2,56,512]{2,1,0:T(8,128)(2,1)S(1)} %get-tuple-element.35), channel_id=1, source_target_pairs={{0,12},{4,8},{8,4},{12,0},{1,13},{5,9},{9,5},{13,1},{2,14},{6,10},... | collective-permute-start | bytes 344072 | tf_op jit(solution)/shard_map/ppermute | solution.py:26
  10.1 12.9 %collective-permute-start.5 = (bf16[2,56,512]{2,1,0:T(8,128)(2,1)S(1)}, bf16[2,56,512]{2,1,0:T(8,128)(2,1)S(1)}, u32[]{:S(2)}, u32[]{:S(2)}) collective-permute-start(bf16[2,56,512]{2,1,0:T(8,128)(2,1)S(1)} %get-tuple-element.36), channel_id=1, source_target_pairs={{0,8},{4,12},{8,0},{12,4},{1,9},{5,13},{9,1},{13,5},{2,10},{6,14},... | collective-permute-start | bytes 344072 | tf_op jit(solution)/shard_map/ppermute | solution.py:26
  10.1 12.9 %collective-permute-start.6 = (bf16[2,56,512]{2,1,0:T(8,128)(2,1)S(1)}, bf16[2,56,512]{2,1,0:T(8,128)(2,1)S(1)}, u32[]{:S(2)}, u32[]{:S(2)}) collective-permute-start(bf16[2,56,512]{2,1,0:T(8,128)(2,1)S(1)} %get-tuple-element.37), channel_id=1, source_target_pairs={{0,4},{4,0},{8,12},{12,8},{1,5},{5,1},{9,13},{13,9},{2,6},{6,2},{1... | collective-permute-start | bytes 344072 | tf_op jit(solution)/shard_map/ppermute | solution.py:26
  12.4 12.8 %collective-permute-start.10 = (bf16[2,56,256]{2,1,0:T(8,128)(2,1)S(1)}, bf16[2,56,256]{2,1,0:T(8,128)(2,1)S(1)}, u32[]{:S(2)}, u32[]{:S(2)}) collective-permute-start(bf16[2,56,256]{2,1,0:T(8,128)(2,1)S(1)} %get-tuple-element.41), channel_id=1, source_target_pairs={{0,8},{4,12},{8,0},{12,4},{1,9},{5,13},{9,1},{13,5},{2,10},{6,14},... | collective-permute-start | bytes 172040 | tf_op jit(solution)/shard_map/ppermute | solution.py:26
  16.8 9.7 %collective-permute-start.11 = (bf16[2,56,256]{2,1,0:T(8,128)(2,1)S(1)}, bf16[2,56,256]{2,1,0:T(8,128)(2,1)S(1)}, u32[]{:S(2)}, u32[]{:S(2)}) collective-permute-start(bf16[2,56,256]{2,1,0:T(8,128)(2,1)S(1)} %get-tuple-element.42), channel_id=1, source_target_pairs={{0,12},{4,8},{8,4},{12,0},{1,13},{5,9},{9,5},{13,1},{2,14},{6,10},... | collective-permute-start | bytes 172040 | tf_op jit(solution)/shard_map/ppermute | solution.py:26
  20.6 5.8 %collective-permute-start.12 = (bf16[2,56,256]{2,1,0:T(8,128)(2,1)S(1)}, bf16[2,56,256]{2,1,0:T(8,128)(2,1)S(1)}, u32[]{:S(2)}, u32[]{:S(2)}) collective-permute-start(bf16[2,56,256]{2,1,0:T(8,128)(2,1)S(1)} %get-tuple-element.43), channel_id=1, source_target_pairs={{0,4},{4,0},{8,12},{12,8},{1,5},{5,1},{9,13},{13,9},{2,6},{6,2},{1... | collective-permute-start | bytes 172040 | tf_op jit(solution)/shard_map/ppermute | solution.py:26
  23.0 5.1 %collective-permute-start.7 = (bf16[2,56,256]{2,1,0:T(8,128)(2,1)S(1)}, bf16[2,56,256]{2,1,0:T(8,128)(2,1)S(1)}, u32[]{:S(2)}, u32[]{:S(2)}) collective-permute-start(bf16[2,56,256]{2,1,0:T(8,128)(2,1)S(1)} %get-tuple-element.38), channel_id=1, source_target_pairs={{0,8},{4,12},{8,0},{12,4},{1,9},{5,13},{9,1},{13,5},{2,10},{6,14},... | collective-permute-start | bytes 172040 | tf_op jit(solution)/shard_map/ppermute | solution.py:26
  23.0 6.0 %collective-permute-start.8 = (bf16[2,56,256]{2,1,0:T(8,128)(2,1)S(1)}, bf16[2,56,256]{2,1,0:T(8,128)(2,1)S(1)}, u32[]{:S(2)}, u32[]{:S(2)}) collective-permute-start(bf16[2,56,256]{2,1,0:T(8,128)(2,1)S(1)} %get-tuple-element.39), channel_id=1, source_target_pairs={{0,12},{4,8},{8,4},{12,0},{1,13},{5,9},{9,5},{13,1},{2,14},{6,10},... | collective-permute-start | bytes 172040 | tf_op jit(solution)/shard_map/ppermute | solution.py:26
  25.1 4.5 %collective-permute-start.9 = (bf16[2,56,256]{2,1,0:T(8,128)(2,1)S(1)}, bf16[2,56,256]{2,1,0:T(8,128)(2,1)S(1)}, u32[]{:S(2)}, u32[]{:S(2)}) collective-permute-start(bf16[2,56,256]{2,1,0:T(8,128)(2,1)S(1)} %get-tuple-element.40), channel_id=1, source_target_pairs={{0,4},{4,0},{8,12},{12,8},{1,5},{5,1},{9,13},{13,9},{2,6},{6,2},{1... | collective-permute-start | bytes 172040 | tf_op jit(solution)/shard_map/ppermute | solution.py:26
  30.5 6.6 %collective-permute-start.15 = (f16[7,56,128]{2,1,0:T(8,128)(2,1)S(1)}, f16[7,56,128]{2,1,0:T(8,128)(2,1)S(1)}, u32[]{:S(2)}, u32[]{:S(2)}) collective-permute-start(f16[7,56,128]{2,1,0:T(8,128)(2,1)S(1)} %convert_element_type.20), channel_id=1, source_target_pairs={{0,12},{4,8},{8,4},{12,0},{1,13},{5,9},{9,5},{13,1},{2,14},{6,10},... | collective-permute-start | bytes 301064 | tf_op jit(solution)/shard_map/ppermute | solution.py:26
  32.8 6.8 %collective-permute-start.13 = (f16[7,56,128]{2,1,0:T(8,128)(2,1)S(1)}, f16[7,56,128]{2,1,0:T(8,128)(2,1)S(1)}, u32[]{:S(2)}, u32[]{:S(2)}) collective-permute-start(f16[7,56,128]{2,1,0:T(8,128)(2,1)S(1)} %convert_element_type.19), channel_id=1, source_target_pairs={{0,8},{4,12},{8,0},{12,4},{1,9},{5,13},{9,1},{13,5},{2,10},{6,14},... | collective-permute-start | bytes 301064 | tf_op jit(solution)/shard_map/ppermute | solution.py:26
  33.1 6.5 %collective-permute-start.14 = (f16[7,56,128]{2,1,0:T(8,128)(2,1)S(1)}, f16[7,56,128]{2,1,0:T(8,128)(2,1)S(1)}, u32[]{:S(2)}, u32[]{:S(2)}) collective-permute-start(f16[7,56,128]{2,1,0:T(8,128)(2,1)S(1)} %convert_element_type.18), channel_id=1, source_target_pairs={{0,4},{4,0},{8,12},{12,8},{1,5},{5,1},{9,13},{13,9},{2,6},{6,2},{1... | collective-permute-start | bytes 301064 | tf_op jit(solution)/shard_map/ppermute | solution.py:26

commit v6 on v5

--- a/solution.py
+++ b/solution.py
@@ -174,24 +174,12 @@
     return [refs[order.index(j)] for j in range(1, len(order) + 1)]
 
 
-def cross_kernel(loop, per, part, rows, last, mine, core, chip, *refs):
-    start, count = part
-    near, far = ordered(refs[: loop - 1], NEAR), ordered(refs[loop - 1 : 2 * loop - 2], FAR)
-    early, outs, blocks = refs[2 * loop - 2 : -1 - loop], refs[-1 - loop : -1], refs[-1]
-    t = lax.axis_index("tm")
-    lane = lane_of(rows)
+def products_of(loop, count, value, blocks, total=None):
+    t = lax.axis_index("tm")
     for s in range(count):
-        at = lanes_at((t * per + start + s) * LANES, LANES)
-        at_near = slice((start + s) * LANES, (start + s + 1) * LANES)
-        at_far = slice(s * LANES, (s + 1) * LANES)
-        at_chip = lanes_at((t * count + s) * LANES, LANES)
         for j in range(loop):
-            if j == 0:
-                values = mine[:, at], core[:, at], chip[0, :, at_chip], chip[1, :, at_chip]
-            else:
-                values = [near[j - 1][k, :, at_near] for k in range(2)] + [far[j - 1][k, :, at_far] for k in range(2)]
-            for k, value in enumerate(values):
-                blocks[s, t ^ j, :, k * LANES : (k + 1) * LANES] = padded(value).astype(jnp.bfloat16)
+            for k in range(2):
+                blocks[s, t ^ j, :, k * LANES : (k + 1) * LANES] = padded(value(s, j, k)).astype(jnp.bfloat16)
     products = {}
     for i in range(loop):
         r = t ^ i
@@ -200,7 +188,38 @@
             right = jnp.concatenate(
                 [blocks[s, (r + 1) % loop], blocks[s, (r + 2) % loop]], axis=0
             )
-            products[i, s] = dot_rows(left, right)
+            product = dot_rows(left, right)
+            products[i, s] = product if total is None else total[i, s] + product
+    return products
+
+
+def near_products_kernel(loop, per, part, mine, core, *refs):
+    near, (out, blocks) = ordered(refs[: loop - 1], NEAR), refs[-2:]
+    start, count = part
+    t = lax.axis_index("tm")
+
+    def value(s, j, k):
+        if j:
+            return near[j - 1][k, :, (start + s) * LANES : (start + s + 1) * LANES]
+        return (mine, core)[k][:, lanes_at((t * per + start + s) * LANES, LANES)]
+
+    for at, product in products_of(loop, count, value, blocks).items():
+        out[at] = product
+
+
+def cross_kernel(loop, part, rows, last, total, chip, *refs):
+    far = ordered(refs[: loop - 1], FAR)
+    early, outs, blocks = refs[loop - 1 : -1 - loop], refs[-1 - loop : -1], refs[-1]
+    count = part[1]
+    t = lax.axis_index("tm")
+    lane = lane_of(rows)
+
+    def value(s, j, k):
+        if j:
+            return far[j - 1][k, :, s * LANES : (s + 1) * LANES]
+        return chip[k, :, lanes_at((t * count + s) * LANES, LANES)]
+
+    products = products_of(loop, count, value, blocks, total)
     for i, out in enumerate(outs):
         new = []
         for s in range(count):
@@ -238,6 +257,7 @@
     tiles, (out, slots, sems) = refs[: len(partners)], refs[-3:]
     t = lax.axis_index("tm")
     lane = lane_of(rows)
+    step = sems.shape[1]
     copies = []
     for n, (i, part) in enumerate(zip(partners, tiles)):
         at = (t ^ i) * cycles
@@ -252,8 +272,16 @@
             value = pltpu.roll(value + 1.0, rows, 1)
             slots[n, c, :, :LANES] = jnp.where(lane < rows, own[at + c], value)
             slots[n, c, :, LANES:] = value[:, : 3 * rows - LANES]
-        copies.append(pltpu.make_async_copy(slots.at[n], out.at[pl.ds(at, cycles)], sems.at[n]))
-        copies[-1].start()
+            if (c + 1) % (cycles // step) == 0:
+                size = cycles // step
+                copies.append(
+                    pltpu.make_async_copy(
+                        slots.at[n, pl.ds(c + 1 - size, size)],
+                        out.at[pl.ds(at + c + 1 - size, size)],
+                        sems.at[n, c // size],
+                    )
+                )
+                copies[-1].start()
     for copy in copies:
         copy.wait()
 
@@ -295,12 +323,19 @@
         )(chip)
         far = [swap(value, "tm", j) for j, value in enumerate(far, 1)]
         last = part is parts[-1]
+        blocks = pltpu.VMEM((part[1], loop, rows + 8, 2 * LANES), bf16)
+        total = local_call(
+            functools.partial(near_products_kernel, loop, per, part),
+            [shape(loop, part[1], 2 * (rows + 8), LANES, dtype=f32)],
+            loop + 1,
+            [blocks],
+        )(mine, core, *[near[j - 1] for j in NEAR])[0]
         early += local_call(
-            functools.partial(cross_kernel, loop, per, part, rows, last),
+            functools.partial(cross_kernel, loop, part, rows, last),
             [tiles(cycles)] + [tiles(cycles - 1)] * (loop - 1) if last else [tiles(2 * part[1])] * loop,
-            2 * loop + 1 + (len(early) if last else 0),
-            [pltpu.VMEM((part[1], loop, rows + 8, groups * LANES), bf16)],
-        )(mine, core, chip, *[near[j - 1] for j in NEAR], *[far[j - 1] for j in FAR], *(early if last else ()))
+            loop + 1 + (len(early) if last else 0),
+            [blocks],
+        )(total, chip, *[far[j - 1] for j in FAR], *(early if last else ()))
     kept, *sent = early[-loop:]
     own_tiles = local_call(
         functools.partial(own_kernel, loop, per, parts, rows),
@@ -319,7 +354,7 @@
             1 + len(parts) + len(filled),
             [
                 pltpu.VMEM((len(partners), cycles, rows, 3 * rows), f32),
-                pltpu.SemaphoreType.DMA((len(partners),)),
+                pltpu.SemaphoreType.DMA((len(partners), 4)),
             ],
             in_specs=[VMEM] * (1 + len(parts)) + [HBM] * len(filled),
             out_specs=[HBM],

time: 41 us -> 40.8 us (level)
  waiting for transfers between devices: 10.4 us -> 9.9 us
    ppermute x16, waiting for transfers between devices: 10.4 us -> 9.9 us  [swap(): return lax.ppermute(shard, axis, [(i, i ^ by) for i in range(size)])]
    pallas_call x9 -> x11, Pallas kernels: 5.01 us -> 5.3 us  [local_call(): return lambda *operands: call(*operands, *after)]
  transfers between devices with their start and end apart: 16 -> 16, of which waited for: 9 -> 9; matrix products, arithmetic and copies ran while one was open for 0% -> 0% of each run, Pallas kernels for 7% -> 8%
where the time goes in v6:
time: 40.8 us; the launch traced here: 40.6 us
  starting transfers between devices  23.2 us (57%)
  waiting for transfers between devices  9.9 us (24%)
  Pallas kernels  5.3 us (13%)
  local copies, waits for them, and re-layouts  1.94 us (5%)
    ppermute x16, starting transfers between devices, swap(): return lax.ppermute(shard, axis, [(i, i ^ by) for i in range(size)])  23.2 us
    ppermute x16, waiting for transfers between devices, swap(): return lax.ppermute(shard, axis, [(i, i ^ by) for i in range(size)])  9.9 us
    pallas_call x11, Pallas kernels, local_call(): return lambda *operands: call(*operands, *after)  5.3 us
    unnamed x4, local copies, waits for them, and re-layouts  1.94 us
  transfers between devices with their start and end apart: 16, of which 9 were waited for; matrix products, arithmetic and copies ran while one was open for 0% of the time, Pallas kernels for 8%

profile of v6, /device:TPU:0, one launch (start us, length us, event | category | flops | bytes accessed | tf_op | source)
XLA Modules:
  0.0 40.6 jit_solution(1319562457529674050)
XLA Ops:
  0.0 0.5 %collective-permute-start = (bf16[56,8192]{1,0:T(8,128)(2,1)}, bf16[56,8192]{1,0:T(8,128)(2,1)S(1)}, u32[]{:S(2)}, u32[]{:S(2)}) collective-permute-start(bf16[56,8192]{1,0:T(8,128)(2,1)} %refs_0_.1), channel_id=1, source_target_pairs={{0,1},{1,0},{2,3},{3,2},{4,5},{5,4},{6,7},{7,6},{8,9},{9,8},{10,11... | collective-permute-start | bytes 2752520 | tf_op jit(solution)/shard_map/ppermute | solution.py:26
  0.5 1.2 %copy-done = bf16[56,8192]{1,0:T(8,128)(2,1)S(1)} copy-done((bf16[56,8192]{1,0:T(8,128)(2,1)S(1)}, bf16[56,8192]{1,0:T(8,128)(2,1)}, u32[]{:S(2)}) %copy-start) | copy-done | bytes 917528
  1.7 0.8 %copy-done.1 = s32[8192]{0:T(1024)S(1)} copy-done((s32[8192]{0:T(1024)S(1)}, s32[8192]{0:T(1024)}, u32[]{:S(2)}) %copy-start.1) | copy-done | bytes 32792
  2.4 0.1 shard_map.28
  2.6 0.2 collective-permute-done.1.refs_3_
  2.8 0.2 shard_map.29
  3.0 2.9 %collective-permute-start.2 = (bf16[2,56,1024]{2,1,0:T(8,128)(2,1)S(1)}, bf16[2,56,1024]{2,1,0:T(8,128)(2,1)S(1)}, u32[]{:S(2)}, u32[]{:S(2)}) collective-permute-start(bf16[2,56,1024]{2,1,0:T(8,128)(2,1)S(1)} %get-tuple-element.33), channel_id=1, source_target_pairs={{0,2},{1,3},{2,0},{3,1},{4,6},{5,7},{6,4},{7,5},{8,10},{9,11},{10,... | collective-permute-start | bytes 688136 | tf_op jit(solution)/shard_map/ppermute | solution.py:26
  5.9 0.1 collective-permute-start.3
  6.0 4.1 %collective-permute-start.4 = (bf16[2,56,512]{2,1,0:T(8,128)(2,1)S(1)}, bf16[2,56,512]{2,1,0:T(8,128)(2,1)S(1)}, u32[]{:S(2)}, u32[]{:S(2)}) collective-permute-start(bf16[2,56,512]{2,1,0:T(8,128)(2,1)S(1)} %get-tuple-element.35), channel_id=1, source_target_pairs={{0,12},{4,8},{8,4},{12,0},{1,13},{5,9},{9,5},{13,1},{2,14},{6,10},... | collective-permute-start | bytes 344072 | tf_op jit(solution)/shard_map/ppermute | solution.py:26
  10.1 0.6 %collective-permute-start.6 = (bf16[2,56,512]{2,1,0:T(8,128)(2,1)S(1)}, bf16[2,56,512]{2,1,0:T(8,128)(2,1)S(1)}, u32[]{:S(2)}, u32[]{:S(2)}) collective-permute-start(bf16[2,56,512]{2,1,0:T(8,128)(2,1)S(1)} %get-tuple-element.37), channel_id=1, source_target_pairs={{0,4},{4,0},{8,12},{12,8},{1,5},{5,1},{9,13},{13,9},{2,6},{6,2},{1... | collective-permute-start | bytes 344072 | tf_op jit(solution)/shard_map/ppermute | solution.py:26
  10.6 1.7 %collective-permute-done.2.refs_2_.refs_0_.refs_1_ = bf16[2,56,1024]{2,1,0:T(8,128)(2,1)S(1)} collective-permute-done((bf16[2,56,1024]{2,1,0:T(8,128)(2,1)S(1)}, bf16[2,56,1024]{2,1,0:T(8,128)(2,1)S(1)}, u32[]{:S(2)}, u32[]{:S(2)}) %collective-permute-start.2) | collective-permute-done | bytes 229408 | tf_op jit(solution)/shard_map/ppermute | solution.py:26
  12.4 3.2 %collective-permute-start.10 = (bf16[2,56,256]{2,1,0:T(8,128)(2,1)S(1)}, bf16[2,56,256]{2,1,0:T(8,128)(2,1)S(1)}, u32[]{:S(2)}, u32[]{:S(2)}) collective-permute-start(bf16[2,56,256]{2,1,0:T(8,128)(2,1)S(1)} %get-tuple-element.41), channel_id=1, source_target_pairs={{0,8},{4,12},{8,0},{12,4},{1,9},{5,13},{9,1},{13,5},{2,10},{6,14},... | collective-permute-start | bytes 172040 | tf_op jit(solution)/shard_map/ppermute | solution.py:26
  15.6 1.2 %collective-permute-done.3.refs_3_.refs_0_.refs_1_ = bf16[2,56,1024]{2,1,0:T(8,128)(2,1)S(1)} collective-permute-done((bf16[2,56,1024]{2,1,0:T(8,128)(2,1)S(1)}, bf16[2,56,1024]{2,1,0:T(8,128)(2,1)S(1)}, u32[]{:S(2)}, u32[]{:S(2)}) %collective-permute-start.3) | collective-permute-done | bytes 229408 | tf_op jit(solution)/shard_map/ppermute | solution.py:26
  16.8 3.9 %collective-permute-start.11 = (bf16[2,56,256]{2,1,0:T(8,128)(2,1)S(1)}, bf16[2,56,256]{2,1,0:T(8,128)(2,1)S(1)}, u32[]{:S(2)}, u32[]{:S(2)}) collective-permute-start(bf16[2,56,256]{2,1,0:T(8,128)(2,1)S(1)} %get-tuple-element.42), channel_id=1, source_target_pairs={{0,12},{4,8},{8,4},{12,0},{1,13},{5,9},{9,5},{13,1},{2,14},{6,10},... | collective-permute-start | bytes 172040 | tf_op jit(solution)/shard_map/ppermute | solution.py:26
  20.7 2.2 %collective-permute-done.5.refs_3_ = bf16[2,56,512]{2,1,0:T(8,128)(2,1)S(1)} collective-permute-done((bf16[2,56,512]{2,1,0:T(8,128)(2,1)S(1)}, bf16[2,56,512]{2,1,0:T(8,128)(2,1)S(1)}, u32[]{:S(2)}, u32[]{:S(2)}) %collective-permute-start.5) | collective-permute-done | bytes 114720 | tf_op jit(solution)/shard_map/ppermute | solution.py:26
  23.0 2.1 %collective-permute-start.8 = (bf16[2,56,256]{2,1,0:T(8,128)(2,1)S(1)}, bf16[2,56,256]{2,1,0:T(8,128)(2,1)S(1)}, u32[]{:S(2)}, u32[]{:S(2)}) collective-permute-start(bf16[2,56,256]{2,1,0:T(8,128)(2,1)S(1)} %get-tuple-element.39), channel_id=1, source_target_pairs={{0,12},{4,8},{8,4},{12,0},{1,13},{5,9},{9,5},{13,1},{2,14},{6,10},... | collective-permute-start | bytes 172040 | tf_op jit(solution)/shard_map/ppermute | solution.py:26
  25.1 1.4 %collective-permute-start.9 = (bf16[2,56,256]{2,1,0:T(8,128)(2,1)S(1)}, bf16[2,56,256]{2,1,0:T(8,128)(2,1)S(1)}, u32[]{:S(2)}, u32[]{:S(2)}) collective-permute-start(bf16[2,56,256]{2,1,0:T(8,128)(2,1)S(1)} %get-tuple-element.40), channel_id=1, source_target_pairs={{0,4},{4,0},{8,12},{12,8},{1,5},{5,1},{9,13},{13,9},{2,6},{6,2},{1... | collective-permute-start | bytes 172040 | tf_op jit(solution)/shard_map/ppermute | solution.py:26
  26.5 0.3 shard_map.33.refs_0_
  26.8 0.4 shard_map.31.refs_0_
  27.2 0.6 %shard_map.35 = (f32[4,56,128]{2,1,0:T(8,128)S(1)}, f32[4,56,128]{2,1,0:T(8,128)S(1)}, f32[4,56,128]{2,1,0:T(8,128)S(1)}, f32[4,56,128]{2,1,0:T(8,128)S(1)}) custom-call(f32[4,2,128,128]{3,2,1,0:T(8,128)S(1)} %shard_map.33.refs_0_, bf16[2,56,1024]{2,1,0:T(8,128)(2,1)S(1)} %collective-permute-done.2.refs_2_.refs_0_.refs_1_, ...), custom_call_target="tpu_custom_call" | custom-call | flops 1 | bytes 1 | tf_op jit(solution)/shard_map/pallas_call | solution.py:100
  27.7 0.3 collective-permute-done.7.refs_2_
  28.1 0.9 %collective-permute-done.8.refs_3_ = bf16[2,56,256]{2,1,0:T(8,128)(2,1)S(1)} collective-permute-done((bf16[2,56,256]{2,1,0:T(8,128)(2,1)S(1)}, bf16[2,56,256]{2,1,0:T(8,128)(2,1)S(1)}, u32[]{:S(2)}, u32[]{:S(2)}) %collective-permute-start.8) | collective-permute-done | bytes 57376 | tf_op jit(solution)/shard_map/ppermute | solution.py:26
  29.0 0.6 %collective-permute-done.9.refs_4_ = bf16[2,56,256]{2,1,0:T(8,128)(2,1)S(1)} collective-permute-done((bf16[2,56,256]{2,1,0:T(8,128)(2,1)S(1)}, bf16[2,56,256]{2,1,0:T(8,128)(2,1)S(1)}, u32[]{:S(2)}, u32[]{:S(2)}) %collective-permute-start.9) | collective-permute-done | bytes 57376 | tf_op jit(solution)/shard_map/ppermute | solution.py:26
  29.6 0.7 %shard_map.36 = (f32[8,56,128]{2,1,0:T(8,128)S(1)}, f32[7,56,128]{2,1,0:T(8,128)S(1)}, f32[7,56,128]{2,1,0:T(8,128)S(1)}, f32[7,56,128]{2,1,0:T(8,128)S(1)}) custom-call(f32[4,2,128,128]{3,2,1,0:T(8,128)S(1)} %shard_map.31.refs_0_, bf16[2,56,1024]{2,1,0:T(8,128)(2,1)S(1)} %collective-permute-done.3.refs_3_.refs_0_.refs_1_, ...), custom_call_target="tpu_custom_call" | custom-call | flops 1 | bytes 1 | tf_op jit(solution)/shard_map/pallas_call | solution.py:100
  30.3 2.3 %collective-permute-start.15 = (f16[7,56,128]{2,1,0:T(8,128)(2,1)S(1)}, f16[7,56,128]{2,1,0:T(8,128)(2,1)S(1)}, u32[]{:S(2)}, u32[]{:S(2)}) collective-permute-start(f16[7,56,128]{2,1,0:T(8,128)(2,1)S(1)} %convert_element_type.20), channel_id=1, source_target_pairs={{0,12},{4,8},{8,4},{12,0},{1,13},{5,9},{9,5},{13,1},{2,14},{6,10},... | collective-permute-start | bytes 301064 | tf_op jit(solution)/shard_map/ppermute | solution.py:26
  32.6 0.3 collective-permute-start.13
  33.0 1.8 %collective-permute-start.14 = (f16[7,56,128]{2,1,0:T(8,128)(2,1)S(1)}, f16[7,56,128]{2,1,0:T(8,128)(2,1)S(1)}, u32[]{:S(2)}, u32[]{:S(2)}) collective-permute-start(f16[7,56,128]{2,1,0:T(8,128)(2,1)S(1)} %convert_element_type.18), channel_id=1, source_target_pairs={{0,4},{4,0},{8,12},{12,8},{1,5},{5,1},{9,13},{13,9},{2,6},{6,2},{1... | collective-permute-start | bytes 301064 | tf_op jit(solution)/shard_map/ppermute | solution.py:26
  34.8 0.8 %shard_map.30.refs_0_ = f32[32,56,128]{2,1,0:T(8,128)S(1)} custom-call(bf16[56,2048]{1,0:T(8,128)(2,1)S(1)} %get-tuple-element.30.refs_0_, bf16[56,2048]{1,0:T(8,128)(2,1)S(1)} %get-tuple-element.32.refs_1_, bf16[2,56,1024]{2,1,0:T(8,128)(2,1)S(1)} %collective-permute-done.2.refs_2_.refs_0_.refs_1_, ...), custom_call_target="tpu_custom_call" | custom-call | flops 1 | bytes 4194304 | tf_op jit(solution)/shard_map/pallas_call | solution.py:100
  35.6 1.4 %collective-permute-done.15 = f16[7,56,128]{2,1,0:T(8,128)(2,1)S(1)} collective-permute-done((f16[7,56,128]{2,1,0:T(8,128)(2,1)S(1)}, f16[7,56,128]{2,1,0:T(8,128)(2,1)S(1)}, u32[]{:S(2)}, u32[]{:S(2)}) %collective-permute-start.15) | collective-permute-done | bytes 100384 | tf_op jit(solution)/shard_map/ppermute | solution.py:26
  37.0 1.1 %shard_map.37.refs_3_ = f32[32,56,168]{2,1,0:T(8,128)} custom-call(f32[32,56,128]{2,1,0:T(8,128)S(1)} %shard_map.30.refs_0_, f32[8,56,128]{2,1,0:T(8,128)S(1)} %get-tuple-element.53.refs_1_, f32[7,56,128]{2,1,0:T(8,128)S(1)} %convert_element_type.23.refs_2_), custom_call_target="tpu_custom_call" | custom-call | flops 1 | bytes 4194304 | tf_op jit(solution)/shard_map/pallas_call | solution.py:100
  38.1 1.3 %collective-permute-done.13 = f16[7,56,128]{2,1,0:T(8,128)(2,1)S(1)} collective-permute-done((f16[7,56,128]{2,1,0:T(8,128)(2,1)S(1)}, f16[7,56,128]{2,1,0:T(8,128)(2,1)S(1)}, u32[]{:S(2)}, u32[]{:S(2)}) %collective-permute-start.13) | collective-permute-done | bytes 100384 | tf_op jit(solution)/shard_map/ppermute | solution.py:26
  39.5 1.1 %shard_map.38 = f32[32,56,168]{2,1,0:T(8,128)} custom-call(f32[32,56,128]{2,1,0:T(8,128)S(1)} %shard_map.30.refs_0_, f32[7,56,128]{2,1,0:T(8,128)S(1)} %convert_element_type.21.refs_1_, f32[7,56,128]{2,1,0:T(8,128)S(1)} %convert_element_type.22.refs_2_, f32[32,56,168]{2,1,0:T(8,128)} %shard_map.37.refs_3_), custom_call_target="tpu_custom_call", output_to_operand_aliasing={{}: (3, {})} | custom-call | flops 1 | bytes 4194304 | tf_op jit(solution)/shard_map/pallas_call | solution.py:100
  (21 shorter events, 0.3 us)
Async XLA Ops:
  0.0 2.8 %collective-permute-start = (bf16[56,8192]{1,0:T(8,128)(2,1)}, bf16[56,8192]{1,0:T(8,128)(2,1)S(1)}, u32[]{:S(2)}, u32[]{:S(2)}) collective-permute-start(bf16[56,8192]{1,0:T(8,128)(2,1)} %refs_0_.1), channel_id=1, source_target_pairs={{0,1},{1,0},{2,3},{3,2},{4,5},{5,4},{6,7},{7,6},{8,9},{9,8},{10,11... | collective-permute-start | bytes 2752520 | tf_op jit(solution)/shard_map/ppermute | solution.py:26
  0.5 2.4 %collective-permute-start.1 = (s32[64,128]{1,0:T(8,128)}, s32[64,128]{1,0:T(8,128)S(1)}, u32[]{:S(2)}, u32[]{:S(2)}) collective-permute-start(s32[64,128]{1,0:T(8,128)} %bitcast.1), channel_id=1, source_target_pairs={{0,1},{1,0},{2,3},{3,2},{4,5},{5,4},{6,7},{7,6},{8,9},{9,8},{10,11... | collective-permute-start | bytes 98312 | tf_op jit(solution)/shard_map/ppermute | solution.py:26
  0.5 1.2 %copy-start = (bf16[56,8192]{1,0:T(8,128)(2,1)S(1)}, bf16[56,8192]{1,0:T(8,128)(2,1)}, u32[]{:S(2)}) copy-start(bf16[56,8192]{1,0:T(8,128)(2,1)} %refs_0_.1) | copy-start | bytes 2752516
  1.7 0.8 %copy-start.1 = (s32[8192]{0:T(1024)S(1)}, s32[8192]{0:T(1024)}, u32[]{:S(2)}) copy-start(s32[8192]{0:T(1024)} %param.3) | copy-start | bytes 98308
  3.0 9.3 %collective-permute-start.2 = (bf16[2,56,1024]{2,1,0:T(8,128)(2,1)S(1)}, bf16[2,56,1024]{2,1,0:T(8,128)(2,1)S(1)}, u32[]{:S(2)}, u32[]{:S(2)}) collective-permute-start(bf16[2,56,1024]{2,1,0:T(8,128)(2,1)S(1)} %get-tuple-element.33), channel_id=1, source_target_pairs={{0,2},{1,3},{2,0},{3,1},{4,6},{5,7},{6,4},{7,5},{8,10},{9,11},{10,... | collective-permute-start | bytes 688136 | tf_op jit(solution)/shard_map/ppermute | solution.py:26
  5.9 10.8 %collective-permute-start.3 = (bf16[2,56,1024]{2,1,0:T(8,128)(2,1)S(1)}, bf16[2,56,1024]{2,1,0:T(8,128)(2,1)S(1)}, u32[]{:S(2)}, u32[]{:S(2)}) collective-permute-start(bf16[2,56,1024]{2,1,0:T(8,128)(2,1)S(1)} %get-tuple-element.34), channel_id=1, source_target_pairs={{0,2},{1,3},{2,0},{3,1},{4,6},{5,7},{6,4},{7,5},{8,10},{9,11},{10,... | collective-permute-start | bytes 688136 | tf_op jit(solution)/shard_map/ppermute | solution.py:26
  6.0 14.6 %collective-permute-start.4 = (bf16[2,56,512]{2,1,0:T(8,128)(2,1)S(1)}, bf16[2,56,512]{2,1,0:T(8,128)(2,1)S(1)}, u32[]{:S(2)}, u32[]{:S(2)}) collective-permute-start(bf16[2,56,512]{2,1,0:T(8,128)(2,1)S(1)} %get-tuple-element.35), channel_id=1, source_target_pairs={{0,12},{4,8},{8,4},{12,0},{1,13},{5,9},{9,5},{13,1},{2,14},{6,10},... | collective-permute-start | bytes 344072 | tf_op jit(solution)/shard_map/ppermute | solution.py:26
  10.1 12.9 %collective-permute-start.5 = (bf16[2,56,512]{2,1,0:T(8,128)(2,1)S(1)}, bf16[2,56,512]{2,1,0:T(8,128)(2,1)S(1)}, u32[]{:S(2)}, u32[]{:S(2)}) collective-permute-start(bf16[2,56,512]{2,1,0:T(8,128)(2,1)S(1)} %get-tuple-element.36), channel_id=1, source_target_pairs={{0,8},{4,12},{8,0},{12,4},{1,9},{5,13},{9,1},{13,5},{2,10},{6,14},... | collective-permute-start | bytes 344072 | tf_op jit(solution)/shard_map/ppermute | solution.py:26
  10.1 12.9 %collective-permute-start.6 = (bf16[2,56,512]{2,1,0:T(8,128)(2,1)S(1)}, bf16[2,56,512]{2,1,0:T(8,128)(2,1)S(1)}, u32[]{:S(2)}, u32[]{:S(2)}) collective-permute-start(bf16[2,56,512]{2,1,0:T(8,128)(2,1)S(1)} %get-tuple-element.37), channel_id=1, source_target_pairs={{0,4},{4,0},{8,12},{12,8},{1,5},{5,1},{9,13},{13,9},{2,6},{6,2},{1... | collective-permute-start | bytes 344072 | tf_op jit(solution)/shard_map/ppermute | solution.py:26
  12.4 12.8 %collective-permute-start.10 = (bf16[2,56,256]{2,1,0:T(8,128)(2,1)S(1)}, bf16[2,56,256]{2,1,0:T(8,128)(2,1)S(1)}, u32[]{:S(2)}, u32[]{:S(2)}) collective-permute-start(bf16[2,56,256]{2,1,0:T(8,128)(2,1)S(1)} %get-tuple-element.41), channel_id=1, source_target_pairs={{0,8},{4,12},{8,0},{12,4},{1,9},{5,13},{9,1},{13,5},{2,10},{6,14},... | collective-permute-start | bytes 172040 | tf_op jit(solution)/shard_map/ppermute | solution.py:26
  16.8 10.4 %collective-permute-start.11 = (bf16[2,56,256]{2,1,0:T(8,128)(2,1)S(1)}, bf16[2,56,256]{2,1,0:T(8,128)(2,1)S(1)}, u32[]{:S(2)}, u32[]{:S(2)}) collective-permute-start(bf16[2,56,256]{2,1,0:T(8,128)(2,1)S(1)} %get-tuple-element.42), channel_id=1, source_target_pairs={{0,12},{4,8},{8,4},{12,0},{1,13},{5,9},{9,5},{13,1},{2,14},{6,10},... | collective-permute-start | bytes 172040 | tf_op jit(solution)/shard_map/ppermute | solution.py:26
  20.6 6.5 %collective-permute-start.12 = (bf16[2,56,256]{2,1,0:T(8,128)(2,1)S(1)}, bf16[2,56,256]{2,1,0:T(8,128)(2,1)S(1)}, u32[]{:S(2)}, u32[]{:S(2)}) collective-permute-start(bf16[2,56,256]{2,1,0:T(8,128)(2,1)S(1)} %get-tuple-element.43), channel_id=1, source_target_pairs={{0,4},{4,0},{8,12},{12,8},{1,5},{5,1},{9,13},{13,9},{2,6},{6,2},{1... | collective-permute-start | bytes 172040 | tf_op jit(solution)/shard_map/ppermute | solution.py:26
  23.0 5.1 %collective-permute-start.7 = (bf16[2,56,256]{2,1,0:T(8,128)(2,1)S(1)}, bf16[2,56,256]{2,1,0:T(8,128)(2,1)S(1)}, u32[]{:S(2)}, u32[]{:S(2)}) collective-permute-start(bf16[2,56,256]{2,1,0:T(8,128)(2,1)S(1)} %get-tuple-element.38), channel_id=1, source_target_pairs={{0,8},{4,12},{8,0},{12,4},{1,9},{5,13},{9,1},{13,5},{2,10},{6,14},... | collective-permute-start | bytes 172040 | tf_op jit(solution)/shard_map/ppermute | solution.py:26
  23.0 6.0 %collective-permute-start.8 = (bf16[2,56,256]{2,1,0:T(8,128)(2,1)S(1)}, bf16[2,56,256]{2,1,0:T(8,128)(2,1)S(1)}, u32[]{:S(2)}, u32[]{:S(2)}) collective-permute-start(bf16[2,56,256]{2,1,0:T(8,128)(2,1)S(1)} %get-tuple-element.39), channel_id=1, source_target_pairs={{0,12},{4,8},{8,4},{12,0},{1,13},{5,9},{9,5},{13,1},{2,14},{6,10},... | collective-permute-start | bytes 172040 | tf_op jit(solution)/shard_map/ppermute | solution.py:26
  25.1 4.5 %collective-permute-start.9 = (bf16[2,56,256]{2,1,0:T(8,128)(2,1)S(1)}, bf16[2,56,256]{2,1,0:T(8,128)(2,1)S(1)}, u32[]{:S(2)}, u32[]{:S(2)}) collective-permute-start(bf16[2,56,256]{2,1,0:T(8,128)(2,1)S(1)} %get-tuple-element.40), channel_id=1, source_target_pairs={{0,4},{4,0},{8,12},{12,8},{1,5},{5,1},{9,13},{13,9},{2,6},{6,2},{1... | collective-permute-start | bytes 172040 | tf_op jit(solution)/shard_map/ppermute | solution.py:26
  30.3 6.6 %collective-permute-start.15 = (f16[7,56,128]{2,1,0:T(8,128)(2,1)S(1)}, f16[7,56,128]{2,1,0:T(8,128)(2,1)S(1)}, u32[]{:S(2)}, u32[]{:S(2)}) collective-permute-start(f16[7,56,128]{2,1,0:T(8,128)(2,1)S(1)} %convert_element_type.20), channel_id=1, source_target_pairs={{0,12},{4,8},{8,4},{12,0},{1,13},{5,9},{9,5},{13,1},{2,14},{6,10},... | collective-permute-start | bytes 301064 | tf_op jit(solution)/shard_map/ppermute | solution.py:26
  32.6 6.8 %collective-permute-start.13 = (f16[7,56,128]{2,1,0:T(8,128)(2,1)S(1)}, f16[7,56,128]{2,1,0:T(8,128)(2,1)S(1)}, u32[]{:S(2)}, u32[]{:S(2)}) collective-permute-start(f16[7,56,128]{2,1,0:T(8,128)(2,1)S(1)} %convert_element_type.19), channel_id=1, source_target_pairs={{0,8},{4,12},{8,0},{12,4},{1,9},{5,13},{9,1},{13,5},{2,10},{6,14},... | collective-permute-start | bytes 301064 | tf_op jit(solution)/shard_map/ppermute | solution.py:26
  33.0 6.5 %collective-permute-start.14 = (f16[7,56,128]{2,1,0:T(8,128)(2,1)S(1)}, f16[7,56,128]{2,1,0:T(8,128)(2,1)S(1)}, u32[]{:S(2)}, u32[]{:S(2)}) collective-permute-start(f16[7,56,128]{2,1,0:T(8,128)(2,1)S(1)} %convert_element_type.18), channel_id=1, source_target_pairs={{0,4},{4,0},{8,12},{12,8},{1,5},{5,1},{9,13},{13,9},{2,6},{6,2},{1... | collective-permute-start | bytes 301064 | tf_op jit(solution)/shard_map/ppermute | solution.py:26

commit v7 on v6

--- a/solution.py
+++ b/solution.py
@@ -142,11 +142,10 @@
 
 
 def halves(block):
-    lane = lax.broadcasted_iota(jnp.int32, block.shape, 1) % LANES
-    zero = jnp.zeros_like(block)
-    return jnp.concatenate(
-        [jnp.where(lane < CYCLE_CAP, block, zero), jnp.where(lane < CYCLE_CAP, zero, block)], axis=0
-    )
+    lane = lax.broadcasted_iota(jnp.int32, (1, block.shape[1]), 1) % LANES
+    even = jnp.where(lane < CYCLE_CAP, 1.0, 0.0).astype(block.dtype)
+    odd = jnp.where(lane < CYCLE_CAP, 0.0, 1.0).astype(block.dtype)
+    return jnp.concatenate([block * even, block * odd], axis=0)
 
 
 def normalized(product, rows):
@@ -154,9 +153,9 @@
     for half in range(2):
         cycle = product[half * (rows + 8) : (half + 1) * (rows + 8)]
         count = cycle[rows : rows + 1, rows : rows + 1]
-        row_scale = count / cycle[:rows, rows : rows + 1]
-        column_scale = 1.0 / cycle[rows : rows + 1, :]
-        result.append(cycle[:rows] * row_scale * column_scale)
+        column_scale = count / cycle[rows : rows + 1, :]
+        row_scale = 1.0 / cycle[:rows, rows : rows + 1]
+        result.append(cycle[:rows] * (row_scale * column_scale))
     return result
 
 
@@ -184,7 +183,7 @@
     for i in range(loop):
         r = t ^ i
         for s in range(count):
-            left = halves(blocks[s, r].astype(jnp.float32)).astype(jnp.bfloat16)
+            left = halves(blocks[s, r])
             right = jnp.concatenate(
                 [blocks[s, (r + 1) % loop], blocks[s, (r + 2) % loop]], axis=0
             )
@@ -246,8 +245,8 @@
                 at_chip = slice((c * count + s) * LANES, (c * count + s + 1) * LANES)
                 values = mine[:, at], core[:, at], chip[0, :, at_chip], chip[1, :, at_chip]
                 block = jnp.concatenate([padded(value) for value in values], axis=1)
-                left = halves(block).astype(jnp.bfloat16)
                 block = block.astype(jnp.bfloat16)
+                left = halves(block)
                 right = jnp.concatenate([block, block], axis=0)
                 for half, cycle in enumerate(normalized(dot_rows(left, right), rows)):
                     out[2 * n + half] = cycle

time: 40.8 us -> 40.8 us (level)
  no operation moved by 1% of the time
where the time goes in v7:
time: 40.8 us; the launch traced here: 40.6 us
  starting transfers between devices  23.2 us (57%)
  waiting for transfers between devices  9.88 us (24%)
  Pallas kernels  5.33 us (13%)
  local copies, waits for them, and re-layouts  1.94 us (5%)
    ppermute x16, starting transfers between devices, swap(): return lax.ppermute(shard, axis, [(i, i ^ by) for i in range(size)])  23.2 us
    ppermute x16, waiting for transfers between devices, swap(): return lax.ppermute(shard, axis, [(i, i ^ by) for i in range(size)])  9.88 us
    pallas_call x11, Pallas kernels, local_call(): return lambda *operands: call(*operands, *after)  5.33 us
    unnamed x4, local copies, waits for them, and re-layouts  1.94 us
  transfers between devices with their start and end apart: 16, of which 9 were waited for; matrix products, arithmetic and copies ran while one was open for 0% of the time, Pallas kernels for 8%

profile of v7, /device:TPU:0, one launch (start us, length us, event | category | flops | bytes accessed | tf_op | source)
XLA Modules:
  0.0 40.6 jit_solution(543838749550132341)
XLA Ops:
  0.0 0.5 %collective-permute-start = (bf16[56,8192]{1,0:T(8,128)(2,1)}, bf16[56,8192]{1,0:T(8,128)(2,1)S(1)}, u32[]{:S(2)}, u32[]{:S(2)}) collective-permute-start(bf16[56,8192]{1,0:T(8,128)(2,1)} %refs_0_.1), channel_id=1, source_target_pairs={{0,1},{1,0},{2,3},{3,2},{4,5},{5,4},{6,7},{7,6},{8,9},{9,8},{10,11... | collective-permute-start | bytes 2752520 | tf_op jit(solution)/shard_map/ppermute | solution.py:26
  0.5 1.2 %copy-done = bf16[56,8192]{1,0:T(8,128)(2,1)S(1)} copy-done((bf16[56,8192]{1,0:T(8,128)(2,1)S(1)}, bf16[56,8192]{1,0:T(8,128)(2,1)}, u32[]{:S(2)}) %copy-start) | copy-done | bytes 917528
  1.7 0.8 %copy-done.1 = s32[8192]{0:T(1024)S(1)} copy-done((s32[8192]{0:T(1024)S(1)}, s32[8192]{0:T(1024)}, u32[]{:S(2)}) %copy-start.1) | copy-done | bytes 32792
  2.4 0.1 shard_map.28
  2.6 0.2 collective-permute-done.1.refs_3_
  2.8 0.2 shard_map.29
  3.0 2.9 %collective-permute-start.2 = (bf16[2,56,1024]{2,1,0:T(8,128)(2,1)S(1)}, bf16[2,56,1024]{2,1,0:T(8,128)(2,1)S(1)}, u32[]{:S(2)}, u32[]{:S(2)}) collective-permute-start(bf16[2,56,1024]{2,1,0:T(8,128)(2,1)S(1)} %get-tuple-element.33), channel_id=1, source_target_pairs={{0,2},{1,3},{2,0},{3,1},{4,6},{5,7},{6,4},{7,5},{8,10},{9,11},{10,... | collective-permute-start | bytes 688136 | tf_op jit(solution)/shard_map/ppermute | solution.py:26
  5.9 0.1 collective-permute-start.3
  6.0 4.1 %collective-permute-start.4 = (bf16[2,56,512]{2,1,0:T(8,128)(2,1)S(1)}, bf16[2,56,512]{2,1,0:T(8,128)(2,1)S(1)}, u32[]{:S(2)}, u32[]{:S(2)}) collective-permute-start(bf16[2,56,512]{2,1,0:T(8,128)(2,1)S(1)} %get-tuple-element.35), channel_id=1, source_target_pairs={{0,12},{4,8},{8,4},{12,0},{1,13},{5,9},{9,5},{13,1},{2,14},{6,10},... | collective-permute-start | bytes 344072 | tf_op jit(solution)/shard_map/ppermute | solution.py:26
  10.1 0.6 %collective-permute-start.6 = (bf16[2,56,512]{2,1,0:T(8,128)(2,1)S(1)}, bf16[2,56,512]{2,1,0:T(8,128)(2,1)S(1)}, u32[]{:S(2)}, u32[]{:S(2)}) collective-permute-start(bf16[2,56,512]{2,1,0:T(8,128)(2,1)S(1)} %get-tuple-element.37), channel_id=1, source_target_pairs={{0,4},{4,0},{8,12},{12,8},{1,5},{5,1},{9,13},{13,9},{2,6},{6,2},{1... | collective-permute-start | bytes 344072 | tf_op jit(solution)/shard_map/ppermute | solution.py:26
  10.6 1.7 %collective-permute-done.2.refs_2_.refs_0_.refs_1_ = bf16[2,56,1024]{2,1,0:T(8,128)(2,1)S(1)} collective-permute-done((bf16[2,56,1024]{2,1,0:T(8,128)(2,1)S(1)}, bf16[2,56,1024]{2,1,0:T(8,128)(2,1)S(1)}, u32[]{:S(2)}, u32[]{:S(2)}) %collective-permute-start.2) | collective-permute-done | bytes 229408 | tf_op jit(solution)/shard_map/ppermute | solution.py:26
  12.4 3.2 %collective-permute-start.10 = (bf16[2,56,256]{2,1,0:T(8,128)(2,1)S(1)}, bf16[2,56,256]{2,1,0:T(8,128)(2,1)S(1)}, u32[]{:S(2)}, u32[]{:S(2)}) collective-permute-start(bf16[2,56,256]{2,1,0:T(8,128)(2,1)S(1)} %get-tuple-element.41), channel_id=1, source_target_pairs={{0,8},{4,12},{8,0},{12,4},{1,9},{5,13},{9,1},{13,5},{2,10},{6,14},... | collective-permute-start | bytes 172040 | tf_op jit(solution)/shard_map/ppermute | solution.py:26
  15.6 1.2 %collective-permute-done.3.refs_3_.refs_0_.refs_1_ = bf16[2,56,1024]{2,1,0:T(8,128)(2,1)S(1)} collective-permute-done((bf16[2,56,1024]{2,1,0:T(8,128)(2,1)S(1)}, bf16[2,56,1024]{2,1,0:T(8,128)(2,1)S(1)}, u32[]{:S(2)}, u32[]{:S(2)}) %collective-permute-start.3) | collective-permute-done | bytes 229408 | tf_op jit(solution)/shard_map/ppermute | solution.py:26
  16.8 3.9 %collective-permute-start.11 = (bf16[2,56,256]{2,1,0:T(8,128)(2,1)S(1)}, bf16[2,56,256]{2,1,0:T(8,128)(2,1)S(1)}, u32[]{:S(2)}, u32[]{:S(2)}) collective-permute-start(bf16[2,56,256]{2,1,0:T(8,128)(2,1)S(1)} %get-tuple-element.42), channel_id=1, source_target_pairs={{0,12},{4,8},{8,4},{12,0},{1,13},{5,9},{9,5},{13,1},{2,14},{6,10},... | collective-permute-start | bytes 172040 | tf_op jit(solution)/shard_map/ppermute | solution.py:26
  20.7 2.2 %collective-permute-done.5.refs_3_ = bf16[2,56,512]{2,1,0:T(8,128)(2,1)S(1)} collective-permute-done((bf16[2,56,512]{2,1,0:T(8,128)(2,1)S(1)}, bf16[2,56,512]{2,1,0:T(8,128)(2,1)S(1)}, u32[]{:S(2)}, u32[]{:S(2)}) %collective-permute-start.5) | collective-permute-done | bytes 114720 | tf_op jit(solution)/shard_map/ppermute | solution.py:26
  23.0 2.1 %collective-permute-start.8 = (bf16[2,56,256]{2,1,0:T(8,128)(2,1)S(1)}, bf16[2,56,256]{2,1,0:T(8,128)(2,1)S(1)}, u32[]{:S(2)}, u32[]{:S(2)}) collective-permute-start(bf16[2,56,256]{2,1,0:T(8,128)(2,1)S(1)} %get-tuple-element.39), channel_id=1, source_target_pairs={{0,12},{4,8},{8,4},{12,0},{1,13},{5,9},{9,5},{13,1},{2,14},{6,10},... | collective-permute-start | bytes 172040 | tf_op jit(solution)/shard_map/ppermute | solution.py:26
  25.1 1.4 %collective-permute-start.9 = (bf16[2,56,256]{2,1,0:T(8,128)(2,1)S(1)}, bf16[2,56,256]{2,1,0:T(8,128)(2,1)S(1)}, u32[]{:S(2)}, u32[]{:S(2)}) collective-permute-start(bf16[2,56,256]{2,1,0:T(8,128)(2,1)S(1)} %get-tuple-element.40), channel_id=1, source_target_pairs={{0,4},{4,0},{8,12},{12,8},{1,5},{5,1},{9,13},{13,9},{2,6},{6,2},{1... | collective-permute-start | bytes 172040 | tf_op jit(solution)/shard_map/ppermute | solution.py:26
  26.5 0.4 shard_map.33.refs_0_
  26.8 0.4 shard_map.31.refs_0_
  27.2 0.6 %shard_map.35 = (f32[4,56,128]{2,1,0:T(8,128)S(1)}, f32[4,56,128]{2,1,0:T(8,128)S(1)}, f32[4,56,128]{2,1,0:T(8,128)S(1)}, f32[4,56,128]{2,1,0:T(8,128)S(1)}) custom-call(f32[4,2,128,128]{3,2,1,0:T(8,128)S(1)} %shard_map.33.refs_0_, bf16[2,56,1024]{2,1,0:T(8,128)(2,1)S(1)} %collective-permute-done.2.refs_2_.refs_0_.refs_1_, ...), custom_call_target="tpu_custom_call" | custom-call | flops 1 | bytes 1 | tf_op jit(solution)/shard_map/pallas_call | solution.py:100
  27.8 0.3 collective-permute-done.7.refs_2_
  28.1 0.9 %collective-permute-done.8.refs_3_ = bf16[2,56,256]{2,1,0:T(8,128)(2,1)S(1)} collective-permute-done((bf16[2,56,256]{2,1,0:T(8,128)(2,1)S(1)}, bf16[2,56,256]{2,1,0:T(8,128)(2,1)S(1)}, u32[]{:S(2)}, u32[]{:S(2)}) %collective-permute-start.8) | collective-permute-done | bytes 57376 | tf_op jit(solution)/shard_map/ppermute | solution.py:26
  29.0 0.6 %collective-permute-done.9.refs_4_ = bf16[2,56,256]{2,1,0:T(8,128)(2,1)S(1)} collective-permute-done((bf16[2,56,256]{2,1,0:T(8,128)(2,1)S(1)}, bf16[2,56,256]{2,1,0:T(8,128)(2,1)S(1)}, u32[]{:S(2)}, u32[]{:S(2)}) %collective-permute-start.9) | collective-permute-done | bytes 57376 | tf_op jit(solution)/shard_map/ppermute | solution.py:26
  29.6 0.7 %shard_map.36 = (f32[8,56,128]{2,1,0:T(8,128)S(1)}, f32[7,56,128]{2,1,0:T(8,128)S(1)}, f32[7,56,128]{2,1,0:T(8,128)S(1)}, f32[7,56,128]{2,1,0:T(8,128)S(1)}) custom-call(f32[4,2,128,128]{3,2,1,0:T(8,128)S(1)} %shard_map.31.refs_0_, bf16[2,56,1024]{2,1,0:T(8,128)(2,1)S(1)} %collective-permute-done.3.refs_3_.refs_0_.refs_1_, ...), custom_call_target="tpu_custom_call" | custom-call | flops 1 | bytes 1 | tf_op jit(solution)/shard_map/pallas_call | solution.py:100
  30.4 2.3 %collective-permute-start.15 = (f16[7,56,128]{2,1,0:T(8,128)(2,1)S(1)}, f16[7,56,128]{2,1,0:T(8,128)(2,1)S(1)}, u32[]{:S(2)}, u32[]{:S(2)}) collective-permute-start(f16[7,56,128]{2,1,0:T(8,128)(2,1)S(1)} %convert_element_type.20), channel_id=1, source_target_pairs={{0,12},{4,8},{8,4},{12,0},{1,13},{5,9},{9,5},{13,1},{2,14},{6,10},... | collective-permute-start | bytes 301064 | tf_op jit(solution)/shard_map/ppermute | solution.py:26
  32.7 0.3 collective-permute-start.13
  33.0 1.8 %collective-permute-start.14 = (f16[7,56,128]{2,1,0:T(8,128)(2,1)S(1)}, f16[7,56,128]{2,1,0:T(8,128)(2,1)S(1)}, u32[]{:S(2)}, u32[]{:S(2)}) collective-permute-start(f16[7,56,128]{2,1,0:T(8,128)(2,1)S(1)} %convert_element_type.18), channel_id=1, source_target_pairs={{0,4},{4,0},{8,12},{12,8},{1,5},{5,1},{9,13},{13,9},{2,6},{6,2},{1... | collective-permute-start | bytes 301064 | tf_op jit(solution)/shard_map/ppermute | solution.py:26
  34.8 0.8 %shard_map.30.refs_0_ = f32[32,56,128]{2,1,0:T(8,128)S(1)} custom-call(bf16[56,2048]{1,0:T(8,128)(2,1)S(1)} %get-tuple-element.30.refs_0_, bf16[56,2048]{1,0:T(8,128)(2,1)S(1)} %get-tuple-element.32.refs_1_, bf16[2,56,1024]{2,1,0:T(8,128)(2,1)S(1)} %collective-permute-done.2.refs_2_.refs_0_.refs_1_, ...), custom_call_target="tpu_custom_call" | custom-call | flops 1 | bytes 4194304 | tf_op jit(solution)/shard_map/pallas_call | solution.py:100
  35.6 1.4 %collective-permute-done.15 = f16[7,56,128]{2,1,0:T(8,128)(2,1)S(1)} collective-permute-done((f16[7,56,128]{2,1,0:T(8,128)(2,1)S(1)}, f16[7,56,128]{2,1,0:T(8,128)(2,1)S(1)}, u32[]{:S(2)}, u32[]{:S(2)}) %collective-permute-start.15) | collective-permute-done | bytes 100384 | tf_op jit(solution)/shard_map/ppermute | solution.py:26
  37.0 1.1 %shard_map.37.refs_3_ = f32[32,56,168]{2,1,0:T(8,128)} custom-call(f32[32,56,128]{2,1,0:T(8,128)S(1)} %shard_map.30.refs_0_, f32[8,56,128]{2,1,0:T(8,128)S(1)} %get-tuple-element.53.refs_1_, f32[7,56,128]{2,1,0:T(8,128)S(1)} %convert_element_type.23.refs_2_), custom_call_target="tpu_custom_call" | custom-call | flops 1 | bytes 4194304 | tf_op jit(solution)/shard_map/pallas_call | solution.py:100
  38.1 1.3 %collective-permute-done.13 = f16[7,56,128]{2,1,0:T(8,128)(2,1)S(1)} collective-permute-done((f16[7,56,128]{2,1,0:T(8,128)(2,1)S(1)}, f16[7,56,128]{2,1,0:T(8,128)(2,1)S(1)}, u32[]{:S(2)}, u32[]{:S(2)}) %collective-permute-start.13) | collective-permute-done | bytes 100384 | tf_op jit(solution)/shard_map/ppermute | solution.py:26
  39.5 1.1 %shard_map.38 = f32[32,56,168]{2,1,0:T(8,128)} custom-call(f32[32,56,128]{2,1,0:T(8,128)S(1)} %shard_map.30.refs_0_, f32[7,56,128]{2,1,0:T(8,128)S(1)} %convert_element_type.21.refs_1_, f32[7,56,128]{2,1,0:T(8,128)S(1)} %convert_element_type.22.refs_2_, f32[32,56,168]{2,1,0:T(8,128)} %shard_map.37.refs_3_), custom_call_target="tpu_custom_call", output_to_operand_aliasing={{}: (3, {})} | custom-call | flops 1 | bytes 4194304 | tf_op jit(solution)/shard_map/pallas_call | solution.py:100
  (21 shorter events, 0.3 us)
Async XLA Ops:
  0.0 2.8 %collective-permute-start = (bf16[56,8192]{1,0:T(8,128)(2,1)}, bf16[56,8192]{1,0:T(8,128)(2,1)S(1)}, u32[]{:S(2)}, u32[]{:S(2)}) collective-permute-start(bf16[56,8192]{1,0:T(8,128)(2,1)} %refs_0_.1), channel_id=1, source_target_pairs={{0,1},{1,0},{2,3},{3,2},{4,5},{5,4},{6,7},{7,6},{8,9},{9,8},{10,11... | collective-permute-start | bytes 2752520 | tf_op jit(solution)/shard_map/ppermute | solution.py:26
  0.5 2.4 %collective-permute-start.1 = (s32[64,128]{1,0:T(8,128)}, s32[64,128]{1,0:T(8,128)S(1)}, u32[]{:S(2)}, u32[]{:S(2)}) collective-permute-start(s32[64,128]{1,0:T(8,128)} %bitcast.1), channel_id=1, source_target_pairs={{0,1},{1,0},{2,3},{3,2},{4,5},{5,4},{6,7},{7,6},{8,9},{9,8},{10,11... | collective-permute-start | bytes 98312 | tf_op jit(solution)/shard_map/ppermute | solution.py:26
  0.5 1.2 %copy-start = (bf16[56,8192]{1,0:T(8,128)(2,1)S(1)}, bf16[56,8192]{1,0:T(8,128)(2,1)}, u32[]{:S(2)}) copy-start(bf16[56,8192]{1,0:T(8,128)(2,1)} %refs_0_.1) | copy-start | bytes 2752516
  1.7 0.8 %copy-start.1 = (s32[8192]{0:T(1024)S(1)}, s32[8192]{0:T(1024)}, u32[]{:S(2)}) copy-start(s32[8192]{0:T(1024)} %param.3) | copy-start | bytes 98308
  3.0 9.3 %collective-permute-start.2 = (bf16[2,56,1024]{2,1,0:T(8,128)(2,1)S(1)}, bf16[2,56,1024]{2,1,0:T(8,128)(2,1)S(1)}, u32[]{:S(2)}, u32[]{:S(2)}) collective-permute-start(bf16[2,56,1024]{2,1,0:T(8,128)(2,1)S(1)} %get-tuple-element.33), channel_id=1, source_target_pairs={{0,2},{1,3},{2,0},{3,1},{4,6},{5,7},{6,4},{7,5},{8,10},{9,11},{10,... | collective-permute-start | bytes 688136 | tf_op jit(solution)/shard_map/ppermute | solution.py:26
  5.9 10.8 %collective-permute-start.3 = (bf16[2,56,1024]{2,1,0:T(8,128)(2,1)S(1)}, bf16[2,56,1024]{2,1,0:T(8,128)(2,1)S(1)}, u32[]{:S(2)}, u32[]{:S(2)}) collective-permute-start(bf16[2,56,1024]{2,1,0:T(8,128)(2,1)S(1)} %get-tuple-element.34), channel_id=1, source_target_pairs={{0,2},{1,3},{2,0},{3,1},{4,6},{5,7},{6,4},{7,5},{8,10},{9,11},{10,... | collective-permute-start | bytes 688136 | tf_op jit(solution)/shard_map/ppermute | solution.py:26
  6.0 14.6 %collective-permute-start.4 = (bf16[2,56,512]{2,1,0:T(8,128)(2,1)S(1)}, bf16[2,56,512]{2,1,0:T(8,128)(2,1)S(1)}, u32[]{:S(2)}, u32[]{:S(2)}) collective-permute-start(bf16[2,56,512]{2,1,0:T(8,128)(2,1)S(1)} %get-tuple-element.35), channel_id=1, source_target_pairs={{0,12},{4,8},{8,4},{12,0},{1,13},{5,9},{9,5},{13,1},{2,14},{6,10},... | collective-permute-start | bytes 344072 | tf_op jit(solution)/shard_map/ppermute | solution.py:26
  10.1 12.9 %collective-permute-start.5 = (bf16[2,56,512]{2,1,0:T(8,128)(2,1)S(1)}, bf16[2,56,512]{2,1,0:T(8,128)(2,1)S(1)}, u32[]{:S(2)}, u32[]{:S(2)}) collective-permute-start(bf16[2,56,512]{2,1,0:T(8,128)(2,1)S(1)} %get-tuple-element.36), channel_id=1, source_target_pairs={{0,8},{4,12},{8,0},{12,4},{1,9},{5,13},{9,1},{13,5},{2,10},{6,14},... | collective-permute-start | bytes 344072 | tf_op jit(solution)/shard_map/ppermute | solution.py:26
  10.1 12.9 %collective-permute-start.6 = (bf16[2,56,512]{2,1,0:T(8,128)(2,1)S(1)}, bf16[2,56,512]{2,1,0:T(8,128)(2,1)S(1)}, u32[]{:S(2)}, u32[]{:S(2)}) collective-permute-start(bf16[2,56,512]{2,1,0:T(8,128)(2,1)S(1)} %get-tuple-element.37), channel_id=1, source_target_pairs={{0,4},{4,0},{8,12},{12,8},{1,5},{5,1},{9,13},{13,9},{2,6},{6,2},{1... | collective-permute-start | bytes 344072 | tf_op jit(solution)/shard_map/ppermute | solution.py:26
  12.4 12.8 %collective-permute-start.10 = (bf16[2,56,256]{2,1,0:T(8,128)(2,1)S(1)}, bf16[2,56,256]{2,1,0:T(8,128)(2,1)S(1)}, u32[]{:S(2)}, u32[]{:S(2)}) collective-permute-start(bf16[2,56,256]{2,1,0:T(8,128)(2,1)S(1)} %get-tuple-element.41), channel_id=1, source_target_pairs={{0,8},{4,12},{8,0},{12,4},{1,9},{5,13},{9,1},{13,5},{2,10},{6,14},... | collective-permute-start | bytes 172040 | tf_op jit(solution)/shard_map/ppermute | solution.py:26
  16.8 10.4 %collective-permute-start.11 = (bf16[2,56,256]{2,1,0:T(8,128)(2,1)S(1)}, bf16[2,56,256]{2,1,0:T(8,128)(2,1)S(1)}, u32[]{:S(2)}, u32[]{:S(2)}) collective-permute-start(bf16[2,56,256]{2,1,0:T(8,128)(2,1)S(1)} %get-tuple-element.42), channel_id=1, source_target_pairs={{0,12},{4,8},{8,4},{12,0},{1,13},{5,9},{9,5},{13,1},{2,14},{6,10},... | collective-permute-start | bytes 172040 | tf_op jit(solution)/shard_map/ppermute | solution.py:26
  20.6 6.6 %collective-permute-start.12 = (bf16[2,56,256]{2,1,0:T(8,128)(2,1)S(1)}, bf16[2,56,256]{2,1,0:T(8,128)(2,1)S(1)}, u32[]{:S(2)}, u32[]{:S(2)}) collective-permute-start(bf16[2,56,256]{2,1,0:T(8,128)(2,1)S(1)} %get-tuple-element.43), channel_id=1, source_target_pairs={{0,4},{4,0},{8,12},{12,8},{1,5},{5,1},{9,13},{13,9},{2,6},{6,2},{1... | collective-permute-start | bytes 172040 | tf_op jit(solution)/shard_map/ppermute | solution.py:26
  23.0 5.1 %collective-permute-start.7 = (bf16[2,56,256]{2,1,0:T(8,128)(2,1)S(1)}, bf16[2,56,256]{2,1,0:T(8,128)(2,1)S(1)}, u32[]{:S(2)}, u32[]{:S(2)}) collective-permute-start(bf16[2,56,256]{2,1,0:T(8,128)(2,1)S(1)} %get-tuple-element.38), channel_id=1, source_target_pairs={{0,8},{4,12},{8,0},{12,4},{1,9},{5,13},{9,1},{13,5},{2,10},{6,14},... | collective-permute-start | bytes 172040 | tf_op jit(solution)/shard_map/ppermute | solution.py:26
  23.0 6.0 %collective-permute-start.8 = (bf16[2,56,256]{2,1,0:T(8,128)(2,1)S(1)}, bf16[2,56,256]{2,1,0:T(8,128)(2,1)S(1)}, u32[]{:S(2)}, u32[]{:S(2)}) collective-permute-start(bf16[2,56,256]{2,1,0:T(8,128)(2,1)S(1)} %get-tuple-element.39), channel_id=1, source_target_pairs={{0,12},{4,8},{8,4},{12,0},{1,13},{5,9},{9,5},{13,1},{2,14},{6,10},... | collective-permute-start | bytes 172040 | tf_op jit(solution)/shard_map/ppermute | solution.py:26
  25.1 4.5 %collective-permute-start.9 = (bf16[2,56,256]{2,1,0:T(8,128)(2,1)S(1)}, bf16[2,56,256]{2,1,0:T(8,128)(2,1)S(1)}, u32[]{:S(2)}, u32[]{:S(2)}) collective-permute-start(bf16[2,56,256]{2,1,0:T(8,128)(2,1)S(1)} %get-tuple-element.40), channel_id=1, source_target_pairs={{0,4},{4,0},{8,12},{12,8},{1,5},{5,1},{9,13},{13,9},{2,6},{6,2},{1... | collective-permute-start | bytes 172040 | tf_op jit(solution)/shard_map/ppermute | solution.py:26
  30.4 6.6 %collective-permute-start.15 = (f16[7,56,128]{2,1,0:T(8,128)(2,1)S(1)}, f16[7,56,128]{2,1,0:T(8,128)(2,1)S(1)}, u32[]{:S(2)}, u32[]{:S(2)}) collective-permute-start(f16[7,56,128]{2,1,0:T(8,128)(2,1)S(1)} %convert_element_type.20), channel_id=1, source_target_pairs={{0,12},{4,8},{8,4},{12,0},{1,13},{5,9},{9,5},{13,1},{2,14},{6,10},... | collective-permute-start | bytes 301064 | tf_op jit(solution)/shard_map/ppermute | solution.py:26
  32.7 6.8 %collective-permute-start.13 = (f16[7,56,128]{2,1,0:T(8,128)(2,1)S(1)}, f16[7,56,128]{2,1,0:T(8,128)(2,1)S(1)}, u32[]{:S(2)}, u32[]{:S(2)}) collective-permute-start(f16[7,56,128]{2,1,0:T(8,128)(2,1)S(1)} %convert_element_type.19), channel_id=1, source_target_pairs={{0,8},{4,12},{8,0},{12,4},{1,9},{5,13},{9,1},{13,5},{2,10},{6,14},... | collective-permute-start | bytes 301064 | tf_op jit(solution)/shard_map/ppermute | solution.py:26
  33.0 6.5 %collective-permute-start.14 = (f16[7,56,128]{2,1,0:T(8,128)(2,1)S(1)}, f16[7,56,128]{2,1,0:T(8,128)(2,1)S(1)}, u32[]{:S(2)}, u32[]{:S(2)}) collective-permute-start(f16[7,56,128]{2,1,0:T(8,128)(2,1)S(1)} %convert_element_type.18), channel_id=1, source_target_pairs={{0,4},{4,0},{8,12},{12,8},{1,5},{5,1},{9,13},{13,9},{2,6},{6,2},{1... | collective-permute-start | bytes 301064 | tf_op jit(solution)/shard_map/ppermute | solution.py:26

commit v8 on v6

--- a/solution.py
+++ b/solution.py
@@ -114,15 +114,19 @@
 
 
 def near_kernel(loop, per, parts, mine, over, frames, labels, core, *outs):
-    to_chip, (*to_time, core_over) = outs[: len(parts)], outs[len(parts) :]
-    t = lax.axis_index("tm")
-    owned_kernel(loop * per, frames, labels, core, core_over)
+    to_chip, to_time = outs[: len(parts)], outs[len(parts) :]
+    t, p = lax.axis_index("tm"), lax.axis_index("pix")
+    owned_kernel(loop * per, frames, labels, core)
     for (start, count), out in zip(parts, to_chip):
         for c in range(loop):
             source = slice((c * per + start) * LANES, (c * per + start + count) * LANES)
             target = slice(c * count * LANES, (c + 1) * count * LANES)
             out[0, :, target] = over[:, source]
-            out[1, :, target] = core_over[:, source]
+            for s in range(count):
+                index = ((p ^ 2) * loop + c) * per + start + s
+                live = jnp.where(labels[pl.ds(index, 1), :] >= 0, 1.0, 0.0).astype(jnp.bfloat16)
+                at = slice((c * count + s) * LANES, (c * count + s + 1) * LANES)
+                out[1, :, at] = frames[:, lanes_at(index * LANES, LANES)] * live
     for j, out in enumerate(to_time, 1):
         lanes = lanes_at((t ^ j) * per * LANES, per * LANES)
         out[0] = mine[:, lanes]
@@ -312,7 +316,6 @@
         + [shape(2, rows, loop * count * LANES) for _, count in parts]
         + [shape(2, rows, per * LANES)] * (loop - 1),
         4,
-        [pltpu.VMEM((rows, span), bf16)],
     )(mine, over, *other)
     chips = [swap(part, "pix", 2) for part in ready[: len(parts)]]
     near = [swap(part, "tm", j) for j, part in enumerate(ready[len(parts) :], 1)]

time: 40.8 us -> 40.8 us (level)
  no operation moved by 1% of the time
where the time goes in v8:
time: 40.8 us; the launch traced here: 40.6 us
  starting transfers between devices  23.2 us (57%)
  waiting for transfers between devices  9.9 us (24%)
  Pallas kernels  5.28 us (13%)
  local copies, waits for them, and re-layouts  1.94 us (5%)
    ppermute x16, starting transfers between devices, swap(): return lax.ppermute(shard, axis, [(i, i ^ by) for i in range(size)])  23.2 us
    ppermute x16, waiting for transfers between devices, swap(): return lax.ppermute(shard, axis, [(i, i ^ by) for i in range(size)])  9.9 us
    pallas_call x11, Pallas kernels, local_call(): return lambda *operands: call(*operands, *after)  5.28 us
    unnamed x4, local copies, waits for them, and re-layouts  1.94 us
  transfers between devices with their start and end apart: 16, of which 9 were waited for; matrix products, arithmetic and copies ran while one was open for 0% of the time, Pallas kernels for 8%

profile of v8, /device:TPU:0, one launch (start us, length us, event | category | flops | bytes accessed | tf_op | source)
XLA Modules:
  0.0 40.6 jit_solution(16323010349701247972)
XLA Ops:
  0.0 0.5 %collective-permute-start = (bf16[56,8192]{1,0:T(8,128)(2,1)}, bf16[56,8192]{1,0:T(8,128)(2,1)S(1)}, u32[]{:S(2)}, u32[]{:S(2)}) collective-permute-start(bf16[56,8192]{1,0:T(8,128)(2,1)} %refs_0_.1), channel_id=1, source_target_pairs={{0,1},{1,0},{2,3},{3,2},{4,5},{5,4},{6,7},{7,6},{8,9},{9,8},{10,11... | collective-permute-start | bytes 2752520 | tf_op jit(solution)/shard_map/ppermute | solution.py:26
  0.5 1.2 %copy-done = bf16[56,8192]{1,0:T(8,128)(2,1)S(1)} copy-done((bf16[56,8192]{1,0:T(8,128)(2,1)S(1)}, bf16[56,8192]{1,0:T(8,128)(2,1)}, u32[]{:S(2)}) %copy-start) | copy-done | bytes 917528
  1.7 0.8 %copy-done.1 = s32[8192]{0:T(1024)S(1)} copy-done((s32[8192]{0:T(1024)S(1)}, s32[8192]{0:T(1024)}, u32[]{:S(2)}) %copy-start.1) | copy-done | bytes 32792
  2.4 0.1 shard_map.28
  2.6 0.2 collective-permute-done.1.refs_3_
  2.8 0.2 shard_map.29
  3.0 2.9 %collective-permute-start.2 = (bf16[2,56,1024]{2,1,0:T(8,128)(2,1)S(1)}, bf16[2,56,1024]{2,1,0:T(8,128)(2,1)S(1)}, u32[]{:S(2)}, u32[]{:S(2)}) collective-permute-start(bf16[2,56,1024]{2,1,0:T(8,128)(2,1)S(1)} %get-tuple-element.33), channel_id=1, source_target_pairs={{0,2},{1,3},{2,0},{3,1},{4,6},{5,7},{6,4},{7,5},{8,10},{9,11},{10,... | collective-permute-start | bytes 688136 | tf_op jit(solution)/shard_map/ppermute | solution.py:26
  5.9 0.1 collective-permute-start.3
  6.0 4.1 %collective-permute-start.4 = (bf16[2,56,512]{2,1,0:T(8,128)(2,1)S(1)}, bf16[2,56,512]{2,1,0:T(8,128)(2,1)S(1)}, u32[]{:S(2)}, u32[]{:S(2)}) collective-permute-start(bf16[2,56,512]{2,1,0:T(8,128)(2,1)S(1)} %get-tuple-element.35), channel_id=1, source_target_pairs={{0,12},{4,8},{8,4},{12,0},{1,13},{5,9},{9,5},{13,1},{2,14},{6,10},... | collective-permute-start | bytes 344072 | tf_op jit(solution)/shard_map/ppermute | solution.py:26
  10.0 0.6 %collective-permute-start.6 = (bf16[2,56,512]{2,1,0:T(8,128)(2,1)S(1)}, bf16[2,56,512]{2,1,0:T(8,128)(2,1)S(1)}, u32[]{:S(2)}, u32[]{:S(2)}) collective-permute-start(bf16[2,56,512]{2,1,0:T(8,128)(2,1)S(1)} %get-tuple-element.37), channel_id=1, source_target_pairs={{0,4},{4,0},{8,12},{12,8},{1,5},{5,1},{9,13},{13,9},{2,6},{6,2},{1... | collective-permute-start | bytes 344072 | tf_op jit(solution)/shard_map/ppermute | solution.py:26
  10.6 1.7 %collective-permute-done.2.refs_2_.refs_0_.refs_1_ = bf16[2,56,1024]{2,1,0:T(8,128)(2,1)S(1)} collective-permute-done((bf16[2,56,1024]{2,1,0:T(8,128)(2,1)S(1)}, bf16[2,56,1024]{2,1,0:T(8,128)(2,1)S(1)}, u32[]{:S(2)}, u32[]{:S(2)}) %collective-permute-start.2) | collective-permute-done | bytes 229408 | tf_op jit(solution)/shard_map/ppermute | solution.py:26
  12.3 3.2 %collective-permute-start.10 = (bf16[2,56,256]{2,1,0:T(8,128)(2,1)S(1)}, bf16[2,56,256]{2,1,0:T(8,128)(2,1)S(1)}, u32[]{:S(2)}, u32[]{:S(2)}) collective-permute-start(bf16[2,56,256]{2,1,0:T(8,128)(2,1)S(1)} %get-tuple-element.41), channel_id=1, source_target_pairs={{0,8},{4,12},{8,0},{12,4},{1,9},{5,13},{9,1},{13,5},{2,10},{6,14},... | collective-permute-start | bytes 172040 | tf_op jit(solution)/shard_map/ppermute | solution.py:26
  15.6 1.2 %collective-permute-done.3.refs_3_.refs_0_.refs_1_ = bf16[2,56,1024]{2,1,0:T(8,128)(2,1)S(1)} collective-permute-done((bf16[2,56,1024]{2,1,0:T(8,128)(2,1)S(1)}, bf16[2,56,1024]{2,1,0:T(8,128)(2,1)S(1)}, u32[]{:S(2)}, u32[]{:S(2)}) %collective-permute-start.3) | collective-permute-done | bytes 229408 | tf_op jit(solution)/shard_map/ppermute | solution.py:26
  16.7 3.8 %collective-permute-start.11 = (bf16[2,56,256]{2,1,0:T(8,128)(2,1)S(1)}, bf16[2,56,256]{2,1,0:T(8,128)(2,1)S(1)}, u32[]{:S(2)}, u32[]{:S(2)}) collective-permute-start(bf16[2,56,256]{2,1,0:T(8,128)(2,1)S(1)} %get-tuple-element.42), channel_id=1, source_target_pairs={{0,12},{4,8},{8,4},{12,0},{1,13},{5,9},{9,5},{13,1},{2,14},{6,10},... | collective-permute-start | bytes 172040 | tf_op jit(solution)/shard_map/ppermute | solution.py:26
  20.7 2.2 %collective-permute-done.5.refs_3_ = bf16[2,56,512]{2,1,0:T(8,128)(2,1)S(1)} collective-permute-done((bf16[2,56,512]{2,1,0:T(8,128)(2,1)S(1)}, bf16[2,56,512]{2,1,0:T(8,128)(2,1)S(1)}, u32[]{:S(2)}, u32[]{:S(2)}) %collective-permute-start.5) | collective-permute-done | bytes 114720 | tf_op jit(solution)/shard_map/ppermute | solution.py:26
  22.9 2.1 %collective-permute-start.8 = (bf16[2,56,256]{2,1,0:T(8,128)(2,1)S(1)}, bf16[2,56,256]{2,1,0:T(8,128)(2,1)S(1)}, u32[]{:S(2)}, u32[]{:S(2)}) collective-permute-start(bf16[2,56,256]{2,1,0:T(8,128)(2,1)S(1)} %get-tuple-element.39), channel_id=1, source_target_pairs={{0,12},{4,8},{8,4},{12,0},{1,13},{5,9},{9,5},{13,1},{2,14},{6,10},... | collective-permute-start | bytes 172040 | tf_op jit(solution)/shard_map/ppermute | solution.py:26
  25.1 1.4 %collective-permute-start.9 = (bf16[2,56,256]{2,1,0:T(8,128)(2,1)S(1)}, bf16[2,56,256]{2,1,0:T(8,128)(2,1)S(1)}, u32[]{:S(2)}, u32[]{:S(2)}) collective-permute-start(bf16[2,56,256]{2,1,0:T(8,128)(2,1)S(1)} %get-tuple-element.40), channel_id=1, source_target_pairs={{0,4},{4,0},{8,12},{12,8},{1,5},{5,1},{9,13},{13,9},{2,6},{6,2},{1... | collective-permute-start | bytes 172040 | tf_op jit(solution)/shard_map/ppermute | solution.py:26
  26.4 0.3 shard_map.33.refs_0_
  26.8 0.4 shard_map.31.refs_0_
  27.2 0.6 %shard_map.35 = (f32[4,56,128]{2,1,0:T(8,128)S(1)}, f32[4,56,128]{2,1,0:T(8,128)S(1)}, f32[4,56,128]{2,1,0:T(8,128)S(1)}, f32[4,56,128]{2,1,0:T(8,128)S(1)}) custom-call(f32[4,2,128,128]{3,2,1,0:T(8,128)S(1)} %shard_map.33.refs_0_, bf16[2,56,1024]{2,1,0:T(8,128)(2,1)S(1)} %collective-permute-done.2.refs_2_.refs_0_.refs_1_, ...), custom_call_target="tpu_custom_call" | custom-call | flops 1 | bytes 1 | tf_op jit(solution)/shard_map/pallas_call | solution.py:100
  27.7 0.3 collective-permute-done.7.refs_2_
  28.1 0.9 %collective-permute-done.8.refs_3_ = bf16[2,56,256]{2,1,0:T(8,128)(2,1)S(1)} collective-permute-done((bf16[2,56,256]{2,1,0:T(8,128)(2,1)S(1)}, bf16[2,56,256]{2,1,0:T(8,128)(2,1)S(1)}, u32[]{:S(2)}, u32[]{:S(2)}) %collective-permute-start.8) | collective-permute-done | bytes 57376 | tf_op jit(solution)/shard_map/ppermute | solution.py:26
  28.9 0.6 %collective-permute-done.9.refs_4_ = bf16[2,56,256]{2,1,0:T(8,128)(2,1)S(1)} collective-permute-done((bf16[2,56,256]{2,1,0:T(8,128)(2,1)S(1)}, bf16[2,56,256]{2,1,0:T(8,128)(2,1)S(1)}, u32[]{:S(2)}, u32[]{:S(2)}) %collective-permute-start.9) | collective-permute-done | bytes 57376 | tf_op jit(solution)/shard_map/ppermute | solution.py:26
  29.5 0.7 %shard_map.36 = (f32[8,56,128]{2,1,0:T(8,128)S(1)}, f32[7,56,128]{2,1,0:T(8,128)S(1)}, f32[7,56,128]{2,1,0:T(8,128)S(1)}, f32[7,56,128]{2,1,0:T(8,128)S(1)}) custom-call(f32[4,2,128,128]{3,2,1,0:T(8,128)S(1)} %shard_map.31.refs_0_, bf16[2,56,1024]{2,1,0:T(8,128)(2,1)S(1)} %collective-permute-done.3.refs_3_.refs_0_.refs_1_, ...), custom_call_target="tpu_custom_call" | custom-call | flops 1 | bytes 1 | tf_op jit(solution)/shard_map/pallas_call | solution.py:100
  30.3 2.3 %collective-permute-start.15 = (f16[7,56,128]{2,1,0:T(8,128)(2,1)S(1)}, f16[7,56,128]{2,1,0:T(8,128)(2,1)S(1)}, u32[]{:S(2)}, u32[]{:S(2)}) collective-permute-start(f16[7,56,128]{2,1,0:T(8,128)(2,1)S(1)} %convert_element_type.20), channel_id=1, source_target_pairs={{0,12},{4,8},{8,4},{12,0},{1,13},{5,9},{9,5},{13,1},{2,14},{6,10},... | collective-permute-start | bytes 301064 | tf_op jit(solution)/shard_map/ppermute | solution.py:26
  32.6 0.3 collective-permute-start.13
  32.9 1.8 %collective-permute-start.14 = (f16[7,56,128]{2,1,0:T(8,128)(2,1)S(1)}, f16[7,56,128]{2,1,0:T(8,128)(2,1)S(1)}, u32[]{:S(2)}, u32[]{:S(2)}) collective-permute-start(f16[7,56,128]{2,1,0:T(8,128)(2,1)S(1)} %convert_element_type.18), channel_id=1, source_target_pairs={{0,4},{4,0},{8,12},{12,8},{1,5},{5,1},{9,13},{13,9},{2,6},{6,2},{1... | collective-permute-start | bytes 301064 | tf_op jit(solution)/shard_map/ppermute | solution.py:26
  34.8 0.8 %shard_map.30.refs_0_ = f32[32,56,128]{2,1,0:T(8,128)S(1)} custom-call(bf16[56,2048]{1,0:T(8,128)(2,1)S(1)} %get-tuple-element.30.refs_0_, bf16[56,2048]{1,0:T(8,128)(2,1)S(1)} %get-tuple-element.32.refs_1_, bf16[2,56,1024]{2,1,0:T(8,128)(2,1)S(1)} %collective-permute-done.2.refs_2_.refs_0_.refs_1_, ...), custom_call_target="tpu_custom_call" | custom-call | flops 1 | bytes 4194304 | tf_op jit(solution)/shard_map/pallas_call | solution.py:100
  35.6 1.4 %collective-permute-done.15 = f16[7,56,128]{2,1,0:T(8,128)(2,1)S(1)} collective-permute-done((f16[7,56,128]{2,1,0:T(8,128)(2,1)S(1)}, f16[7,56,128]{2,1,0:T(8,128)(2,1)S(1)}, u32[]{:S(2)}, u32[]{:S(2)}) %collective-permute-start.15) | collective-permute-done | bytes 100384 | tf_op jit(solution)/shard_map/ppermute | solution.py:26
  37.0 1.1 %shard_map.37.refs_3_ = f32[32,56,168]{2,1,0:T(8,128)} custom-call(f32[32,56,128]{2,1,0:T(8,128)S(1)} %shard_map.30.refs_0_, f32[8,56,128]{2,1,0:T(8,128)S(1)} %get-tuple-element.53.refs_1_, f32[7,56,128]{2,1,0:T(8,128)S(1)} %convert_element_type.23.refs_2_), custom_call_target="tpu_custom_call" | custom-call | flops 1 | bytes 4194304 | tf_op jit(solution)/shard_map/pallas_call | solution.py:100
  38.1 1.3 %collective-permute-done.13 = f16[7,56,128]{2,1,0:T(8,128)(2,1)S(1)} collective-permute-done((f16[7,56,128]{2,1,0:T(8,128)(2,1)S(1)}, f16[7,56,128]{2,1,0:T(8,128)(2,1)S(1)}, u32[]{:S(2)}, u32[]{:S(2)}) %collective-permute-start.13) | collective-permute-done | bytes 100384 | tf_op jit(solution)/shard_map/ppermute | solution.py:26
  39.5 1.1 %shard_map.38 = f32[32,56,168]{2,1,0:T(8,128)} custom-call(f32[32,56,128]{2,1,0:T(8,128)S(1)} %shard_map.30.refs_0_, f32[7,56,128]{2,1,0:T(8,128)S(1)} %convert_element_type.21.refs_1_, f32[7,56,128]{2,1,0:T(8,128)S(1)} %convert_element_type.22.refs_2_, f32[32,56,168]{2,1,0:T(8,128)} %shard_map.37.refs_3_), custom_call_target="tpu_custom_call", output_to_operand_aliasing={{}: (3, {})} | custom-call | flops 1 | bytes 4194304 | tf_op jit(solution)/shard_map/pallas_call | solution.py:100
  (21 shorter events, 0.3 us)
Async XLA Ops:
  0.0 2.8 %collective-permute-start = (bf16[56,8192]{1,0:T(8,128)(2,1)}, bf16[56,8192]{1,0:T(8,128)(2,1)S(1)}, u32[]{:S(2)}, u32[]{:S(2)}) collective-permute-start(bf16[56,8192]{1,0:T(8,128)(2,1)} %refs_0_.1), channel_id=1, source_target_pairs={{0,1},{1,0},{2,3},{3,2},{4,5},{5,4},{6,7},{7,6},{8,9},{9,8},{10,11... | collective-permute-start | bytes 2752520 | tf_op jit(solution)/shard_map/ppermute | solution.py:26
  0.5 2.4 %collective-permute-start.1 = (s32[64,128]{1,0:T(8,128)}, s32[64,128]{1,0:T(8,128)S(1)}, u32[]{:S(2)}, u32[]{:S(2)}) collective-permute-start(s32[64,128]{1,0:T(8,128)} %bitcast.1), channel_id=1, source_target_pairs={{0,1},{1,0},{2,3},{3,2},{4,5},{5,4},{6,7},{7,6},{8,9},{9,8},{10,11... | collective-permute-start | bytes 98312 | tf_op jit(solution)/shard_map/ppermute | solution.py:26
  0.5 1.2 %copy-start = (bf16[56,8192]{1,0:T(8,128)(2,1)S(1)}, bf16[56,8192]{1,0:T(8,128)(2,1)}, u32[]{:S(2)}) copy-start(bf16[56,8192]{1,0:T(8,128)(2,1)} %refs_0_.1) | copy-start | bytes 2752516
  1.7 0.8 %copy-start.1 = (s32[8192]{0:T(1024)S(1)}, s32[8192]{0:T(1024)}, u32[]{:S(2)}) copy-start(s32[8192]{0:T(1024)} %param.3) | copy-start | bytes 98308
  3.0 9.3 %collective-permute-start.2 = (bf16[2,56,1024]{2,1,0:T(8,128)(2,1)S(1)}, bf16[2,56,1024]{2,1,0:T(8,128)(2,1)S(1)}, u32[]{:S(2)}, u32[]{:S(2)}) collective-permute-start(bf16[2,56,1024]{2,1,0:T(8,128)(2,1)S(1)} %get-tuple-element.33), channel_id=1, source_target_pairs={{0,2},{1,3},{2,0},{3,1},{4,6},{5,7},{6,4},{7,5},{8,10},{9,11},{10,... | collective-permute-start | bytes 688136 | tf_op jit(solution)/shard_map/ppermute | solution.py:26
  5.9 10.8 %collective-permute-start.3 = (bf16[2,56,1024]{2,1,0:T(8,128)(2,1)S(1)}, bf16[2,56,1024]{2,1,0:T(8,128)(2,1)S(1)}, u32[]{:S(2)}, u32[]{:S(2)}) collective-permute-start(bf16[2,56,1024]{2,1,0:T(8,128)(2,1)S(1)} %get-tuple-element.34), channel_id=1, source_target_pairs={{0,2},{1,3},{2,0},{3,1},{4,6},{5,7},{6,4},{7,5},{8,10},{9,11},{10,... | collective-permute-start | bytes 688136 | tf_op jit(solution)/shard_map/ppermute | solution.py:26
  6.0 14.6 %collective-permute-start.4 = (bf16[2,56,512]{2,1,0:T(8,128)(2,1)S(1)}, bf16[2,56,512]{2,1,0:T(8,128)(2,1)S(1)}, u32[]{:S(2)}, u32[]{:S(2)}) collective-permute-start(bf16[2,56,512]{2,1,0:T(8,128)(2,1)S(1)} %get-tuple-element.35), channel_id=1, source_target_pairs={{0,12},{4,8},{8,4},{12,0},{1,13},{5,9},{9,5},{13,1},{2,14},{6,10},... | collective-permute-start | bytes 344072 | tf_op jit(solution)/shard_map/ppermute | solution.py:26
  10.0 12.9 %collective-permute-start.5 = (bf16[2,56,512]{2,1,0:T(8,128)(2,1)S(1)}, bf16[2,56,512]{2,1,0:T(8,128)(2,1)S(1)}, u32[]{:S(2)}, u32[]{:S(2)}) collective-permute-start(bf16[2,56,512]{2,1,0:T(8,128)(2,1)S(1)} %get-tuple-element.36), channel_id=1, source_target_pairs={{0,8},{4,12},{8,0},{12,4},{1,9},{5,13},{9,1},{13,5},{2,10},{6,14},... | collective-permute-start | bytes 344072 | tf_op jit(solution)/shard_map/ppermute | solution.py:26
  10.0 12.9 %collective-permute-start.6 = (bf16[2,56,512]{2,1,0:T(8,128)(2,1)S(1)}, bf16[2,56,512]{2,1,0:T(8,128)(2,1)S(1)}, u32[]{:S(2)}, u32[]{:S(2)}) collective-permute-start(bf16[2,56,512]{2,1,0:T(8,128)(2,1)S(1)} %get-tuple-element.37), channel_id=1, source_target_pairs={{0,4},{4,0},{8,12},{12,8},{1,5},{5,1},{9,13},{13,9},{2,6},{6,2},{1... | collective-permute-start | bytes 344072 | tf_op jit(solution)/shard_map/ppermute | solution.py:26
  12.3 12.7 %collective-permute-start.10 = (bf16[2,56,256]{2,1,0:T(8,128)(2,1)S(1)}, bf16[2,56,256]{2,1,0:T(8,128)(2,1)S(1)}, u32[]{:S(2)}, u32[]{:S(2)}) collective-permute-start(bf16[2,56,256]{2,1,0:T(8,128)(2,1)S(1)} %get-tuple-element.41), channel_id=1, source_target_pairs={{0,8},{4,12},{8,0},{12,4},{1,9},{5,13},{9,1},{13,5},{2,10},{6,14},... | collective-permute-start | bytes 172040 | tf_op jit(solution)/shard_map/ppermute | solution.py:26
  16.7 10.4 %collective-permute-start.11 = (bf16[2,56,256]{2,1,0:T(8,128)(2,1)S(1)}, bf16[2,56,256]{2,1,0:T(8,128)(2,1)S(1)}, u32[]{:S(2)}, u32[]{:S(2)}) collective-permute-start(bf16[2,56,256]{2,1,0:T(8,128)(2,1)S(1)} %get-tuple-element.42), channel_id=1, source_target_pairs={{0,12},{4,8},{8,4},{12,0},{1,13},{5,9},{9,5},{13,1},{2,14},{6,10},... | collective-permute-start | bytes 172040 | tf_op jit(solution)/shard_map/ppermute | solution.py:26
  20.6 6.5 %collective-permute-start.12 = (bf16[2,56,256]{2,1,0:T(8,128)(2,1)S(1)}, bf16[2,56,256]{2,1,0:T(8,128)(2,1)S(1)}, u32[]{:S(2)}, u32[]{:S(2)}) collective-permute-start(bf16[2,56,256]{2,1,0:T(8,128)(2,1)S(1)} %get-tuple-element.43), channel_id=1, source_target_pairs={{0,4},{4,0},{8,12},{12,8},{1,5},{5,1},{9,13},{13,9},{2,6},{6,2},{1... | collective-permute-start | bytes 172040 | tf_op jit(solution)/shard_map/ppermute | solution.py:26
  22.9 5.1 %collective-permute-start.7 = (bf16[2,56,256]{2,1,0:T(8,128)(2,1)S(1)}, bf16[2,56,256]{2,1,0:T(8,128)(2,1)S(1)}, u32[]{:S(2)}, u32[]{:S(2)}) collective-permute-start(bf16[2,56,256]{2,1,0:T(8,128)(2,1)S(1)} %get-tuple-element.38), channel_id=1, source_target_pairs={{0,8},{4,12},{8,0},{12,4},{1,9},{5,13},{9,1},{13,5},{2,10},{6,14},... | collective-permute-start | bytes 172040 | tf_op jit(solution)/shard_map/ppermute | solution.py:26
  22.9 6.0 %collective-permute-start.8 = (bf16[2,56,256]{2,1,0:T(8,128)(2,1)S(1)}, bf16[2,56,256]{2,1,0:T(8,128)(2,1)S(1)}, u32[]{:S(2)}, u32[]{:S(2)}) collective-permute-start(bf16[2,56,256]{2,1,0:T(8,128)(2,1)S(1)} %get-tuple-element.39), channel_id=1, source_target_pairs={{0,12},{4,8},{8,4},{12,0},{1,13},{5,9},{9,5},{13,1},{2,14},{6,10},... | collective-permute-start | bytes 172040 | tf_op jit(solution)/shard_map/ppermute | solution.py:26
  25.1 4.5 %collective-permute-start.9 = (bf16[2,56,256]{2,1,0:T(8,128)(2,1)S(1)}, bf16[2,56,256]{2,1,0:T(8,128)(2,1)S(1)}, u32[]{:S(2)}, u32[]{:S(2)}) collective-permute-start(bf16[2,56,256]{2,1,0:T(8,128)(2,1)S(1)} %get-tuple-element.40), channel_id=1, source_target_pairs={{0,4},{4,0},{8,12},{12,8},{1,5},{5,1},{9,13},{13,9},{2,6},{6,2},{1... | collective-permute-start | bytes 172040 | tf_op jit(solution)/shard_map/ppermute | solution.py:26
  30.3 6.6 %collective-permute-start.15 = (f16[7,56,128]{2,1,0:T(8,128)(2,1)S(1)}, f16[7,56,128]{2,1,0:T(8,128)(2,1)S(1)}, u32[]{:S(2)}, u32[]{:S(2)}) collective-permute-start(f16[7,56,128]{2,1,0:T(8,128)(2,1)S(1)} %convert_element_type.20), channel_id=1, source_target_pairs={{0,12},{4,8},{8,4},{12,0},{1,13},{5,9},{9,5},{13,1},{2,14},{6,10},... | collective-permute-start | bytes 301064 | tf_op jit(solution)/shard_map/ppermute | solution.py:26
  32.6 6.8 %collective-permute-start.13 = (f16[7,56,128]{2,1,0:T(8,128)(2,1)S(1)}, f16[7,56,128]{2,1,0:T(8,128)(2,1)S(1)}, u32[]{:S(2)}, u32[]{:S(2)}) collective-permute-start(f16[7,56,128]{2,1,0:T(8,128)(2,1)S(1)} %convert_element_type.19), channel_id=1, source_target_pairs={{0,8},{4,12},{8,0},{12,4},{1,9},{5,13},{9,1},{13,5},{2,10},{6,14},... | collective-permute-start | bytes 301064 | tf_op jit(solution)/shard_map/ppermute | solution.py:26
  32.9 6.5 %collective-permute-start.14 = (f16[7,56,128]{2,1,0:T(8,128)(2,1)S(1)}, f16[7,56,128]{2,1,0:T(8,128)(2,1)S(1)}, u32[]{:S(2)}, u32[]{:S(2)}) collective-permute-start(f16[7,56,128]{2,1,0:T(8,128)(2,1)S(1)} %convert_element_type.18), channel_id=1, source_target_pairs={{0,4},{4,0},{8,12},{12,8},{1,5},{5,1},{9,13},{13,9},{2,6},{6,2},{1... | collective-permute-start | bytes 301064 | tf_op jit(solution)/shard_map/ppermute | solution.py:26
